TPU v7x, 32 devices: a whole 2x2x4 slice. The times are simulated.
32 devices in a mesh: rows: 16 (over z, y, core), rep: 2 (over x).
Axes of the slice: x: 2, y: 2, z: 4, core: 2. Of those that a mesh axis runs over, the one named last changes fastest.
Arguments:
- features: bfloat16 [16384, 256], P(('rows', 'rep')), may hold values from -6 to 6
- node_order: int32 [16384], P(('rows', 'rep')), may hold values from 0 to 16383, as said below
- layer_weight: bfloat16 [256, 256], replicated, may hold values from -0.375 to 0.375
- layer_bias: float32 [256], replicated, may hold values from -3 to 3
- tile_values: bfloat16 [3072, 128, 128], P(('rows', 'rep')), may hold values from 0.0009994507 to 0.049804688
- tile_coords: int32 [3072, 2], P(('rows', 'rep')), may hold values from 0 to 127, as said below
- tile_count: int32 [32], P(('rows', 'rep')), may hold values from 24 to 96, as said below
Outputs:
- mixed_out: bfloat16 [16384, 256], P(('rows', 'rep'))
Inputs may be any that keep to these rules, and one draw needn't show every extreme that they name: `node_order`: each aligned block of 512 entries is a permutation of the positions of that block. `tile_coords`: with b = g // 2 and c = g % 2, every entry of group g names a tile row p with b * 8 <= p < (b + 1) * 8 and a tile column q with (q // 8) % 2 = c; no tile appears twice in a group. `tile_count`: in every block b the group with c = b % 2 is full.
All inputs are finite; a program needn't handle non-finite values.
Results may differ from a plain program's by a relative error of at most 0.014.
Values may be sent and summed in bfloat16 or wider, within the bound.
No kernel may reach another device: no remote copies, remote signals or barrier semaphores. Data moves between devices by JAX's collectives and lax.ppermute only.
A program may use at most 128 MiB of HBM per device.

v0:
```python
import jax
import jax.numpy as jnp
from jax import lax
from jax.sharding import PartitionSpec as P


def broadcast(x, axis, root):
    mine = lax.axis_index(axis) == root
    return lax.psum(jnp.where(mine, x, jnp.zeros_like(x)), axis)


def tile_products(panels, tile_values, tile_coords, tile_count, first_section):
    section_count, block_rows, feature_width = panels.shape
    tile_size = tile_values.shape[1]
    tile_rows = block_rows // tile_size
    replicas = lax.axis_size("rep")
    flat_panels = panels.reshape(section_count * tile_rows, tile_size, feature_width)
    column_ids = tile_coords[:, 1]
    section_ids = column_ids // tile_rows // replicas
    slot_ids = (
        jnp.mod(section_ids - first_section, section_count) * tile_rows + column_ids % tile_rows
    )
    gathered = flat_panels[slot_ids]
    products = jnp.einsum("tij,tjf->tif", tile_values, gathered, preferred_element_type=jnp.float32)
    live_mask = (jnp.arange(tile_values.shape[0], dtype=jnp.int32) < tile_count[0]).astype(
        jnp.float32
    )
    local_rows = tile_coords[:, 0] - lax.axis_index("rows") * tile_rows
    selector = (local_rows[None, :] == jnp.arange(tile_rows, dtype=jnp.int32)[:, None]).astype(
        jnp.float32
    ) * live_mask[None, :]
    summed = jnp.einsum("qt,tif->qif", selector, products, precision=lax.Precision.HIGHEST)
    return summed.reshape(block_rows, feature_width)


def build_panels(own_rows):
    replicas = lax.axis_size("rep")
    section_count = lax.axis_size("rows") // replicas
    whole_block = lax.all_gather(own_rows, "rep", axis=0, tiled=True)
    replica_index = lax.axis_index("rep")
    first_section = 0
    received = []
    for position in range(section_count):
        section_now = jnp.mod(position + first_section, section_count)
        received.append(broadcast(whole_block, "rows", section_now * replicas + replica_index))
    return (jnp.stack(received), first_section)


def shards(features, node_order, layer_weight, layer_bias, tile_values, tile_coords, tile_count):
    shard_rows = features.shape[0]
    replicas = lax.axis_size("rep")
    replica_index = lax.axis_index("rep")
    shard_start = (lax.axis_index("rows") * replicas + replica_index) * shard_rows
    clustered = features[node_order - shard_start]
    own_rows = jnp.dot(clustered, layer_weight, preferred_element_type=jnp.float32).astype(
        jnp.bfloat16
    )
    panels, first_section = build_panels(own_rows)
    group_partial = tile_products(
        panels, tile_values, tile_coords, tile_count, first_section
    ).astype(jnp.bfloat16)
    shared = lax.psum_scatter(group_partial, "rep", scatter_dimension=0, tiled=True).astype(
        jnp.float32
    )
    return jax.nn.relu(shared + layer_bias).astype(jnp.bfloat16)


def solution(mesh):
    placed = (
        P(("rows", "rep"), None),
        P(("rows", "rep")),
        P(),
        P(),
        P(("rows", "rep"), None, None),
        P(("rows", "rep"), None),
        P(("rows", "rep")),
    )
    return jax.shard_map(
        shards, mesh=mesh, in_specs=placed, out_specs=P(("rows", "rep"), None), check_vma=False
    )
```

profile of v0, /device:TPU:0, one launch (start us, length us, event | category | flops | bytes accessed | tf_op | source)
XLA Modules:
  0.0 214.2 jit_solution(9987496767767701095)
XLA Ops:
  6.5 0.0 copy-start
  6.5 0.0 all-reduce.3.cloned.1.call-start
  6.5 0.8 compare_select_fusion
  7.4 0.8 subtract_bitcast_fusion
  8.2 2.5 %gather_fusion = bf16[512,256]{1,0:T(8,128)(2,1)S(1)} fusion(bf16[512,256]{1,0:T(8,128)(2,1)} %param.7, s32[1024]{0:T(1024)S(1)} %get-tuple-element.24), kind=kCustom, calls=%fused_computation | custom fusion | bytes 526336 | tf_op jit(solution)/shard_map/gather | solution.py:54
  10.8 1.1 convolution_convert_fusion
  11.9 10.0 %all_gather.3 = bf16[1024,256]{1,0:T(8,128)(2,1)} all-gather(bf16[512,256]{1,0:T(8,128)(2,1)S(1)} %convolution_convert_fusion), channel_id=1, replica_groups=mesh['rows'=16,'rep'=2] {'rep'}, dimensions={0}, use_global_device_ids=true | all-gather | bytes 786432 | tf_op jit(solution)/shard_map/all_gather | solution.py:39
  21.9 3.1 %select_bitcast_fusion = (bf16[1,1024,256]{2,1,0:T(8,128)(2,1)}, bf16[1,1024,256]{2,1,0:T(8,128)(2,1)}, bf16[1,1024,256]{2,1,0:T(8,128)(2,1)}, bf16[1,1024,256]{...) fusion(bf16[1024,256]{1,0:T(8,128)(2,1)} %all_gather.3, ...), kind=kLoop, calls=%fused_computation.7 | loop fusion | flops 2097152 | bytes 4718600 | tf_op jit(solution)/shard_map/stack | solution.py:46
  25.0 0.0 all-reduce.3.cloned.1.call-update
  25.0 0.0 reduce-scatter.2.cloned.1.call-start
  25.7 114.7 %all-reduce.3.cloned.1.call-done = (bf16[1,1024,256]{2,1,0:T(8,128)(2,1)}, bf16[1,1024,256]{2,1,0:T(8,128)(2,1)}, bf16[1,1024,256]{2,1,0:T(8,128)(2,1)}, bf16[1,...) async-done(((bf16[1,1024,256]{2,1,0:T(8,128)(2,1)}, ...) | async-done | bytes 4194320 | tf_op jit(solution)/shard_map/psum | solution.py:9
  140.4 2.0 constant_dynamic-update-slice_fusion.7
  142.4 1.9 constant_dynamic-update-slice_fusion.6
  144.3 1.9 constant_dynamic-update-slice_fusion.5
  146.2 1.9 constant_dynamic-update-slice_fusion.4
  148.0 0.0 copy-done.4
  148.0 0.8 constant_dynamic-update-slice_fusion.3
  148.9 0.0 copy-done.3
  148.9 0.8 constant_dynamic-update-slice_fusion.2
  149.7 0.0 copy-done.2
  149.7 0.9 constant_dynamic-update-slice_fusion.1
  150.6 0.0 copy-done.1
  150.6 0.8 constant_dynamic-update-slice_fusion
  151.4 8.1 %gather_fusion.1 = bf16[96,128,256]{2,1,0:T(8,128)(2,1)} fusion(bf16[64,128,256]{2,1,0:T(8,128)(2,1)} %bitcast.11, s32[1024]{0:T(1024)S(1)} %get-tuple-element.23), kind=kCustom, calls=%fused_computation.1 | custom fusion | bytes 12583296 | tf_op jit(solution)/shard_map/gather | solution.py:23
  159.5 0.0 copy-done
  159.5 9.2 %fusion.15 = f32[96,256,128]{2,1,0:T(8,128)} fusion(bf16[96,128,256]{2,1,0:T(8,128)(2,1)} %gather_fusion.1, bf16[96,128,128]{2,1,0:T(8,128)(2,1)S(1)} %copy-done), kind=kOutput, calls=%fused_computation.52 | convolution fusion | flops 805306368 | bytes 22020096 | tf_op jit(solution)/shard_map/tij,tjf->tif/dot_general | solution.py:24
  168.7 12.6 %copy.9 = f32[96,256,128]{1,0,2:T(8,128)} copy(f32[96,256,128]{2,1,0:T(8,128)} %fusion.15) | data formatting | bytes 25165824 | tf_op jit(solution)/shard_map/tij,tjf->tif/dot_general | solution.py:24
  181.3 8.9 %fusion.2 = bf16[8,128,256]{2,0,1:T(8,128)(2,1)S(1)} fusion(f32[96,256,128]{1,0,2:T(8,128)} %copy.9, f32[96]{0:T(128)S(1)} %compare_convert_fusion, s32[96]{0:T(128)S(1)} %get-tuple-element.21), kind=kOutput, calls=%fused_computation.4 | convolution fusion | flops 302253568 | bytes 13107968 | tf_op jit(solution)/shard_map/qt,tif->qif/dot_general | solution.py:32
  190.2 0.9 copy.8
  191.1 0.0 reduce-scatter.2.cloned.1.call-update
  191.1 14.6 %reduce-scatter.2.cloned.1.call-done = bf16[512,256]{1,0:T(8,128)(2,1)} async-done(((bf16[1024,256]{1,0:T(8,128)(2,1)}), bf16[512,256]{1,0:T(8,128)(2,1)}) %reduce-scatter.2.cloned.1.call-update) | async-done | bytes 262160 | tf_op jit(solution)/shard_map/reduce_scatter | solution.py:62
  205.7 1.7 maximum_convert_fusion
  (8 shorter events, 0.0 us)
Async XLA Ops:
  6.5 153.0 %copy-start = (bf16[96,128,128]{2,1,0:T(8,128)(2,1)S(1)}, bf16[96,128,128]{2,1,0:T(8,128)(2,1)}, u32[]{:S(2)}) copy-start(bf16[96,128,128]{2,1,0:T(8,128)(2,1)} %param.11) | copy-start | bytes 9437188
  6.5 133.8 %all-reduce.3.cloned.1.call-start = ((), (), s32[]{:S(2)}) async-start(), calls=%async_computation.2 | async-start | bytes 8388608 | tf_op jit(solution)/shard_map/psum | solution.py:9
  25.0 180.7 %reduce-scatter.2.cloned.1.call-start = ((), (), s32[]{:S(2)}) async-start(), calls=%async_computation.1 | async-start | bytes 786432 | tf_op jit(solution)/shard_map/reduce_scatter | solution.py:62
  140.4 7.6 %copy-start.4 = (bf16[1,1024,256]{2,1,0:T(8,128)(2,1)S(1)}, bf16[1,1024,256]{2,1,0:T(8,128)(2,1)}, u32[]{:S(2)}) copy-start(bf16[1,1024,256]{2,1,0:T(8,128)(2,1)} %get-tuple-element.9) | copy-start | bytes 1572868
  140.4 8.5 %copy-start.3 = (bf16[1,1024,256]{2,1,0:T(8,128)(2,1)S(1)}, bf16[1,1024,256]{2,1,0:T(8,128)(2,1)}, u32[]{:S(2)}) copy-start(bf16[1,1024,256]{2,1,0:T(8,128)(2,1)} %get-tuple-element.10) | copy-start | bytes 1572868
  140.4 9.3 %copy-start.2 = (bf16[1,1024,256]{2,1,0:T(8,128)(2,1)S(1)}, bf16[1,1024,256]{2,1,0:T(8,128)(2,1)}, u32[]{:S(2)}) copy-start(bf16[1,1024,256]{2,1,0:T(8,128)(2,1)} %get-tuple-element.11) | copy-start | bytes 1572868
  140.4 10.2 %copy-start.1 = (bf16[1,1024,256]{2,1,0:T(8,128)(2,1)S(1)}, bf16[1,1024,256]{2,1,0:T(8,128)(2,1)}, u32[]{:S(2)}) copy-start(bf16[1,1024,256]{2,1,0:T(8,128)(2,1)} %get-tuple-element.12) | copy-start | bytes 1572868
  181.3 24.4 %copy-start.5 = (f32[256]{0:T(256)S(1)}, f32[256]{0:T(256)}, u32[]{:S(2)}) copy-start(f32[256]{0:T(256)} %param.10) | copy-start | bytes 3076
Sparse Core Ops, SparseCore 0:
  25.1 115.1 all-reduce.2
  191.2 14.3 reduce-scatter.1
where the time goes:
time: 215 us; the launch traced here: 214 us
  waiting for transfers between devices  129 us (60%)
  local copies, waits for them, and re-layouts  35.2 us (16%)
  matrix products  19.2 us (9%)
  between operations  14.1 us (7%)
  blocking collectives  10 us (5%)
  other arithmetic  6.48 us (3%)
    psum x1, waiting for transfers between devices, broadcast(): return lax.psum(jnp.where(mine, x, jnp.zeros_like(x)), axis)  115 us
    reduce_scatter x1, waiting for transfers between devices, shards(): lax.psum_scatter(group_partial, 'rep', scatter_dimension=0, tiled=True)  14.6 us
    dot_general x1, local copies, waits for them, and re-layouts, tile_products(): jnp.einsum('tij,tjf->tif', tile_values, gathered, preferred_element_type=...  12.6 us
    unnamed x19, local copies, waits for them, and re-layouts  10.2 us
    all_gather x1, blocking collectives, build_panels(): whole_block = lax.all_gather(own_rows, 'rep', axis=0, tiled=True)  10 us
    dot_general x1, matrix products, tile_products(): jnp.einsum('tij,tjf->tif', tile_values, gathered, preferred_element_type=...  9.16 us
    dot_general x1, matrix products, tile_products(): jnp.einsum('qt,tif->qif', selector, products, precision=lax.Precision.HIG...  8.9 us
    gather x1, local copies, waits for them, and re-layouts, tile_products(): gathered = flat_panels[slot_ids]  8.12 us
  transfers between devices with their start and end apart: 2, of which 2 were waited for; matrix products, arithmetic and copies ran while one was open for 0% of the time, Pallas kernels for 0%

commit v1 on v0

v1 whole, which is shorter than its diff:
```python
import functools
import jax
import jax.numpy as jnp
from jax import lax
from jax.experimental import pallas as pl
from jax.experimental.pallas import tpu as pltpu
from jax.sharding import PartitionSpec as P

AXES = ("rows", "rep")
VMEM_LIMIT = 40 * 1024 * 1024


def whole(count):
    return [pl.BlockSpec(memory_space=pltpu.VMEM)] * count


def scalars():
    return pl.BlockSpec(memory_space=pltpu.SMEM)


def cost(flops, moved):
    return pl.CostEstimate(flops=flops, bytes_accessed=moved, transcendentals=0)


def prepare_kernel(mine_ref, own_ref, got_ref, own_order_ref, got_order_ref, weight_ref, out_ref):
    shard_rows = own_ref.shape[0]

    def project(rows_ref, order_ref):
        projected = jnp.dot(
            rows_ref[...], weight_ref[...], preferred_element_type=jnp.float32
        ).astype(jnp.bfloat16)
        within = lax.rem(order_ref[...], shard_rows)
        node = lax.broadcasted_iota(jnp.int32, (shard_rows, shard_rows), 0)
        chosen = (node == within).astype(jnp.float32).astype(jnp.bfloat16)
        out_ref[...] = lax.dot_general(
            chosen, projected, (((0,), (0,)), ((), ())), preferred_element_type=jnp.float32
        ).astype(jnp.bfloat16)

    @pl.when(mine_ref[0] == 1)
    def _():
        project(own_ref, own_order_ref)

    @pl.when(mine_ref[0] == 0)
    def _():
        project(got_ref, got_order_ref)


def prepare(mine, own, got, own_order, got_order, weight):
    return pl.pallas_call(
        prepare_kernel,
        out_shape=jax.ShapeDtypeStruct(own.shape, own.dtype),
        in_specs=[scalars()] + whole(5),
        out_specs=pl.BlockSpec(memory_space=pltpu.VMEM),
        compiler_params=pltpu.CompilerParams(vmem_limit_bytes=VMEM_LIMIT),
        cost_estimate=cost(4 * own.shape[0] ** 2 * own.shape[1], 3 * own.size),
        name="prepare",
    )(mine, own, got, own_order[None], got_order[None], weight)


def stage_kernel(n_pieces, has_sum, tile_rows, base_ref, table_ref, tiles_ref, *refs):
    pieces = refs[:n_pieces]
    sum_ref = refs[n_pieces] if has_sum else None
    out_ref, dense_ref = refs[-2:]
    tile = tiles_ref.shape[1]
    slots = table_ref.shape[1]
    start = 0
    spans = []
    for i, piece in enumerate(pieces):
        count = piece.shape[0] // tile
        for j in range(count):
            for p in range(tile_rows):
                entry = table_ref[p, base_ref[i] + j]
                live = jnp.where(entry >= 0, 1.0, 0.0).astype(jnp.bfloat16)
                dense_ref[p * tile : (p + 1) * tile, start + j * tile : start + (j + 1) * tile] = (
                    tiles_ref[jnp.maximum(entry, 0)] * live
                )
        spans.append((start, start + count * tile))
        start += count * tile
    strip = 2 * tile
    for top in range(0, out_ref.shape[0], strip):
        total = sum_ref[top : top + strip] if has_sum else None
        for piece, (first, last) in zip(pieces, spans):
            product = jnp.dot(
                dense_ref[top : top + strip, first:last],
                piece[...],
                preferred_element_type=jnp.float32,
            )
            total = product if total is None else total + product
        out_ref[top : top + strip] = total


def stage(pieces, bases, table, tiles, total):
    width = pieces[0].shape[1]
    tile_rows, tile = table.shape[0], tiles.shape[1]
    depth = sum(p.shape[0] for p in pieces)
    rows = tile_rows * tile
    operands = list(pieces) + ([] if total is None else [total])
    return pl.pallas_call(
        functools.partial(stage_kernel, len(pieces), total is not None, tile_rows),
        out_shape=jax.ShapeDtypeStruct((rows, width), jnp.float32),
        in_specs=[scalars(), scalars()] + whole(1 + len(operands)),
        out_specs=pl.BlockSpec(memory_space=pltpu.VMEM),
        scratch_shapes=[pltpu.VMEM((rows, depth), jnp.bfloat16)],
        compiler_params=pltpu.CompilerParams(vmem_limit_bytes=VMEM_LIMIT),
        cost_estimate=cost(2 * rows * depth * width, 2 * rows * depth + 8 * rows * width),
        name="stage",
    )(jnp.stack(bases).astype(jnp.int32), table, tiles, *operands)


def tile_table(tile_coords, tile_count, tile_rows, slots):
    replicas = lax.axis_size("rep")
    column_ids = tile_coords[:, 1]
    slot = column_ids // (tile_rows * replicas) * tile_rows + column_ids % tile_rows
    local_row = tile_coords[:, 0] - lax.axis_index("rows") * tile_rows
    entry = jnp.arange(tile_coords.shape[0], dtype=jnp.int32)
    code = jnp.where(entry < tile_count[0], local_row * slots + slot, -1)
    at = jnp.arange(tile_rows * slots, dtype=jnp.int32)
    found = jnp.max(jnp.where(code[None, :] == at[:, None], entry[None, :], -1), axis=1)
    return found.reshape(tile_rows, slots)


def device_id(row, rep, replicas):
    return row * replicas + rep


def ring_stages(own, table, tiles, tile_rows):
    replicas, row_count = lax.axis_size("rep"), lax.axis_size("rows")
    chips = row_count // replicas
    ring = list(range(0, chips, 2)) + list(range(chips - 1, 0, -2))
    place = {chip: i for i, chip in enumerate(ring)}

    def around(step):
        return [
            (
                device_id(chip * replicas + core, rep, replicas),
                device_id(ring[(place[chip] + step) % chips] * replicas + core, rep, replicas),
            )
            for chip in range(chips)
            for core in range(replicas)
            for rep in range(replicas)
        ]

    other_core = [
        (
            device_id(chip * replicas + core, rep, replicas),
            device_id(chip * replicas + 1 - core, rep, replicas),
        )
        for chip in range(chips)
        for core in range(replicas)
        for rep in range(replicas)
    ]
    up, down = around(1), around(-1)
    row = lax.axis_index("rows")
    chip, core = row // replicas, row % replicas
    here = jnp.asarray([place[c] for c in range(chips)], jnp.int32)[chip]
    order = jnp.asarray(ring, jnp.int32)
    tile = tiles.shape[1]
    half_slots = own.shape[0] // tile

    def base(offset, side, extra=0):
        return order[(here + offset) % chips] * tile_rows + side * half_slots + extra

    def both(piece):
        return piece, lax.ppermute(piece, AXES, other_core)

    def held(pieces):
        arrays, bases = [], []
        for piece, offset, extra in pieces:
            mine, theirs = both(piece)
            arrays += [mine, theirs]
            bases += [base(offset, core, extra), base(offset, 1 - core, extra)]
        return arrays, bases

    total = stage(*held([(own, 0, 0)]), table, tiles, None)
    left, right = own, own
    for step in range(1, chips // 2):
        left, right = lax.ppermute(left, AXES, up), lax.ppermute(right, AXES, down)
        total = stage(*held([(left, -step, 0), (right, step, 0)]), table, tiles, total)
    half = own.shape[0] // 2
    left, right = lax.ppermute(left[:half], AXES, up), lax.ppermute(right[half:], AXES, down)
    far = chips // 2
    return stage(*held([(left, far, 0), (right, far, half // tile)]), table, tiles, total)


def gathered_stages(own, table, tiles, tile_rows):
    panels = lax.all_gather(own, "rows", axis=0, tiled=True)
    depth = tile_rows * tiles.shape[1]
    total = None
    for section in range(panels.shape[0] // depth):
        base = jnp.int32(section * tile_rows)
        total = stage(
            [panels[section * depth : (section + 1) * depth]], [base], table, tiles, total
        )
    return total


def shards(features, node_order, layer_weight, layer_bias, tile_values, tile_coords, tile_count):
    shard_rows, width = features.shape
    replicas, row_count = lax.axis_size("rep"), lax.axis_size("rows")
    rep, row = lax.axis_index("rep"), lax.axis_index("rows")
    tile = tile_values.shape[1]
    tile_rows = shard_rows * replicas // tile
    trade = [
        (
            device_id(s * replicas + c, r, replicas),
            device_id(s * replicas + r, c, replicas),
        )
        for s in range(row_count // replicas)
        for r in range(replicas)
        for c in range(replicas)
        if r != c
    ]
    got = lax.ppermute(features, AXES, trade)
    got_order = lax.ppermute(node_order, AXES, trade)
    mine = (row % replicas == rep).astype(jnp.int32)[None]
    own = prepare(mine, features, got, node_order, got_order, layer_weight)
    slots = row_count // replicas * tile_rows
    table = tile_table(tile_coords, tile_count, tile_rows, slots)
    stages = ring_stages if replicas == 2 else gathered_stages
    total = stages(own, table, tile_values, tile_rows).astype(jnp.bfloat16)

    def part(of):
        return lax.dynamic_slice_in_dim(total, of * shard_rows, shard_rows, 0)

    result = part(rep).astype(jnp.float32)
    for step in range(1, replicas):
        result += lax.ppermute(
            part((rep + step) % replicas),
            "rep",
            [(r, (r + step) % replicas) for r in range(replicas)],
        ).astype(jnp.float32)
    return jax.nn.relu(result + layer_bias).astype(jnp.bfloat16)


def solution(mesh):
    placed = (
        P(("rows", "rep"), None),
        P(("rows", "rep")),
        P(),
        P(),
        P(("rows", "rep"), None, None),
        P(("rows", "rep"), None),
        P(("rows", "rep")),
    )
    return jax.shard_map(
        shards, mesh=mesh, in_specs=placed, out_specs=P(("rows", "rep"), None), check_vma=False
    )
```

time: 215 us -> 72.1 us (0.34)
  waiting for transfers between devices: 129 us -> 17.1 us
  local copies, waits for them, and re-layouts: 35.2 us -> 7.82 us
  starting transfers between devices: 0.04 us -> 21.2 us
  matrix products: 19.2 us -> 0 us
  Pallas kernels: 0 us -> 10.6 us
  blocking collectives: 10 us -> 0 us
  other arithmetic: 6.48 us -> 2.11 us
    psum x1 -> x0, waiting for transfers between devices: 115 us -> none  [broadcast(): return lax.psum(jnp.where(mine, x, jnp.zeros_like(x)), axis)]
    ppermute x0 -> x20, starting transfers between devices: none -> 21.2 us  [the longest x9 10.5 us: both(): return (piece, lax.ppermute(piece, AXES, other_core))]
    dot_general x3 -> x0, matrix products: 19.2 us -> none  [the longest x1 9.16 us: tile_products(): jnp.einsum('tij,tjf->tif', tile_values, gathered, preferred_element_type=...]
    ppermute x0 -> x20, waiting for transfers between devices: none -> 17.1 us  [the longest x1 8.27 us: shards(): lax.ppermute(part((rep + step) % replicas), 'rep', [(r, (r + step) % repl...]
    reduce_scatter x1 -> x0, waiting for transfers between devices: 14.6 us -> none  [shards(): lax.psum_scatter(group_partial, 'rep', scatter_dimension=0, tiled=True)]
    dot_general x1 -> x0, local copies, waits for them, and re-layouts: 12.6 us -> none  [tile_products(): jnp.einsum('tij,tjf->tif', tile_values, gathered, preferred_element_type=...]
    gather x2 -> x0, local copies, waits for them, and re-layouts: 10.7 us -> none  [the longest x1 8.12 us: tile_products(): gathered = flat_panels[slot_ids]]
    pallas_call x0 -> x6, Pallas kernels: none -> 10.6 us  [the longest x5 10 us: stage(): pl.pallas_call(functools.partial(stage_kernel, len(pieces), total is not...]
  transfers between devices with their start and end apart: 2 -> 20, of which waited for: 2 -> 4; matrix products, arithmetic and copies ran while one was open for 0% -> 6% of each run, Pallas kernels for 0% -> 12%
where the time goes in v1:
time: 72.1 us; the launch traced here: 71.6 us
  starting transfers between devices  21.2 us (29%)
  waiting for transfers between devices  17.1 us (24%)
  between operations  12.8 us (18%)
  Pallas kernels  10.6 us (15%)
  local copies, waits for them, and re-layouts  7.82 us (11%)
  other arithmetic  2.11 us (3%)
    ppermute x9, starting transfers between devices, both(): return (piece, lax.ppermute(piece, AXES, other_core))  10.5 us
    pallas_call x5, Pallas kernels, stage(): pl.pallas_call(functools.partial(stage_kernel, len(pieces), total is not...  10 us
    ppermute x1, waiting for transfers between devices, shards(): lax.ppermute(part((rep + step) % replicas), 'rep', [(r, (r + step) % repl...  8.27 us
    ppermute x3, waiting for transfers between devices, ring_stages(): lax.ppermute(left, AXES, up)  7.34 us
    ppermute x3, starting transfers between devices, ring_stages(): lax.ppermute(left, AXES, up)  6.95 us
    unnamed x12, local copies, waits for them, and re-layouts  4.8 us
    dynamic_slice x1, local copies, waits for them, and re-layouts, base(): order[(here + offset) % chips] * tile_rows + side * half_slots + extra  1.65 us
    ppermute x3, waiting for transfers between devices, ring_stages(): lax.ppermute(right, AXES, down)  1.47 us
  transfers between devices with their start and end apart: 20, of which 4 were waited for; matrix products, arithmetic and copies ran while one was open for 6% of the time, Pallas kernels for 12%

profile of v1, /device:TPU:0, one launch (start us, length us, event | category | flops | bytes accessed | tf_op | source)
XLA Modules:
  0.0 71.6 jit_solution(12216920616099434933)
XLA Ops:
  0.0 0.7 collective-permute-start
  0.7 0.7 collective-permute-start.1
  1.4 0.9 %copy-done.2 = bf16[512,256]{1,0:T(8,128)(2,1)S(1)} copy-done((bf16[512,256]{1,0:T(8,128)(2,1)S(1)}, bf16[512,256]{1,0:T(8,128)(2,1)}, u32[]{:S(2)}) %copy-start.2) | copy-done | bytes 262168
  2.3 0.9 %copy-done.3 = bf16[256,256]{1,0:T(8,128)(2,1)S(1)} copy-done((bf16[256,256]{1,0:T(8,128)(2,1)S(1)}, bf16[256,256]{1,0:T(8,128)(2,1)}, u32[]{:S(2)}) %copy-start.3) | copy-done | bytes 131096
  3.2 0.7 copy-done.4
  3.9 0.6 prepare.1.refs_0_
  4.5 3.1 %collective-permute-start.2 = (bf16[512,256]{1,0:T(8,128)(2,1)S(1)}, bf16[512,256]{1,0:T(8,128)(2,1)S(1)}, u32[]{:S(2)}, u32[]{:S(2)}) collective-permute-start(bf16[512,256]{1,0:T(8,128)(2,1)S(1)} %prepare.1.refs_0_), channel_id=1, source_target_pairs={{0,8},{1,9},{2,10},{3,11},{4,0},{5,1},{6,2},{7,3},{8,16},{9,17},{1... | collective-permute-start | bytes 786440 | tf_op jit(solution)/shard_map/ppermute | solution.py:177
  8.2 3.6 %collective-permute-done.2.refs_0_ = bf16[512,256]{1,0:T(8,128)(2,1)S(1)} collective-permute-done((bf16[512,256]{1,0:T(8,128)(2,1)S(1)}, bf16[512,256]{1,0:T(8,128)(2,1)S(1)}, u32[]{:S(2)}, u32[]{:S(2)}) %collective-permute-start.2) | collective-permute-done | bytes 262176 | tf_op jit(solution)/shard_map/ppermute | solution.py:177
  11.9 2.1 %collective-permute-start.3 = (bf16[512,256]{1,0:T(8,128)(2,1)S(1)}, bf16[512,256]{1,0:T(8,128)(2,1)S(1)}, u32[]{:S(2)}, u32[]{:S(2)}) collective-permute-start(bf16[512,256]{1,0:T(8,128)(2,1)S(1)} %collective-permute-done.2.refs_0_), channel_id=1, source_target_pairs={{0,8},{1,9},{2,10},{3,11},{4,0},{5,1},{6,2},{7,3},{8,16},{9,17},{1... | collective-permute-start | bytes 786440 | tf_op jit(solution)/shard_map/ppermute | solution.py:177
  13.9 0.8 %compare_select_fusion = s32[96]{0:T(128)S(1)} fusion(s32[96,2]{0,1:T(2,128)} %param.14, s32[]{:T(128)S(6)} %mul.116, s32[]{:T(128)} %bitcast.48), kind=kLoop, calls=%fused_computation.5 | loop fusion | flops 2880 | bytes 1160 | tf_op jit(solution)/shard_map/jit(_where)/select_n | solution.py:116
  14.7 1.2 %dynamic_slice.43 = s32[1]{0:T(128)} dynamic-slice(s32[8]{0:T(128)} %constant.152.clone, s32[]{:T(128)S(6)} %select_n.144), dynamic_slice_sizes={1} | dynamic-slice | bytes 12 | tf_op jit(solution)/shard_map/dynamic_slice | solution.py:155
  22.6 1.7 %fusion.2 = (s32[1]{0:T(128)}, s32[1]{0:T(128)}, s32[1]{0:T(128)}, s32[1]{0:T(128)}, s32[1]{0:T(128)}, /*index=5*/s32[1]{0:T(128)}, s32[1]{0:T(128)}, s32[1]{0:T(128)}) fusion(s32[8]{0:T(128)} %constant.153.clone, s32[]{:T(128)S(6)} %select_n.165, s32[]{:T(128)S(6)} %select_n.161, s32[]{:T(128)S(6)} %select_n.159, s32[]{:T(128)S(6)} %select_n.157, ...), kind=kLoop, calls=%fused_computation.19 | loop fusion | bytes 96 | tf_op jit(solution)/shard_map/dynamic_slice | solution.py:161
  24.9 9.2 %collective-permute-start.18 = (bf16[512,256]{1,0:T(8,128)(2,1)S(1)}, bf16[512,256]{1,0:T(8,128)(2,1)S(1)}, u32[]{:S(2)}, u32[]{:S(2)}) collective-permute-start(bf16[512,256]{1,0:T(8,128)(2,1)S(1)} %prepare.1.refs_0_), channel_id=1, source_target_pairs={{0,2},{1,3},{2,0},{3,1},{4,6},{5,7},{6,4},{7,5},{8,10},{9,11},{10,... | collective-permute-start | bytes 786440 | tf_op jit(solution)/shard_map/ppermute | solution.py:164
  36.9 1.8 %collective-permute-start.4 = (bf16[512,256]{1,0:T(8,128)(2,1)S(1)}, bf16[512,256]{1,0:T(8,128)(2,1)S(1)}, u32[]{:S(2)}, u32[]{:S(2)}) collective-permute-start(bf16[512,256]{1,0:T(8,128)(2,1)S(1)} %collective-permute-done.3.refs_0_), channel_id=1, source_target_pairs={{0,8},{1,9},{2,10},{3,11},{4,0},{5,1},{6,2},{7,3},{8,16},{9,17},{1... | collective-permute-start | bytes 786440 | tf_op jit(solution)/shard_map/ppermute | solution.py:177
  38.7 0.3 collective-permute-start.9
  40.4 0.5 collective-permute-start.14
  41.6 0.1 select_reduce_fusion
  41.7 0.2 collective-permute-start.15
  41.9 3.7 %collective-permute-done.4.refs_0_ = bf16[512,256]{1,0:T(8,128)(2,1)S(1)} collective-permute-done((bf16[512,256]{1,0:T(8,128)(2,1)S(1)}, bf16[512,256]{1,0:T(8,128)(2,1)S(1)}, u32[]{:S(2)}, u32[]{:S(2)}) %collective-permute-start.4) | collective-permute-done | bytes 262176 | tf_op jit(solution)/shard_map/ppermute | solution.py:177
  45.6 1.5 %collective-permute-done.9.refs_2_ = bf16[512,256]{1,0:T(8,128)(2,1)S(1)} collective-permute-done((bf16[512,256]{1,0:T(8,128)(2,1)S(1)}, bf16[512,256]{1,0:T(8,128)(2,1)S(1)}, u32[]{:S(2)}, u32[]{:S(2)}) %collective-permute-start.9) | collective-permute-done | bytes 262176 | tf_op jit(solution)/shard_map/ppermute | solution.py:177
  47.3 0.8 %collective-permute-start.10 = (bf16[256,256]{1,0:T(8,128)(2,1)S(1)}, bf16[256,256]{1,0:T(8,128)(2,1)S(1)}, u32[]{:S(2)}, u32[]{:S(2)}) collective-permute-start(bf16[256,256]{1,0:T(8,128)(2,1)S(1)} %slice.17), channel_id=1, source_target_pairs={{0,4},{1,5},{2,6},{3,7},{4,12},{5,13},{6,14},{7,15},{8,0},{9,1},{1... | collective-permute-start | bytes 393224 | tf_op jit(solution)/shard_map/ppermute | solution.py:180
  48.0 1.3 %collective-permute-start.5 = (bf16[256,256]{1,0:T(8,128)(2,1)S(1)}, bf16[256,256]{1,0:T(8,128)(2,1)S(1)}, u32[]{:S(2)}, u32[]{:S(2)}) collective-permute-start(bf16[256,256]{1,0:T(8,128)(2,1)S(1)} %slice.16), channel_id=1, source_target_pairs={{0,8},{1,9},{2,10},{3,11},{4,0},{5,1},{6,2},{7,3},{8,16},{9,17},{1... | collective-permute-start | bytes 393224 | tf_op jit(solution)/shard_map/ppermute | solution.py:180
  49.3 1.9 %copy-done = bf16[96,128,128]{2,1,0:T(8,128)(2,1)S(1)} copy-done((bf16[96,128,128]{2,1,0:T(8,128)(2,1)S(1)}, bf16[96,128,128]{2,1,0:T(8,128)(2,1)}, u32[]{:S(2)}) %copy-start) | copy-done | bytes 3145752
  51.2 1.5 %stage.5.refs_4_ = f32[1024,256]{1,0:T(8,128)S(1)} custom-call(s32[2]{0:T(128)S(1)} %pad_add_fusion.4.base_ref, s32[8,64]{1,0:T(8,128)S(1)} %reshape.86.table_ref, bf16[96,128,128]{2,1,0:T(8,128)(2,1)S(1)} %copy-done, bf16[512,256]{1,0:T(8,128)(2,1)S(1)} %prepare.1.refs_0_, bf16[512,256]{1,0:T(8,128)(2,1)S(1)} %collective-permute-done.18.refs_1_), custom_call_target="tpu_custom_call" | custom-call | flops 536870912 | bytes 4194304 | tf_op jit(solution)/shard_map/stage/pallas_call | solution.py:98
  52.8 0.4 copy-done.1
  53.1 2.2 %stage.6.refs_4_ = f32[1024,256]{1,0:T(8,128)S(1)} custom-call(s32[4]{0:T(128)S(1)} %pad_add_fusion.3.base_ref, s32[8,64]{1,0:T(8,128)S(1)} %reshape.86.table_ref, bf16[96,128,128]{2,1,0:T(8,128)(2,1)S(1)} %copy-done.1, bf16[512,256]{1,0:T(8,128)(2,1)S(1)} %collective-permute-done.2.refs_0_, bf16[512,256]{1,0:T(8,128)(2,1)S(1)} %collective-permute-done.16.refs_1_, ...), custom_call_target="tpu_custom_call" | custom-call | flops 1073741824 | bytes 6291456 | tf_op jit(solution)/shard_map/stage/pallas_call | solution.py:98
  55.4 0.5 collective-permute-start.6
  55.9 2.2 %stage.7.refs_4_ = f32[1024,256]{1,0:T(8,128)S(1)} custom-call(s32[4]{0:T(128)S(1)} %pad_add_fusion.2.base_ref, s32[8,64]{1,0:T(8,128)S(1)} %reshape.86.table_ref, bf16[96,128,128]{2,1,0:T(8,128)(2,1)S(1)} %copy-done.1, bf16[512,256]{1,0:T(8,128)(2,1)S(1)} %collective-permute-done.3.refs_0_, bf16[512,256]{1,0:T(8,128)(2,1)S(1)} %collective-permute-done.14.refs_1_, ...), custom_call_target="tpu_custom_call" | custom-call | flops 1073741824 | bytes 6291456 | tf_op jit(solution)/shard_map/stage/pallas_call | solution.py:98
  58.2 2.6 %stage.8.refs_4_ = f32[1024,256]{1,0:T(8,128)S(1)} custom-call(s32[4]{0:T(128)S(1)} %pad_add_fusion.1.base_ref, s32[8,64]{1,0:T(8,128)S(1)} %reshape.86.table_ref, bf16[96,128,128]{2,1,0:T(8,128)(2,1)S(1)} %copy-done.1, bf16[512,256]{1,0:T(8,128)(2,1)S(1)} %collective-permute-done.4.refs_0_, bf16[512,256]{1,0:T(8,128)(2,1)S(1)} %collective-permute-done.12.refs_1_, ...), custom_call_target="tpu_custom_call" | custom-call | flops 1073741824 | bytes 6291456 | tf_op jit(solution)/shard_map/stage/pallas_call | solution.py:98
  60.8 1.5 %stage.9 = f32[1024,256]{1,0:T(8,128)S(1)} custom-call(s32[4]{0:T(128)S(1)} %pad_add_fusion.base_ref, s32[8,64]{1,0:T(8,128)S(1)} %reshape.86.table_ref, bf16[96,128,128]{2,1,0:T(8,128)(2,1)S(1)} %copy-done.1, bf16[256,256]{1,0:T(8,128)(2,1)S(1)} %collective-permute-done.5.refs_0_, bf16[256,256]{1,0:T(8,128)(2,1)S(1)} %collective-permute-done.6.refs_1_, ...), custom_call_target="tpu_custom_call" | custom-call | flops 536870912 | bytes 4194304 | tf_op jit(solution)/shard_map/stage/pallas_call | solution.py:98
  62.5 8.3 %collective-permute-done.19 = bf16[512,256]{1,0:T(8,128)(2,1)S(1)} collective-permute-done((bf16[512,256]{1,0:T(8,128)(2,1)S(1)}, bf16[512,256]{1,0:T(8,128)(2,1)S(1)}, u32[]{:S(2)}, u32[]{:S(2)}) %collective-permute-start.19) | collective-permute-done | bytes 262176 | tf_op jit(solution)/shard_map/ppermute | solution.py:227
  70.8 0.8 %maximum_convert_fusion = bf16[512,256]{1,0:T(8,128)(2,1)} fusion(bf16[512,256]{1,0:T(8,128)(2,1)S(1)} %collective-permute-done.19, f32[256]{0:T(256)S(1)} %copy-done.5, bf16[1024,256]{1,0:T(8,128)(2,1)S(1)} %convert_element_type.13, s32[]{:T(128)S(6)} %select_n.166), kind=kLoop, calls=%fused_computation | loop fusion | flops 786432 | bytes 787460 | tf_op jit(solution)/shard_map/convert_element_type | solution.py:232
  (41 shorter events, 0.9 us)
Async XLA Ops:
  0.0 1.4 %collective-permute-start = (bf16[512,256]{1,0:T(8,128)(2,1)}, bf16[512,256]{1,0:T(8,128)(2,1)S(1)}, u32[]{:S(2)}, u32[]{:S(2)}) collective-permute-start(bf16[512,256]{1,0:T(8,128)(2,1)} %own_ref.1), channel_id=1, source_target_pairs={{2,1},{1,2},{6,5},{5,6},{10,9},{9,10},{14,13},{13,14},{18,17},{17,... | collective-permute-start | bytes 786440 | tf_op jit(solution)/shard_map/ppermute | solution.py:213
  0.7 0.7 collective-permute-start.1
  1.4 1.0 %copy-start.2 = (bf16[512,256]{1,0:T(8,128)(2,1)S(1)}, bf16[512,256]{1,0:T(8,128)(2,1)}, u32[]{:S(2)}) copy-start(bf16[512,256]{1,0:T(8,128)(2,1)} %own_ref.1) | copy-start | bytes 786436
  2.3 0.9 %copy-start.3 = (bf16[256,256]{1,0:T(8,128)(2,1)S(1)}, bf16[256,256]{1,0:T(8,128)(2,1)}, u32[]{:S(2)}) copy-start(bf16[256,256]{1,0:T(8,128)(2,1)} %weight_ref.1) | copy-start | bytes 393220
  3.2 0.7 copy-start.4
  4.5 7.4 %collective-permute-start.2 = (bf16[512,256]{1,0:T(8,128)(2,1)S(1)}, bf16[512,256]{1,0:T(8,128)(2,1)S(1)}, u32[]{:S(2)}, u32[]{:S(2)}) collective-permute-start(bf16[512,256]{1,0:T(8,128)(2,1)S(1)} %prepare.1.refs_0_), channel_id=1, source_target_pairs={{0,8},{1,9},{2,10},{3,11},{4,0},{5,1},{6,2},{7,3},{8,16},{9,17},{1... | collective-permute-start | bytes 786440 | tf_op jit(solution)/shard_map/ppermute | solution.py:177
  7.6 6.4 %collective-permute-start.7 = (bf16[512,256]{1,0:T(8,128)(2,1)S(1)}, bf16[512,256]{1,0:T(8,128)(2,1)S(1)}, u32[]{:S(2)}, u32[]{:S(2)}) collective-permute-start(bf16[512,256]{1,0:T(8,128)(2,1)S(1)} %prepare.1.refs_0_), channel_id=1, source_target_pairs={{0,4},{1,5},{2,6},{3,7},{4,12},{5,13},{6,14},{7,15},{8,0},{9,1},{1... | collective-permute-start | bytes 786440 | tf_op jit(solution)/shard_map/ppermute | solution.py:177
  11.9 25.0 %collective-permute-start.3 = (bf16[512,256]{1,0:T(8,128)(2,1)S(1)}, bf16[512,256]{1,0:T(8,128)(2,1)S(1)}, u32[]{:S(2)}, u32[]{:S(2)}) collective-permute-start(bf16[512,256]{1,0:T(8,128)(2,1)S(1)} %collective-permute-done.2.refs_0_), channel_id=1, source_target_pairs={{0,8},{1,9},{2,10},{3,11},{4,0},{5,1},{6,2},{7,3},{8,16},{9,17},{1... | collective-permute-start | bytes 786440 | tf_op jit(solution)/shard_map/ppermute | solution.py:177
  13.9 24.8 %collective-permute-start.8 = (bf16[512,256]{1,0:T(8,128)(2,1)S(1)}, bf16[512,256]{1,0:T(8,128)(2,1)S(1)}, u32[]{:S(2)}, u32[]{:S(2)}) collective-permute-start(bf16[512,256]{1,0:T(8,128)(2,1)S(1)} %collective-permute-done.7.refs_2_), channel_id=1, source_target_pairs={{0,4},{1,5},{2,6},{3,7},{4,12},{5,13},{6,14},{7,15},{8,0},{9,1},{1... | collective-permute-start | bytes 786440 | tf_op jit(solution)/shard_map/ppermute | solution.py:177
  24.9 15.5 %collective-permute-start.18 = (bf16[512,256]{1,0:T(8,128)(2,1)S(1)}, bf16[512,256]{1,0:T(8,128)(2,1)S(1)}, u32[]{:S(2)}, u32[]{:S(2)}) collective-permute-start(bf16[512,256]{1,0:T(8,128)(2,1)S(1)} %prepare.1.refs_0_), channel_id=1, source_target_pairs={{0,2},{1,3},{2,0},{3,1},{4,6},{5,7},{6,4},{7,5},{8,10},{9,11},{10,... | collective-permute-start | bytes 786440 | tf_op jit(solution)/shard_map/ppermute | solution.py:164
  36.9 4.9 %collective-permute-start.16 = (bf16[512,256]{1,0:T(8,128)(2,1)S(1)}, bf16[512,256]{1,0:T(8,128)(2,1)S(1)}, u32[]{:S(2)}, u32[]{:S(2)}) collective-permute-start(bf16[512,256]{1,0:T(8,128)(2,1)S(1)} %collective-permute-done.2.refs_0_), channel_id=1, source_target_pairs={{0,2},{1,3},{2,0},{3,1},{4,6},{5,7},{6,4},{7,5},{8,10},{9,11},{10,... | collective-permute-start | bytes 786440 | tf_op jit(solution)/shard_map/ppermute | solution.py:164
  36.9 8.7 %collective-permute-start.4 = (bf16[512,256]{1,0:T(8,128)(2,1)S(1)}, bf16[512,256]{1,0:T(8,128)(2,1)S(1)}, u32[]{:S(2)}, u32[]{:S(2)}) collective-permute-start(bf16[512,256]{1,0:T(8,128)(2,1)S(1)} %collective-permute-done.3.refs_0_), channel_id=1, source_target_pairs={{0,8},{1,9},{2,10},{3,11},{4,0},{5,1},{6,2},{7,3},{8,16},{9,17},{1... | collective-permute-start | bytes 786440 | tf_op jit(solution)/shard_map/ppermute | solution.py:177
  38.7 8.4 %collective-permute-start.9 = (bf16[512,256]{1,0:T(8,128)(2,1)S(1)}, bf16[512,256]{1,0:T(8,128)(2,1)S(1)}, u32[]{:S(2)}, u32[]{:S(2)}) collective-permute-start(bf16[512,256]{1,0:T(8,128)(2,1)S(1)} %collective-permute-done.8.refs_2_), channel_id=1, source_target_pairs={{0,4},{1,5},{2,6},{3,7},{4,12},{5,13},{6,14},{7,15},{8,0},{9,1},{1... | collective-permute-start | bytes 786440 | tf_op jit(solution)/shard_map/ppermute | solution.py:177
  40.3 6.9 %collective-permute-start.17 = (bf16[512,256]{1,0:T(8,128)(2,1)S(1)}, bf16[512,256]{1,0:T(8,128)(2,1)S(1)}, u32[]{:S(2)}, u32[]{:S(2)}) collective-permute-start(bf16[512,256]{1,0:T(8,128)(2,1)S(1)} %collective-permute-done.7.refs_2_), channel_id=1, source_target_pairs={{0,2},{1,3},{2,0},{3,1},{4,6},{5,7},{6,4},{7,5},{8,10},{9,11},{10,... | collective-permute-start | bytes 786440 | tf_op jit(solution)/shard_map/ppermute | solution.py:164
  40.4 7.6 %collective-permute-start.14 = (bf16[512,256]{1,0:T(8,128)(2,1)S(1)}, bf16[512,256]{1,0:T(8,128)(2,1)S(1)}, u32[]{:S(2)}, u32[]{:S(2)}) collective-permute-start(bf16[512,256]{1,0:T(8,128)(2,1)S(1)} %collective-permute-done.3.refs_0_), channel_id=1, source_target_pairs={{0,2},{1,3},{2,0},{3,1},{4,6},{5,7},{6,4},{7,5},{8,10},{9,11},{10,... | collective-permute-start | bytes 786440 | tf_op jit(solution)/shard_map/ppermute | solution.py:164
  41.7 14.2 %collective-permute-start.15 = (bf16[512,256]{1,0:T(8,128)(2,1)S(1)}, bf16[512,256]{1,0:T(8,128)(2,1)S(1)}, u32[]{:S(2)}, u32[]{:S(2)}) collective-permute-start(bf16[512,256]{1,0:T(8,128)(2,1)S(1)} %collective-permute-done.8.refs_2_), channel_id=1, source_target_pairs={{0,2},{1,3},{2,0},{3,1},{4,6},{5,7},{6,4},{7,5},{8,10},{9,11},{10,... | collective-permute-start | bytes 786440 | tf_op jit(solution)/shard_map/ppermute | solution.py:164
  45.6 12.6 %collective-permute-start.12 = (bf16[512,256]{1,0:T(8,128)(2,1)S(1)}, bf16[512,256]{1,0:T(8,128)(2,1)S(1)}, u32[]{:S(2)}, u32[]{:S(2)}) collective-permute-start(bf16[512,256]{1,0:T(8,128)(2,1)S(1)} %collective-permute-done.4.refs_0_), channel_id=1, source_target_pairs={{0,2},{1,3},{2,0},{3,1},{4,6},{5,7},{6,4},{7,5},{8,10},{9,11},{10,... | collective-permute-start | bytes 786440 | tf_op jit(solution)/shard_map/ppermute | solution.py:164
  47.1 11.1 %collective-permute-start.13 = (bf16[512,256]{1,0:T(8,128)(2,1)S(1)}, bf16[512,256]{1,0:T(8,128)(2,1)}, u32[]{:S(2)}, u32[]{:S(2)}) collective-permute-start(bf16[512,256]{1,0:T(8,128)(2,1)S(1)} %collective-permute-done.9.refs_2_), channel_id=1, source_target_pairs={{0,2},{1,3},{2,0},{3,1},{4,6},{5,7},{6,4},{7,5},{8,10},{9,11},{10,... | collective-permute-start | bytes 786440 | tf_op jit(solution)/shard_map/ppermute | solution.py:164
  47.3 8.1 %collective-permute-start.10 = (bf16[256,256]{1,0:T(8,128)(2,1)S(1)}, bf16[256,256]{1,0:T(8,128)(2,1)S(1)}, u32[]{:S(2)}, u32[]{:S(2)}) collective-permute-start(bf16[256,256]{1,0:T(8,128)(2,1)S(1)} %slice.17), channel_id=1, source_target_pairs={{0,4},{1,5},{2,6},{3,7},{4,12},{5,13},{6,14},{7,15},{8,0},{9,1},{1... | collective-permute-start | bytes 393224 | tf_op jit(solution)/shard_map/ppermute | solution.py:180
  48.0 7.4 %collective-permute-start.5 = (bf16[256,256]{1,0:T(8,128)(2,1)S(1)}, bf16[256,256]{1,0:T(8,128)(2,1)S(1)}, u32[]{:S(2)}, u32[]{:S(2)}) collective-permute-start(bf16[256,256]{1,0:T(8,128)(2,1)S(1)} %slice.16), channel_id=1, source_target_pairs={{0,8},{1,9},{2,10},{3,11},{4,0},{5,1},{6,2},{7,3},{8,16},{9,17},{1... | collective-permute-start | bytes 393224 | tf_op jit(solution)/shard_map/ppermute | solution.py:180
  49.3 1.9 %copy-start = (bf16[96,128,128]{2,1,0:T(8,128)(2,1)S(1)}, bf16[96,128,128]{2,1,0:T(8,128)(2,1)}, u32[]{:S(2)}) copy-start(bf16[96,128,128]{2,1,0:T(8,128)(2,1)} %tiles_ref.9) | copy-start | bytes 9437188
  51.2 1.9 %copy-start.1 = (bf16[96,128,128]{2,1,0:T(8,128)(2,1)S(1)}, bf16[96,128,128]{2,1,0:T(8,128)(2,1)}, u32[]{:S(2)}) copy-start(bf16[96,128,128]{2,1,0:T(8,128)(2,1)} %tiles_ref.9) | copy-start | bytes 9437188
  55.4 5.4 %collective-permute-start.11 = (bf16[256,256]{1,0:T(8,128)(2,1)S(1)}, bf16[256,256]{1,0:T(8,128)(2,1)S(1)}, u32[]{:S(2)}, u32[]{:S(2)}) collective-permute-start(bf16[256,256]{1,0:T(8,128)(2,1)S(1)} %collective-permute-done.10.refs_2_), channel_id=1, source_target_pairs={{0,2},{1,3},{2,0},{3,1},{4,6},{5,7},{6,4},{7,5},{8,10},{9,11},{10,... | collective-permute-start | bytes 393224 | tf_op jit(solution)/shard_map/ppermute | solution.py:164
  55.4 5.3 %collective-permute-start.6 = (bf16[256,256]{1,0:T(8,128)(2,1)S(1)}, bf16[256,256]{1,0:T(8,128)(2,1)S(1)}, u32[]{:S(2)}, u32[]{:S(2)}) collective-permute-start(bf16[256,256]{1,0:T(8,128)(2,1)S(1)} %collective-permute-done.5.refs_0_), channel_id=1, source_target_pairs={{0,2},{1,3},{2,0},{3,1},{4,6},{5,7},{6,4},{7,5},{8,10},{9,11},{10,... | collective-permute-start | bytes 393224 | tf_op jit(solution)/shard_map/ppermute | solution.py:164
  60.8 10.0 %copy-start.5 = (f32[256]{0:T(256)S(1)}, f32[256]{0:T(256)}, u32[]{:S(2)}) copy-start(f32[256]{0:T(256)} %param.12) | copy-start | bytes 3076
  62.4 8.4 %collective-permute-start.19 = (bf16[512,256]{1,0:T(8,128)(2,1)S(1)}, bf16[512,256]{1,0:T(8,128)(2,1)S(1)}, u32[]{:S(2)}, u32[]{:S(2)}) collective-permute-start(bf16[512,256]{1,0:T(8,128)(2,1)S(1)} %constant_dynamic-slice_fusion), channel_id=1, source_target_pairs={{0,1},{1,0},{2,3},{3,2},{4,5},{5,4},{6,7},{7,6},{8,9},{9,8},{10,11... | collective-permute-start | bytes 786440 | tf_op jit(solution)/shard_map/ppermute | solution.py:227

commit v2 on v0

v2 whole, which is shorter than its diff:
```python
import functools
import jax
import jax.numpy as jnp
from jax import lax
from jax.experimental import pallas as pl
from jax.experimental.pallas import tpu as pltpu
from jax.sharding import PartitionSpec as P

AXES = ("rows", "rep")
MIB = 1024 * 1024
VMEM = pl.BlockSpec(memory_space=pltpu.VMEM)
ANY = pl.BlockSpec(memory_space=pl.ANY)
HBM = pl.BlockSpec(memory_space=pltpu.HBM)


def in_hbm(*arrays):
    return [pltpu.with_memory_space_constraint(a, pltpu.HBM) for a in arrays]


def cost(flops, moved):
    return pl.CostEstimate(flops=flops, bytes_accessed=moved, transcendentals=0)


def prepare_kernel(rows_hbm, order_hbm, weight_hbm, out_ref, rows, order, weight, sems):
    copies = [
        pltpu.make_async_copy(src, dst, sems.at[i])
        for i, (src, dst) in enumerate(
            ((order_hbm, order), (weight_hbm, weight), (rows_hbm, rows))
        )
    ]
    for copy in copies:
        copy.start()
    shard_rows = rows.shape[0]
    copies[0].wait()
    within = lax.rem(order[...], shard_rows)
    node = lax.broadcasted_iota(jnp.int32, (shard_rows, shard_rows), 0)
    chosen = (node == within).astype(jnp.float32).astype(jnp.bfloat16)
    copies[1].wait()
    copies[2].wait()
    projected = jnp.dot(rows[...], weight[...], preferred_element_type=jnp.float32)
    out_ref[...] = lax.dot_general(
        chosen,
        projected.astype(jnp.bfloat16),
        (((0,), (0,)), ((), ())),
        preferred_element_type=jnp.float32,
    ).astype(jnp.bfloat16)


def prepare(features, node_order, weight):
    shard_rows, width = features.shape
    order = node_order.reshape(1, shard_rows)
    return pl.pallas_call(
        prepare_kernel,
        out_shape=jax.ShapeDtypeStruct(features.shape, features.dtype),
        in_specs=[HBM] * 3,
        out_specs=VMEM,
        scratch_shapes=[
            pltpu.VMEM(features.shape, features.dtype),
            pltpu.VMEM(order.shape, jnp.int32),
            pltpu.VMEM(weight.shape, weight.dtype),
            pltpu.SemaphoreType.DMA((3,)),
        ],
        compiler_params=pltpu.CompilerParams(vmem_limit_bytes=4 * MIB),
        cost_estimate=cost(4 * shard_rows * shard_rows * width, 4 * features.size),
        name="prepare",
    )(*in_hbm(features, order, weight))


def ring_chip(place, chips):
    return 2 * place if place < chips // 2 else 2 * (chips - 1 - place) + 1


def ring_place(chip, chips):
    return jnp.where(chip % 2 == 0, chip // 2, chips - 1 - chip // 2)


class Layout:
    def __init__(self, halves, sections, replicas, tile_rows, groups, tile, slots):
        self.halves, self.sections, self.replicas = halves, sections, replicas
        self.tile_rows, self.groups, self.tile, self.slots = tile_rows, groups, tile, slots
        self.width = tile_rows // 2 if halves else tile_rows
        spans = [1] + [2] * (sections // 2 - 1) + [1] if halves else [1] * sections
        self.widths = [self.width * span for span in spans]
        self.rows = groups * tile_rows
        self.line = -(-self.rows * max(self.widths) // 128) * 128

    def block(self, stage):
        return (self.rows * self.tile, self.widths[stage] * self.tile)


def plan(layout, counts, coords, table):
    sections, width, line = layout.sections, layout.width, layout.line
    row = lax.axis_index("rows")
    core = lax.rem(row, layout.replicas)
    shape = (layout.slots, layout.slots)
    square = [lax.broadcasted_iota(jnp.int32, shape, axis) for axis in (0, 1)]
    lane = lax.broadcasted_iota(jnp.int32, (1, layout.slots), 1)
    entry = lax.broadcasted_iota(jnp.int32, (layout.slots, 1), 0)
    at = lax.broadcasted_iota(jnp.int32, (1, line), 1)
    lines = [None] * len(layout.widths)
    for g in range(layout.groups):
        block_row = row if g == 0 else row + 1 - 2 * core
        tile_row, column = coords[g, 0:1], coords[g, 1:2]
        tile_row = tile_row + (g - block_row) * layout.tile_rows
        step = column // (layout.tile_rows * layout.replicas)
        across, right = width, 0
        wanted = lane < counts[g][0]
        if layout.halves:
            ahead = ring_place(step, sections) - ring_place(row // layout.replicas, sections)
            ahead = jnp.where(ahead < 0, ahead + sections, ahead)
            step = jnp.minimum(ahead, sections - ahead)
            middle = (step > 0) & (2 * step < sections)
            across = jnp.where(middle, 2 * width, width)
            right = jnp.where(middle & (ahead == step), width, 0)
            wanted = wanted & ((column // width) % 2 == core)
        code = step * line + tile_row * across + right + column % width
        code = jnp.where(wanted, code, -1).astype(jnp.float32)
        code = jnp.sum(jnp.where(square[0] == square[1], code, 0.0), axis=1, keepdims=True)
        code = code.astype(jnp.int32)
        for i in range(len(lines)):
            found = jnp.where(code == at + i * line, entry + g * layout.slots, -1)
            found = jnp.max(found.astype(jnp.float32), axis=0, keepdims=True)
            lines[i] = found if g == 0 else jnp.maximum(lines[i], found)
    for i, found in enumerate(lines):
        table[i : i + 1] = found.astype(jnp.int32)


def fill(layout, stage, table, tiles, block, sem):
    tile, width = layout.tile, layout.widths[stage]
    strip = 32

    @pl.loop(0, block.shape[0], step=strip)
    def _(top):
        rows = pl.ds(pl.multiple_of(top, strip), strip)
        block[rows] = jnp.zeros((strip, block.shape[1]), block.dtype)

    started = jnp.int32(0)
    for g in range(layout.groups):

        def line(row, started, g=g):
            row = row + g * layout.tile_rows
            top = pl.ds(pl.multiple_of(row * tile, tile), tile)
            for c in range(width):
                entry = table[stage, row * width + c]

                @pl.when(entry >= 0)
                def _(entry=entry, c=c):
                    target = block.at[top, c * tile : (c + 1) * tile]
                    source = tiles[g].at[entry - g * layout.slots]
                    pltpu.make_async_copy(source, target, sem).start()

                started = started + (entry >= 0).astype(jnp.int32)
            return started

        started = lax.fori_loop(0, layout.tile_rows, line, started)
    return started


def finish_fill(layout, tiles, started, sem):
    size = 1
    while size <= layout.slots * layout.groups:

        @pl.when((started & size) != 0)
        def _(size=size):
            for first in range(0, size, layout.slots):
                some = tiles[0].at[pl.ds(0, min(layout.slots, size - first))]
                pltpu.make_async_copy(some, some, sem).wait()

        size *= 2


def multiply(block, pieces, total, out, first_row=0, more=None):
    strip = min(256, out.shape[0])
    for top in range(0, out.shape[0], strip):
        at = pl.ds(pl.multiple_of(first_row + top, strip), strip)
        result = total[at] if total is not None else None
        if more is not None:
            result += more[top : top + strip].astype(jnp.float32)
        column = 0
        for piece in pieces:
            product = jnp.dot(
                block[at, column : column + piece.shape[0]],
                piece[...],
                preferred_element_type=jnp.float32,
            )
            result = product if result is None else result + product
            column += piece.shape[0]
        out[top : top + strip] = result.astype(out.dtype)


def first_kernel(layout, *refs):
    groups = layout.groups
    counts, coords_hbm, tiles = (refs[i * groups : (i + 1) * groups] for i in range(3))
    piece, table, block, total, first, coords, entries, coords_sems, sems = refs[3 * groups :]
    loads = [
        pltpu.make_async_copy(coords_hbm[g], coords.at[g], coords_sems.at[g])
        for g in range(groups)
    ]
    for load in loads:
        load.start()
    for load in loads:
        load.wait()
    plan(layout, counts, coords, table)
    load = pltpu.make_async_copy(table, entries, coords_sems.at[0])
    load.start()
    load.wait()
    started = fill(layout, 0, entries, tiles, first, sems.at[0])
    more = fill(layout, 1, entries, tiles, block, sems.at[1])
    finish_fill(layout, tiles, started, sems.at[0])
    multiply(first, [piece], None, total)
    finish_fill(layout, tiles, more, sems.at[1])


def next_kernel(layout, stage, n_pieces, *refs):
    groups = layout.groups
    table, tiles = refs[0], refs[1 : 1 + groups]
    block, *pieces = refs[1 + groups : 2 + groups + n_pieces]
    total, next_block, next_total, sem = refs[2 + groups + n_pieces :]
    started = fill(layout, stage + 1, table, tiles, next_block, sem)
    multiply(block, pieces, total, next_total)
    finish_fill(layout, tiles, started, sem)


def last_kernel(n_pieces, which, has_more, block, *refs):
    pieces, total, out = refs[:n_pieces], refs[n_pieces], refs[-1]
    more = refs[n_pieces + 1] if has_more else None
    multiply(block, pieces, total, out, which() * out.shape[0], more)


SMEM = pl.BlockSpec(memory_space=pltpu.SMEM)
PARAMS = pltpu.CompilerParams(vmem_limit_bytes=16 * MIB)


def in_vmem(*arrays):
    return [pltpu.with_memory_space_constraint(a, pltpu.VMEM) for a in arrays]


def stage_cost(layout, stage, width):
    rows, depth = layout.block(stage)
    return cost(2 * rows * depth * width, 4 * rows * depth + 8 * rows * width)


def first_stage(layout, groups, piece):
    counts, coords, tiles = zip(*groups)
    n, width = layout.groups, piece.shape[1]
    coords = [c.T for c in coords]
    dtype = tiles[0].dtype
    return pl.pallas_call(
        functools.partial(first_kernel, layout),
        out_shape=[
            pltpu.VMEM((len(layout.widths), layout.line), jnp.int32),
            pltpu.VMEM(layout.block(1), dtype),
            pltpu.VMEM((layout.block(0)[0], width), jnp.float32),
        ],
        in_specs=[SMEM] * n + [ANY] * 2 * n + [VMEM],
        out_specs=[VMEM] * 3,
        scratch_shapes=[
            pltpu.VMEM(layout.block(0), dtype),
            pltpu.VMEM((n, *coords[0].shape), jnp.int32),
            pltpu.SMEM((len(layout.widths), layout.line), jnp.int32),
            pltpu.SemaphoreType.DMA((n,)),
            pltpu.SemaphoreType.DMA((2,)),
        ],
        compiler_params=PARAMS,
        cost_estimate=stage_cost(layout, 0, width),
        name="first_stage",
    )(*counts, *in_hbm(coords[0]), *coords[1:], *in_hbm(tiles[0]), *tiles[1:], *in_vmem(piece))


def next_stage(layout, stage, table, groups, block, pieces, total):
    tiles = [g[2] for g in groups]
    width = total.shape[1]
    held = in_vmem(block, *pieces, total)
    return pl.pallas_call(
        functools.partial(next_kernel, layout, stage, len(pieces)),
        out_shape=[
            pltpu.VMEM(layout.block(stage + 1), block.dtype),
            pltpu.VMEM(total.shape, total.dtype),
        ],
        in_specs=[SMEM] + [ANY] * layout.groups + [VMEM] * len(held),
        out_specs=[VMEM] * 2,
        scratch_shapes=[pltpu.SemaphoreType.DMA],
        compiler_params=PARAMS,
        cost_estimate=stage_cost(layout, stage, width),
        name="next_stage",
    )(table, *in_hbm(tiles[0]), *tiles[1:], *held)


def last_stage(block, pieces, total, part, more=None, dtype=jnp.bfloat16):
    which, rows = part
    width, depth = total.shape[1], block.shape[1]
    held = in_vmem(block, *pieces, total, *([] if more is None else [more]))
    return pl.pallas_call(
        functools.partial(last_kernel, len(pieces), which, more is not None),
        out_shape=jax.ShapeDtypeStruct((rows, width), dtype),
        in_specs=[VMEM] * len(held),
        out_specs=VMEM,
        compiler_params=PARAMS,
        cost_estimate=cost(2 * rows * depth * width, 2 * rows * depth + 8 * rows * width),
        name="last_stage",
    )(*held)


def device_id(row, rep, replicas):
    return row * replicas + rep


def core_pairs(row_count, replicas):
    return [
        (device_id(row, rep, replicas), device_id(row ^ 1, rep, replicas))
        for row in range(row_count)
        for rep in range(replicas)
    ]


def ring_stages(own, groups, layout):
    replicas, row_count = lax.axis_size("rep"), lax.axis_size("rows")
    chips = row_count // replicas
    ring = [ring_chip(i, chips) for i in range(chips)]

    def around(step):
        return [
            (
                device_id(ring[p] * replicas + c, r, replicas),
                device_id(ring[(p + step) % chips] * replicas + c, r, replicas),
            )
            for p in range(chips)
            for c in range(replicas)
            for r in range(replicas)
        ]

    up, down = around(1), around(-1)
    rows, far = own.shape[0], chips // 2
    left = right = own
    for step in range(far):
        if step == far - 1:
            left, right = left[: rows // 2], right[rows // 2 :]
        left, right = lax.ppermute(left, AXES, up), lax.ppermute(right, AXES, down)
        if step == 0:
            table, block, total = first_stage(layout, groups, own)
        else:
            block, total = next_stage(layout, step, table, groups, block, pieces, total)
        left, right, total = lax.optimization_barrier((left, right, total))
        pieces = [left, right]

    parts = block.shape[0] // rows // 2

    def finish(whose, near, more=None, dtype=jnp.bfloat16):
        def which():
            rep = lax.axis_index("rep")
            return whose * parts + (rep if near else 1 - rep)

        return last_stage(block, pieces, total, (which, rows), more, dtype)

    trade = core_pairs(row_count, replicas)
    theirs = lax.ppermute(finish(1, False), AXES, trade)
    mine = lax.ppermute(finish(1, True), AXES, trade)
    got = lax.ppermute(finish(0, False, theirs), "rep", [(0, 1), (1, 0)])
    return finish(0, True, mine, jnp.float32), got


def gathered_stages(own, groups, layout):
    panels = lax.all_gather(own, "rows", axis=0, tiled=True)
    shard_rows = own.shape[0]
    replicas, rep = lax.axis_size("rep"), lax.axis_index("rep")
    depth, last = layout.block(0)[1], layout.sections - 1
    pieces = [panels[i * depth : (i + 1) * depth] for i in range(last + 1)]
    table, block, total = first_stage(layout, groups, pieces[0])
    for i in range(1, last):
        block, total = next_stage(layout, i, table, groups, block, [pieces[i]], total)
    total = last_stage(block, [pieces[last]], total, (lambda: 0, depth), None, jnp.float32)
    total = total.astype(jnp.bfloat16)

    def part(of):
        return lax.dynamic_slice_in_dim(total, of * shard_rows, shard_rows, 0)

    kept, got = part(rep).astype(jnp.float32), 0.0
    for step in range(1, replicas):
        got += lax.ppermute(
            part((rep + step) % replicas),
            "rep",
            [(r, (r + step) % replicas) for r in range(replicas)],
        ).astype(jnp.float32)
    return kept, got


def shards(features, node_order, layer_weight, layer_bias, tile_values, tile_coords, tile_count):
    shard_rows = features.shape[0]
    replicas, row_count = lax.axis_size("rep"), lax.axis_size("rows")
    rep, row = lax.axis_index("rep"), lax.axis_index("rows")
    tile_rows = shard_rows * replicas // tile_values.shape[1]
    trade = [
        (
            device_id(s * replicas + c, r, replicas),
            device_id(s * replicas + r, c, replicas),
        )
        for s in range(row_count // replicas)
        for r in range(replicas)
        for c in range(replicas)
        if r != c
    ]
    groups = [(tile_count, tile_coords, tile_values)]
    ring = replicas == 2
    if ring:
        pairs = core_pairs(row_count, replicas)
        count, coords = (lax.ppermute(x, AXES, pairs) for x in groups[0][:2])
    own = prepare(features, node_order, layer_weight)
    if ring:
        own, tiles, count, coords = lax.optimization_barrier((own, tile_values, count, coords))
        groups.append((count, coords, lax.ppermute(tiles, AXES, pairs)))
    got = lax.ppermute(own, AXES, trade)
    own = jnp.where(row % replicas == rep, own, got)
    sections = row_count // replicas
    slots, tile = tile_values.shape[:2]
    layout = Layout(ring, sections, replicas, tile_rows, len(groups), tile, slots)
    kept, got = (ring_stages if ring else gathered_stages)(own, groups, layout)
    return jax.nn.relu(kept + got + layer_bias).astype(jnp.bfloat16)


def solution(mesh):
    placed = (
        P(("rows", "rep"), None),
        P(("rows", "rep")),
        P(),
        P(),
        P(("rows", "rep"), None, None),
        P(("rows", "rep"), None),
        P(("rows", "rep")),
    )
    return jax.shard_map(
        shards, mesh=mesh, in_specs=placed, out_specs=P(("rows", "rep"), None), check_vma=False
    )
```

time: 215 us -> 57.5 us (0.27)
  waiting for transfers between devices: 129 us -> 14.8 us
  local copies, waits for them, and re-layouts: 35.2 us -> 0.03 us
  starting transfers between devices: 0.04 us -> 23 us
  matrix products: 19.2 us -> 0 us
  Pallas kernels: 0 us -> 17.9 us
  between operations: 14.1 us -> 0.78 us
  blocking collectives: 10 us -> 0 us
  other arithmetic: 6.48 us -> 0.81 us
    psum x1 -> x0, waiting for transfers between devices: 115 us -> none  [broadcast(): return lax.psum(jnp.where(mine, x, jnp.zeros_like(x)), axis)]
    ppermute x0 -> x15, starting transfers between devices: none -> 23 us  [the longest x1 8.37 us: ring_stages(): got = lax.ppermute(finish(0, False, theirs), 'rep', [(0, 1), (1, 0)])]
    dot_general x3 -> x0, matrix products: 19.2 us -> none  [the longest x1 9.16 us: tile_products(): jnp.einsum('tij,tjf->tif', tile_values, gathered, preferred_element_type=...]
    pallas_call x0 -> x9, Pallas kernels: none -> 17.9 us  [the longest x3 9.82 us: next_stage(): pl.pallas_call(functools.partial(next_kernel, layout, stage, len(pieces))...]
    ppermute x0 -> x15, waiting for transfers between devices: none -> 14.8 us  [the longest x1 6.3 us: ring_stages(): got = lax.ppermute(finish(0, False, theirs), 'rep', [(0, 1), (1, 0)])]
    reduce_scatter x1 -> x0, waiting for transfers between devices: 14.6 us -> none  [shards(): lax.psum_scatter(group_partial, 'rep', scatter_dimension=0, tiled=True)]
    dot_general x1 -> x0, local copies, waits for them, and re-layouts: 12.6 us -> none  [tile_products(): jnp.einsum('tij,tjf->tif', tile_values, gathered, preferred_element_type=...]
    gather x2 -> x0, local copies, waits for them, and re-layouts: 10.7 us -> none  [the longest x1 8.12 us: tile_products(): gathered = flat_panels[slot_ids]]
  transfers between devices with their start and end apart: 2 -> 15, of which waited for: 2 -> 9; matrix products, arithmetic and copies ran while one was open for 0% -> 0% of each run, Pallas kernels for 0% -> 31%
where the time goes in v2:
time: 57.5 us; the launch traced here: 57.3 us
  starting transfers between devices  23 us (40%)
  Pallas kernels  17.9 us (31%)
  waiting for transfers between devices  14.8 us (26%)
  other arithmetic  0.81 us (1%)
  between operations  0.78 us (1%)
    pallas_call x3, Pallas kernels, next_stage(): pl.pallas_call(functools.partial(next_kernel, layout, stage, len(pieces))...  9.82 us
    ppermute x1, starting transfers between devices, ring_stages(): got = lax.ppermute(finish(0, False, theirs), 'rep', [(0, 1), (1, 0)])  8.37 us
    ppermute x4, starting transfers between devices, ring_stages(): lax.ppermute(left, AXES, up)  6.31 us
    ppermute x1, waiting for transfers between devices, ring_stages(): got = lax.ppermute(finish(0, False, theirs), 'rep', [(0, 1), (1, 0)])  6.3 us
    pallas_call x1, Pallas kernels, first_stage(): pl.pallas_call(functools.partial(first_kernel, layout), out_shape=[pltpu....  5.25 us
    ppermute x4, waiting for transfers between devices, ring_stages(): lax.ppermute(left, AXES, up)  4.55 us
    ppermute x4, starting transfers between devices, ring_stages(): lax.ppermute(right, AXES, down)  3.51 us
    ppermute x4, waiting for transfers between devices, ring_stages(): lax.ppermute(right, AXES, down)  2.41 us
  transfers between devices with their start and end apart: 15, of which 9 were waited for; matrix products, arithmetic and copies ran while one was open for 0% of the time, Pallas kernels for 31%

profile of v2, /device:TPU:0, one launch (start us, length us, event | category | flops | bytes accessed | tf_op | source)
XLA Modules:
  0.0 57.3 jit_solution(3874275214180714304)
XLA Ops:
  0.0 0.5 collective-permute-start
  0.5 0.1 collective-permute-start.1
  0.5 1.6 %prepare.1 = bf16[512,256]{1,0:T(8,128)(2,1)S(1)} custom-call(bf16[512,256]{1,0:T(8,128)(2,1)} %rows_hbm.1, s32[1,512]{1,0:T(1,128)} %bitcast.5, bf16[256,256]{1,0:T(8,128)(2,1)} %weight_hbm.1), custom_call_target="tpu_custom_call" | custom-call | flops 268435456 | bytes 524288 | tf_op jit(solution)/shard_map/prepare/pallas_call | solution.py:52
  2.2 0.5 collective-permute-start.2
  2.7 1.3 %collective-permute-start.3 = (bf16[512,256]{1,0:T(8,128)(2,1)S(1)}, bf16[512,256]{1,0:T(8,128)(2,1)}, u32[]{:S(2)}, u32[]{:S(2)}) collective-permute-start(bf16[512,256]{1,0:T(8,128)(2,1)S(1)} %prepare.1), channel_id=1, source_target_pairs={{2,1},{1,2},{6,5},{5,6},{10,9},{9,10},{14,13},{13,14},{18,17},{17,... | collective-permute-start | bytes 786440 | tf_op jit(solution)/shard_map/ppermute | solution.py:411
  4.1 2.6 %collective-permute-start.5 = (bf16[512,256]{1,0:T(8,128)(2,1)S(1)}, bf16[512,256]{1,0:T(8,128)(2,1)S(1)}, u32[]{:S(2)}, u32[]{:S(2)}) collective-permute-start(bf16[512,256]{1,0:T(8,128)(2,1)S(1)} %broadcast_select_fusion.refs_6_), channel_id=1, source_target_pairs={{0,4},{1,5},{2,6},{3,7},{8,0},{9,1},{10,2},{11,3},{16,8},{17,9},{1... | collective-permute-start | bytes 786440 | tf_op jit(solution)/shard_map/ppermute | solution.py:338
  6.7 0.1 collective-permute-start.4
  7.4 0.7 %collective-permute-done.2.refs_5_.refs_2_ = bf16[96,128,128]{2,1,0:T(8,128)(2,1)S(1)} collective-permute-done((bf16[96,128,128]{2,1,0:T(8,128)(2,1)}, bf16[96,128,128]{2,1,0:T(8,128)(2,1)S(1)}, u32[]{:S(2)}, u32[]{:S(2)}) %collective-permute-start.2) | collective-permute-done | bytes 3145760 | tf_op jit(solution)/shard_map/ppermute | solution.py:410
  8.2 5.2 %first_stage.1 = (s32[5,128]{1,0:T(8,128)S(1)}, bf16[2048,1024]{1,0:T(8,128)(2,1)S(1)}, f32[2048,256]{1,0:T(8,128)S(1)}) custom-call(s32[1]{0:T(128)S(6)} %copy.8.refs_0_, s32[1]{0:T(128)} %collective-permute-done.refs_1_, s32[2,96]{1,0:T(2,128)} %bitcast.4, s32[2,96]{1,0:T(2,128)S(1)} %bitcast.3, bf16[96,128,128]{2,1,0:T(8,128)(2,1)} %refs_1_.5, ...), custom_call_target="tpu_custom_call" | custom-call | flops 536870912 | bytes 8388608 | tf_op jit(solution)/shard_map/first_stage/pallas_call | solution.py:248
  13.5 3.0 %collective-permute-start.6 = (bf16[512,256]{1,0:T(8,128)(2,1)S(1)}, bf16[512,256]{1,0:T(8,128)(2,1)S(1)}, u32[]{:S(2)}, u32[]{:S(2)}) collective-permute-start(bf16[512,256]{1,0:T(8,128)(2,1)S(1)} %collective-permute-done.4.refs_4_), channel_id=1, source_target_pairs={{0,8},{1,9},{2,10},{3,11},{8,16},{9,17},{10,18},{11,19},{16,24},{1... | collective-permute-start | bytes 786440 | tf_op jit(solution)/shard_map/ppermute | solution.py:338
  16.5 3.5 %next_stage.3 = (bf16[2048,1024]{1,0:T(8,128)(2,1)S(1)}, f32[2048,256]{1,0:T(8,128)S(1)}) custom-call(s32[5,128]{1,0:T(8,128)S(1)} %get-tuple-element.34.refs_0_, bf16[96,128,128]{2,1,0:T(8,128)(2,1)} %refs_1_.5, bf16[96,128,128]{2,1,0:T(8,128)(2,1)S(1)} %collective-permute-done.2.refs_5_.refs_2_, bf16[2048,1024]{1,0:T(8,128)(2,1)S(1)} %get-tuple-element.35.refs_3_, ...), custom_call_target="tpu_custom_call" | custom-call | flops 1073741824 | bytes 12582912 | tf_op jit(solution)/shard_map/next_stage/pallas_call | solution.py:274
  19.9 2.7 %collective-permute-done.6.refs_4_ = bf16[512,256]{1,0:T(8,128)(2,1)S(1)} collective-permute-done((bf16[512,256]{1,0:T(8,128)(2,1)S(1)}, bf16[512,256]{1,0:T(8,128)(2,1)S(1)}, u32[]{:S(2)}, u32[]{:S(2)}) %collective-permute-start.6) | collective-permute-done | bytes 262176 | tf_op jit(solution)/shard_map/ppermute | solution.py:338
  22.6 0.2 collective-permute-done.7.refs_5_
  22.8 1.6 %collective-permute-start.8 = (bf16[512,256]{1,0:T(8,128)(2,1)S(1)}, bf16[512,256]{1,0:T(8,128)(2,1)S(1)}, u32[]{:S(2)}, u32[]{:S(2)}) collective-permute-start(bf16[512,256]{1,0:T(8,128)(2,1)S(1)} %collective-permute-done.6.refs_4_), channel_id=1, source_target_pairs={{0,8},{1,9},{2,10},{3,11},{8,16},{9,17},{10,18},{11,19},{16,24},{1... | collective-permute-start | bytes 786440 | tf_op jit(solution)/shard_map/ppermute | solution.py:338
  24.4 0.4 collective-permute-start.9
  24.8 3.5 %next_stage.4 = (bf16[2048,1024]{1,0:T(8,128)(2,1)S(1)}, f32[2048,256]{1,0:T(8,128)S(1)}) custom-call(s32[5,128]{1,0:T(8,128)S(1)} %get-tuple-element.34.refs_0_, bf16[96,128,128]{2,1,0:T(8,128)(2,1)} %refs_1_.5, bf16[96,128,128]{2,1,0:T(8,128)(2,1)S(1)} %collective-permute-done.2.refs_5_.refs_2_, bf16[2048,1024]{1,0:T(8,128)(2,1)S(1)} %get-tuple-element.40.refs_3_, ...), custom_call_target="tpu_custom_call" | custom-call | flops 1073741824 | bytes 12582912 | tf_op jit(solution)/shard_map/next_stage/pallas_call | solution.py:274
  28.3 1.8 %collective-permute-done.8.refs_4_ = bf16[512,256]{1,0:T(8,128)(2,1)S(1)} collective-permute-done((bf16[512,256]{1,0:T(8,128)(2,1)S(1)}, bf16[512,256]{1,0:T(8,128)(2,1)S(1)}, u32[]{:S(2)}, u32[]{:S(2)}) %collective-permute-start.8) | collective-permute-done | bytes 262176 | tf_op jit(solution)/shard_map/ppermute | solution.py:338
  30.1 0.7 %collective-permute-done.9.refs_5_ = bf16[512,256]{1,0:T(8,128)(2,1)S(1)} collective-permute-done((bf16[512,256]{1,0:T(8,128)(2,1)S(1)}, bf16[512,256]{1,0:T(8,128)(2,1)S(1)}, u32[]{:S(2)}, u32[]{:S(2)}) %collective-permute-start.9) | collective-permute-done | bytes 262176 | tf_op jit(solution)/shard_map/ppermute | solution.py:338
  30.8 1.6 %collective-permute-start.10 = (bf16[256,256]{1,0:T(8,128)(2,1)S(1)}, bf16[256,256]{1,0:T(8,128)(2,1)S(1)}, u32[]{:S(2)}, u32[]{:S(2)}) collective-permute-start(bf16[256,256]{1,0:T(8,128)(2,1)S(1)} %slice.6), channel_id=1, source_target_pairs={{0,8},{1,9},{2,10},{3,11},{8,16},{9,17},{10,18},{11,19},{16,24},{1... | collective-permute-start | bytes 393224 | tf_op jit(solution)/shard_map/ppermute | solution.py:338
  32.4 0.5 collective-permute-start.11
  32.9 2.9 %next_stage.5 = (bf16[2048,512]{1,0:T(8,128)(2,1)S(1)}, f32[2048,256]{1,0:T(8,128)S(1)}) custom-call(s32[5,128]{1,0:T(8,128)S(1)} %get-tuple-element.34.refs_0_, bf16[96,128,128]{2,1,0:T(8,128)(2,1)} %refs_1_.5, bf16[96,128,128]{2,1,0:T(8,128)(2,1)S(1)} %collective-permute-done.2.refs_5_.refs_2_, bf16[2048,1024]{1,0:T(8,128)(2,1)S(1)} %get-tuple-element.45.refs_3_, ...), custom_call_target="tpu_custom_call" | custom-call | flops 1073741824 | bytes 12582912 | tf_op jit(solution)/shard_map/next_stage/pallas_call | solution.py:274
  35.8 1.6 %collective-permute-done.11.refs_1_ = bf16[256,256]{1,0:T(8,128)(2,1)S(1)} collective-permute-done((bf16[256,256]{1,0:T(8,128)(2,1)S(1)}, bf16[256,256]{1,0:T(8,128)(2,1)S(1)}, u32[]{:S(2)}, u32[]{:S(2)}) %collective-permute-start.11) | collective-permute-done | bytes 131104 | tf_op jit(solution)/shard_map/ppermute | solution.py:338
  37.4 0.3 last_stage.6
  37.7 2.4 %collective-permute-start.13 = (bf16[512,256]{1,0:T(8,128)(2,1)S(1)}, bf16[512,256]{1,0:T(8,128)(2,1)S(1)}, u32[]{:S(2)}, u32[]{:S(2)}) collective-permute-start(bf16[512,256]{1,0:T(8,128)(2,1)S(1)} %last_stage.6), channel_id=1, source_target_pairs={{0,2},{1,3},{2,0},{3,1},{4,6},{5,7},{6,4},{7,5},{8,10},{9,11},{10,... | collective-permute-start | bytes 786440 | tf_op jit(solution)/shard_map/ppermute | solution.py:356
  40.1 0.3 last_stage.4
  40.4 0.1 collective-permute-start.12
  40.5 0.8 %collective-permute-done.13.refs_3_ = bf16[512,256]{1,0:T(8,128)(2,1)S(1)} collective-permute-done((bf16[512,256]{1,0:T(8,128)(2,1)S(1)}, bf16[512,256]{1,0:T(8,128)(2,1)S(1)}, u32[]{:S(2)}, u32[]{:S(2)}) %collective-permute-start.13) | collective-permute-done | bytes 262176 | tf_op jit(solution)/shard_map/ppermute | solution.py:356
  41.3 0.3 last_stage.7
  41.6 8.4 %collective-permute-start.14 = (bf16[512,256]{1,0:T(8,128)(2,1)S(1)}, bf16[512,256]{1,0:T(8,128)(2,1)S(1)}, u32[]{:S(2)}, u32[]{:S(2)}) collective-permute-start(bf16[512,256]{1,0:T(8,128)(2,1)S(1)} %last_stage.7), channel_id=1, source_target_pairs={{0,1},{1,0},{2,3},{3,2},{4,5},{5,4},{6,7},{7,6},{8,9},{9,8},{10,11... | collective-permute-start | bytes 786440 | tf_op jit(solution)/shard_map/ppermute | solution.py:358
  49.9 0.3 last_stage.5
  50.3 6.3 %collective-permute-done.14 = bf16[512,256]{1,0:T(8,128)(2,1)S(1)} collective-permute-done((bf16[512,256]{1,0:T(8,128)(2,1)S(1)}, bf16[512,256]{1,0:T(8,128)(2,1)S(1)}, u32[]{:S(2)}, u32[]{:S(2)}) %collective-permute-start.14) | collective-permute-done | bytes 262176 | tf_op jit(solution)/shard_map/ppermute | solution.py:358
  56.6 0.8 %maximum_convert_fusion = bf16[512,256]{1,0:T(8,128)(2,1)} fusion(f32[512,256]{1,0:T(8,128)S(1)} %last_stage.5, bf16[512,256]{1,0:T(8,128)(2,1)S(1)} %collective-permute-done.14, f32[256]{0:T(256)S(1)} %copy-done), kind=kLoop, calls=%fused_computation | loop fusion | flops 655360 | bytes 1049600 | tf_op jit(solution)/shard_map/convert_element_type | solution.py:417
  (13 shorter events, 0.1 us)
Async XLA Ops:
  0.0 2.1 %collective-permute-start = (s32[1]{0:T(128)}, s32[1]{0:T(128)}, u32[]{:S(2)}, u32[]{:S(2)}) collective-permute-start(s32[1]{0:T(128)} %param.13), channel_id=1, source_target_pairs={{0,2},{1,3},{2,0},{3,1},{4,6},{5,7},{6,4},{7,5},{8,10},{9,11},{10,... | collective-permute-start | bytes 20 | tf_op jit(solution)/shard_map/ppermute | solution.py:406
  0.5 1.7 %collective-permute-start.1 = (s32[96,2]{0,1:T(2,128)}, s32[96,2]{0,1:T(2,128)S(1)}, u32[]{:S(2)}, u32[]{:S(2)}) collective-permute-start(s32[96,2]{0,1:T(2,128)} %param.12), channel_id=1, source_target_pairs={{0,2},{1,3},{2,0},{3,1},{4,6},{5,7},{6,4},{7,5},{8,10},{9,11},{10,... | collective-permute-start | bytes 2312 | tf_op jit(solution)/shard_map/ppermute | solution.py:406
  2.2 6.0 %collective-permute-start.2 = (bf16[96,128,128]{2,1,0:T(8,128)(2,1)}, bf16[96,128,128]{2,1,0:T(8,128)(2,1)S(1)}, u32[]{:S(2)}, u32[]{:S(2)}) collective-permute-start(bf16[96,128,128]{2,1,0:T(8,128)(2,1)} %refs_1_.5), channel_id=1, source_target_pairs={{0,2},{1,3},{2,0},{3,1},{4,6},{5,7},{6,4},{7,5},{8,10},{9,11},{10,... | collective-permute-start | bytes 9437192 | tf_op jit(solution)/shard_map/ppermute | solution.py:410
  2.7 1.4 %collective-permute-start.3 = (bf16[512,256]{1,0:T(8,128)(2,1)S(1)}, bf16[512,256]{1,0:T(8,128)(2,1)}, u32[]{:S(2)}, u32[]{:S(2)}) collective-permute-start(bf16[512,256]{1,0:T(8,128)(2,1)S(1)} %prepare.1), channel_id=1, source_target_pairs={{2,1},{1,2},{6,5},{5,6},{10,9},{9,10},{14,13},{13,14},{18,17},{17,... | collective-permute-start | bytes 786440 | tf_op jit(solution)/shard_map/ppermute | solution.py:411
  4.1 9.4 %collective-permute-start.5 = (bf16[512,256]{1,0:T(8,128)(2,1)S(1)}, bf16[512,256]{1,0:T(8,128)(2,1)S(1)}, u32[]{:S(2)}, u32[]{:S(2)}) collective-permute-start(bf16[512,256]{1,0:T(8,128)(2,1)S(1)} %broadcast_select_fusion.refs_6_), channel_id=1, source_target_pairs={{0,4},{1,5},{2,6},{3,7},{8,0},{9,1},{10,2},{11,3},{16,8},{17,9},{1... | collective-permute-start | bytes 786440 | tf_op jit(solution)/shard_map/ppermute | solution.py:338
  6.7 6.8 %collective-permute-start.4 = (bf16[512,256]{1,0:T(8,128)(2,1)S(1)}, bf16[512,256]{1,0:T(8,128)(2,1)S(1)}, u32[]{:S(2)}, u32[]{:S(2)}) collective-permute-start(bf16[512,256]{1,0:T(8,128)(2,1)S(1)} %broadcast_select_fusion.refs_6_), channel_id=1, source_target_pairs={{0,8},{1,9},{2,10},{3,11},{8,16},{9,17},{10,18},{11,19},{16,24},{1... | collective-permute-start | bytes 786440 | tf_op jit(solution)/shard_map/ppermute | solution.py:338
  13.5 9.2 %collective-permute-start.6 = (bf16[512,256]{1,0:T(8,128)(2,1)S(1)}, bf16[512,256]{1,0:T(8,128)(2,1)S(1)}, u32[]{:S(2)}, u32[]{:S(2)}) collective-permute-start(bf16[512,256]{1,0:T(8,128)(2,1)S(1)} %collective-permute-done.4.refs_4_), channel_id=1, source_target_pairs={{0,8},{1,9},{2,10},{3,11},{8,16},{9,17},{10,18},{11,19},{16,24},{1... | collective-permute-start | bytes 786440 | tf_op jit(solution)/shard_map/ppermute | solution.py:338
  16.4 6.4 %collective-permute-start.7 = (bf16[512,256]{1,0:T(8,128)(2,1)S(1)}, bf16[512,256]{1,0:T(8,128)(2,1)S(1)}, u32[]{:S(2)}, u32[]{:S(2)}) collective-permute-start(bf16[512,256]{1,0:T(8,128)(2,1)S(1)} %collective-permute-done.5.refs_5_), channel_id=1, source_target_pairs={{0,4},{1,5},{2,6},{3,7},{8,0},{9,1},{10,2},{11,3},{16,8},{17,9},{1... | collective-permute-start | bytes 786440 | tf_op jit(solution)/shard_map/ppermute | solution.py:338
  22.8 7.3 %collective-permute-start.8 = (bf16[512,256]{1,0:T(8,128)(2,1)S(1)}, bf16[512,256]{1,0:T(8,128)(2,1)S(1)}, u32[]{:S(2)}, u32[]{:S(2)}) collective-permute-start(bf16[512,256]{1,0:T(8,128)(2,1)S(1)} %collective-permute-done.6.refs_4_), channel_id=1, source_target_pairs={{0,8},{1,9},{2,10},{3,11},{8,16},{9,17},{10,18},{11,19},{16,24},{1... | collective-permute-start | bytes 786440 | tf_op jit(solution)/shard_map/ppermute | solution.py:338
  24.4 6.4 %collective-permute-start.9 = (bf16[512,256]{1,0:T(8,128)(2,1)S(1)}, bf16[512,256]{1,0:T(8,128)(2,1)S(1)}, u32[]{:S(2)}, u32[]{:S(2)}) collective-permute-start(bf16[512,256]{1,0:T(8,128)(2,1)S(1)} %collective-permute-done.7.refs_5_), channel_id=1, source_target_pairs={{0,4},{1,5},{2,6},{3,7},{8,0},{9,1},{10,2},{11,3},{16,8},{17,9},{1... | collective-permute-start | bytes 786440 | tf_op jit(solution)/shard_map/ppermute | solution.py:338
  30.8 5.0 %collective-permute-start.10 = (bf16[256,256]{1,0:T(8,128)(2,1)S(1)}, bf16[256,256]{1,0:T(8,128)(2,1)S(1)}, u32[]{:S(2)}, u32[]{:S(2)}) collective-permute-start(bf16[256,256]{1,0:T(8,128)(2,1)S(1)} %slice.6), channel_id=1, source_target_pairs={{0,8},{1,9},{2,10},{3,11},{8,16},{9,17},{10,18},{11,19},{16,24},{1... | collective-permute-start | bytes 393224 | tf_op jit(solution)/shard_map/ppermute | solution.py:338
  32.4 5.0 %collective-permute-start.11 = (bf16[256,256]{1,0:T(8,128)(2,1)S(1)}, bf16[256,256]{1,0:T(8,128)(2,1)S(1)}, u32[]{:S(2)}, u32[]{:S(2)}) collective-permute-start(bf16[256,256]{1,0:T(8,128)(2,1)S(1)} %slice.7), channel_id=1, source_target_pairs={{0,4},{1,5},{2,6},{3,7},{8,0},{9,1},{10,2},{11,3},{16,8},{17,9},{1... | collective-permute-start | bytes 393224 | tf_op jit(solution)/shard_map/ppermute | solution.py:338
  37.7 3.6 %collective-permute-start.13 = (bf16[512,256]{1,0:T(8,128)(2,1)S(1)}, bf16[512,256]{1,0:T(8,128)(2,1)S(1)}, u32[]{:S(2)}, u32[]{:S(2)}) collective-permute-start(bf16[512,256]{1,0:T(8,128)(2,1)S(1)} %last_stage.6), channel_id=1, source_target_pairs={{0,2},{1,3},{2,0},{3,1},{4,6},{5,7},{6,4},{7,5},{8,10},{9,11},{10,... | collective-permute-start | bytes 786440 | tf_op jit(solution)/shard_map/ppermute | solution.py:356
  40.4 9.5 %collective-permute-start.12 = (bf16[512,256]{1,0:T(8,128)(2,1)S(1)}, bf16[512,256]{1,0:T(8,128)(2,1)S(1)}, u32[]{:S(2)}, u32[]{:S(2)}) collective-permute-start(bf16[512,256]{1,0:T(8,128)(2,1)S(1)} %last_stage.4), channel_id=1, source_target_pairs={{0,2},{1,3},{2,0},{3,1},{4,6},{5,7},{6,4},{7,5},{8,10},{9,11},{10,... | collective-permute-start | bytes 786440 | tf_op jit(solution)/shard_map/ppermute | solution.py:357
  41.6 15.0 %copy-start = (f32[256]{0:T(256)S(1)}, f32[256]{0:T(256)}, u32[]{:S(2)}) copy-start(f32[256]{0:T(256)} %param.10) | copy-start | bytes 3076
  41.6 15.0 %collective-permute-start.14 = (bf16[512,256]{1,0:T(8,128)(2,1)S(1)}, bf16[512,256]{1,0:T(8,128)(2,1)S(1)}, u32[]{:S(2)}, u32[]{:S(2)}) collective-permute-start(bf16[512,256]{1,0:T(8,128)(2,1)S(1)} %last_stage.7), channel_id=1, source_target_pairs={{0,1},{1,0},{2,3},{3,2},{4,5},{5,4},{6,7},{7,6},{8,9},{9,8},{10,11... | collective-permute-start | bytes 786440 | tf_op jit(solution)/shard_map/ppermute | solution.py:358

commit v3 on v2

v3 whole, which is shorter than its diff:
```python
import functools
import jax
import jax.numpy as jnp
from jax import lax
from jax.experimental import pallas as pl
from jax.experimental.pallas import tpu as pltpu
from jax.sharding import PartitionSpec as P

AXES = ("rows", "rep")
MIB = 1024 * 1024
VMEM = pl.BlockSpec(memory_space=pltpu.VMEM)
ANY = pl.BlockSpec(memory_space=pl.ANY)
HBM = pl.BlockSpec(memory_space=pltpu.HBM)


def in_hbm(*arrays):
    return [pltpu.with_memory_space_constraint(a, pltpu.HBM) for a in arrays]


def cost(flops, moved):
    return pl.CostEstimate(flops=flops, bytes_accessed=moved, transcendentals=0)


def prepare_kernel(rows_hbm, order_hbm, weight_hbm, *refs):
    *outs, rows, order, weight, sems = refs
    copies = [
        pltpu.make_async_copy(src, dst, sems.at[i])
        for i, (src, dst) in enumerate(
            ((order_hbm, order), (weight_hbm, weight), (rows_hbm, rows))
        )
    ]
    for copy in copies:
        copy.start()
    shard_rows = rows.shape[0]
    copies[0].wait()
    within = lax.rem(order[...], shard_rows)
    node = lax.broadcasted_iota(jnp.int32, (shard_rows, shard_rows), 0)
    chosen = (node == within).astype(jnp.float32).astype(jnp.bfloat16)
    copies[1].wait()
    copies[2].wait()
    projected = jnp.dot(rows[...], weight[...], preferred_element_type=jnp.float32)
    result = lax.dot_general(
        chosen,
        projected.astype(jnp.bfloat16),
        (((0,), (0,)), ((), ())),
        preferred_element_type=jnp.float32,
    ).astype(jnp.bfloat16)
    width = result.shape[1] // len(outs)
    for i, out in enumerate(outs):
        out[...] = result[:, i * width : (i + 1) * width]


def prepare(features, node_order, weight, parts):
    shard_rows, width = features.shape
    order = node_order.reshape(1, shard_rows)
    return pl.pallas_call(
        prepare_kernel,
        out_shape=[jax.ShapeDtypeStruct((shard_rows, width // parts), features.dtype)] * parts,
        in_specs=[HBM] * 3,
        out_specs=[VMEM] * parts,
        scratch_shapes=[
            pltpu.VMEM(features.shape, features.dtype),
            pltpu.VMEM(order.shape, jnp.int32),
            pltpu.VMEM(weight.shape, weight.dtype),
            pltpu.SemaphoreType.DMA((3,)),
        ],
        compiler_params=pltpu.CompilerParams(vmem_limit_bytes=4 * MIB),
        cost_estimate=cost(4 * shard_rows * shard_rows * width, 4 * features.size),
        name="prepare",
    )(*in_hbm(features, order, weight))


def ring_chip(place, chips):
    return 2 * place if place < chips // 2 else 2 * (chips - 1 - place) + 1


def ring_place(chip, chips):
    return jnp.where(chip % 2 == 0, chip // 2, chips - 1 - chip // 2)


PLACE = 4096


class Layout:
    def __init__(self, halves, sections, replicas, tile_rows, groups, tile, slots):
        self.halves, self.sections, self.replicas = halves, sections, replicas
        self.tile_rows, self.groups, self.tile, self.slots = tile_rows, groups, tile, slots
        self.width = tile_rows // 2 if halves else tile_rows
        spans = [1] + [2] * (sections // 2 - 1) + [1] if halves else [1] * sections
        self.widths = [self.width * span for span in spans]
        self.line = -(-(slots + 1) // 128) * 128
        self.lines = groups * len(self.widths)

    def block(self, stage):
        return (self.tile_rows * self.tile, self.widths[stage] * self.tile)


def plan(layout, counts, coords, table):
    sections, width, slots, line = layout.sections, layout.width, layout.slots, layout.line
    row = lax.axis_index("rows")
    core = lax.rem(row, layout.replicas)
    before, after = (lax.broadcasted_iota(jnp.int32, (slots, slots), axis) for axis in (1, 0))
    lane = lax.broadcasted_iota(jnp.int32, (1, slots), 1)
    at = lax.broadcasted_iota(jnp.int32, (1, line), 1)

    def upright(values):
        kept = jnp.where(before == after, values.astype(jnp.float32), 0.0)
        return jnp.sum(kept, axis=1, keepdims=True)

    for g in range(layout.groups):
        block_row = row if g == 0 else row + 1 - 2 * core
        tile_row, column = coords[g, 0:1], coords[g, 1:2]
        tile_row = tile_row - block_row * layout.tile_rows
        step = column // (layout.tile_rows * layout.replicas)
        across, right = width, 0
        wanted = lane < counts[g][0]
        if layout.halves:
            ahead = ring_place(step, sections) - ring_place(row // layout.replicas, sections)
            ahead = jnp.where(ahead < 0, ahead + sections, ahead)
            step = jnp.minimum(ahead, sections - ahead)
            middle = (step > 0) & (2 * step < sections)
            across = jnp.where(middle, 2 * width, width)
            right = jnp.where(middle & (ahead == step), width, 0)
            wanted = wanted & ((column // width) % 2 == 1 - core)
        step = jnp.where(wanted, step, -1)
        packed = upright((tile_row * across + right + column % width) * PLACE + lane)
        step_up = upright(step)
        same = (step_up == step.astype(jnp.float32)) & (before < after)
        rank = jnp.sum(same.astype(jnp.float32), axis=1, keepdims=True)
        for stage in range(len(layout.widths)):
            here = step_up == stage
            found = jnp.where(here & (rank.astype(jnp.int32) == at), packed, 0.0)
            found = jnp.max(found, axis=0, keepdims=True)
            count = jnp.sum(here.astype(jnp.float32), axis=0, keepdims=True)
            found = jnp.where(at == line - 1, count, found)
            n = stage * layout.groups + g
            table[n : n + 1] = found.astype(jnp.int32)


def clear(*blocks):
    strip = 128
    for block in blocks:

        @pl.loop(0, block.shape[0], step=strip)
        def _(top, block=block):
            rows = pl.ds(pl.multiple_of(top, strip), strip)
            block[rows] = jnp.zeros((strip, block.shape[1]), block.dtype)


def fill(layout, stage, g, table, tiles, block, sem):
    tile, width = layout.tile, layout.widths[stage]
    n = stage * layout.groups + g
    count = table[n, layout.line - 1]

    @pl.loop(0, count)
    def _(i):
        packed = table[n, i]
        place = lax.shift_right_logical(packed, PLACE.bit_length() - 1)
        row = lax.shift_right_logical(place, width.bit_length() - 1)
        column = place & (width - 1)
        target = block.at[
            pl.ds(pl.multiple_of(row * tile, tile), tile),
            pl.ds(pl.multiple_of(column * tile, tile), tile),
        ]
        pltpu.make_async_copy(tiles.at[packed & (PLACE - 1)], target, sem).start()

    return count


def finish_fill(layout, tiles, started, sem):
    size = 1
    while size <= layout.slots * layout.groups:

        @pl.when((started & size) != 0)
        def _(size=size):
            for first in range(0, size, layout.slots):
                some = tiles.at[pl.ds(0, min(layout.slots, size - first))]
                pltpu.make_async_copy(some, some, sem).wait()

        size *= 2


def whole(piece):
    return jnp.concatenate([part[...] for part in piece], axis=1)


def grouped(refs, parts):
    return [refs[i : i + parts] for i in range(0, len(refs), parts)]


def multiply(blocks, pieces, total, out):
    strip = min(256, blocks[0].shape[0])
    for g, block in enumerate(blocks):
        for top in range(0, block.shape[0], strip):
            to = slice(g * block.shape[0] + top, g * block.shape[0] + top + strip)
            result = None if total is None else total[to]
            column = 0
            for piece in pieces:
                depth = piece[0].shape[0]
                product = jnp.dot(
                    block[top : top + strip, column : column + depth],
                    whole(piece),
                    preferred_element_type=jnp.float32,
                )
                result = product if result is None else result + product
                column += depth
            out[to] = result


def begin_kernel(layout, *refs):
    groups = layout.groups
    counts, coords_hbm, tiles = refs[:groups], refs[groups : 2 * groups], refs[2 * groups]
    table, block, coords, entries, coords_sems, sem, table_sem = refs[2 * groups + 1 :]
    loads = [
        pltpu.make_async_copy(coords_hbm[g], coords.at[g], coords_sems.at[g])
        for g in range(groups)
    ]
    for load in loads:
        load.start()
    clear(block)
    for load in loads:
        load.wait()
    plan(layout, counts, coords, table)
    load = pltpu.make_async_copy(table, entries, table_sem)
    load.start()
    load.wait()
    started = fill(layout, 0, 0, entries, tiles, block, sem)
    finish_fill(layout, tiles, started, sem)


def first_kernel(layout, parts, *refs):
    groups = layout.groups
    table, tiles, own, refs = refs[0], refs[1 : 1 + groups], refs[1 + groups], refs[2 + groups :]
    piece, refs = refs[:parts], refs[parts:]
    outs, scratch = refs[: 1 + 2 * groups], refs[1 + 2 * groups :]
    total, seconds, lasts = outs[0], outs[1 : 1 + groups], outs[1 + groups :]
    *firsts, entries, sems, table_sem = scratch
    load = pltpu.make_async_copy(table, entries, table_sem)
    load.start()
    clear(*firsts)
    load.wait()
    last = len(layout.widths) - 1
    started = [jnp.int32(0)] * 3
    for g in range(1, groups):
        started[0] += fill(layout, 0, g, entries, tiles[g], firsts[g - 1], sems.at[0])
    clear(*seconds, *lasts)
    for g in range(groups):
        started[1] += fill(layout, 1, g, entries, tiles[g], seconds[g], sems.at[1])
        started[2] += fill(layout, last, g, entries, tiles[g], lasts[g], sems.at[2])
    finish_fill(layout, tiles[0], started[0], sems.at[0])
    multiply([own, *firsts], [piece], None, total)
    finish_fill(layout, tiles[0], started[1], sems.at[1])
    finish_fill(layout, tiles[0], started[2], sems.at[2])


def next_kernel(layout, stage, n_pieces, parts, building, *refs):
    groups = layout.groups
    if building:
        table, tiles, refs = refs[0], refs[1 : 1 + groups], refs[1 + groups :]
    blocks, refs = refs[:groups], refs[groups:]
    pieces, refs = grouped(refs[: n_pieces * parts], parts), refs[n_pieces * parts :]
    total, next_total, *rest = refs
    if building:
        *next_blocks, entries, sem, table_sem = rest
        load = pltpu.make_async_copy(table, entries, table_sem)
        load.start()
        clear(*next_blocks)
        load.wait()
        started = jnp.int32(0)
        for g in range(groups):
            started += fill(layout, stage + 1, g, entries, tiles[g], next_blocks[g], sem)
    multiply(blocks, pieces, total, next_total)
    if building:
        finish_fill(layout, tiles[0], started, sem)


def last_kernel(n_pieces, parts, whose, which, lanes, has_more, block, *refs):
    pieces, total, out = grouped(refs[: n_pieces * parts], parts), refs[n_pieces * parts], refs[-1]
    first_row = which() * out.shape[0]
    strip = min(256, out.shape[0])
    for top in range(0, out.shape[0], strip):
        at = pl.multiple_of(first_row + top, strip)
        result = total[pl.ds(whose * block.shape[0] + at, strip), lanes]
        if has_more:
            result += refs[-2][top : top + strip].astype(jnp.float32)
        column = 0
        for piece in pieces:
            depth = piece[0].shape[0]
            result += jnp.dot(
                block[pl.ds(at, strip), column : column + depth],
                whole(piece),
                preferred_element_type=jnp.float32,
            )
            column += depth
        out[top : top + strip] = result.astype(out.dtype)


def result_kernel(kept, bias, *refs):
    *got, out = refs
    width = got[0].shape[1]
    for i, part in enumerate(got):
        lanes = slice(i * width, (i + 1) * width)
        total = kept[:, lanes] + part[...].astype(jnp.float32) + bias[:, lanes]
        out[:, lanes] = jnp.maximum(total, 0.0).astype(out.dtype)


SMEM = pl.BlockSpec(memory_space=pltpu.SMEM)
PARAMS = pltpu.CompilerParams(vmem_limit_bytes=16 * MIB)


def in_vmem(*arrays):
    return [pltpu.with_memory_space_constraint(a, pltpu.VMEM) for a in arrays]


def stage_cost(layout, stage, width):
    rows, depth = layout.block(stage)
    rows *= layout.groups
    return cost(2 * rows * depth * width, 4 * rows * depth + 8 * rows * width)


def begin(layout, groups):
    counts, coords, tiles = zip(*groups)
    n, dtype = layout.groups, tiles[0].dtype
    coords = [c.T for c in coords]
    lines = (layout.lines, layout.line)
    return pl.pallas_call(
        functools.partial(begin_kernel, layout),
        out_shape=[pltpu.VMEM(lines, jnp.int32), pltpu.VMEM(layout.block(0), dtype)],
        in_specs=[SMEM] * n + [ANY] * (n + 1),
        out_specs=[VMEM] * 2,
        scratch_shapes=[
            pltpu.VMEM((n, *coords[0].shape), jnp.int32),
            pltpu.SMEM(lines, jnp.int32),
            pltpu.SemaphoreType.DMA((n,)),
            pltpu.SemaphoreType.DMA,
            pltpu.SemaphoreType.DMA,
        ],
        compiler_params=PARAMS,
        cost_estimate=cost(0, 4 * layout.block(0)[0] * layout.block(0)[1]),
        name="begin",
    )(*counts, *in_hbm(coords[0]), *coords[1:], *in_hbm(tiles[0]))


def first_stage(layout, table, groups, own, piece):
    tiles = [g[2] for g in groups]
    n, width, dtype = layout.groups, sum(x.shape[1] for x in piece), tiles[0].dtype
    last = len(layout.widths) - 1
    rows = layout.block(0)[0] * n
    outs = pl.pallas_call(
        functools.partial(first_kernel, layout, len(piece)),
        out_shape=[pltpu.VMEM((rows, width), jnp.float32)]
        + [pltpu.VMEM(layout.block(1), dtype)] * n
        + [pltpu.VMEM(layout.block(last), dtype)] * n,
        in_specs=[VMEM] + [ANY] * n + [VMEM] * (1 + len(piece)),
        out_specs=[VMEM] * (2 * n + 1),
        scratch_shapes=[pltpu.VMEM(layout.block(0), dtype)] * (n - 1)
        + [
            pltpu.SMEM(table.shape, jnp.int32),
            pltpu.SemaphoreType.DMA((3,)),
            pltpu.SemaphoreType.DMA,
        ],
        compiler_params=PARAMS,
        cost_estimate=stage_cost(layout, 0, width),
        name="first_stage",
    )(*in_vmem(table), *in_hbm(tiles[0]), *tiles[1:], *in_vmem(own, *piece))
    return outs[0], outs[1 : n + 1], outs[n + 1 :]


def next_stage(layout, stage, table, groups, blocks, pieces, total):
    tiles = [g[2] for g in groups]
    width, n = total.shape[1], layout.groups
    building = table is not None
    parts = len(pieces[0])
    held = in_vmem(*blocks, *[x for piece in pieces for x in piece], total)
    sources = [*in_vmem(table), *in_hbm(tiles[0]), *tiles[1:]] if building else []
    outs = pl.pallas_call(
        functools.partial(next_kernel, layout, stage, len(pieces), parts, building),
        out_shape=[pltpu.VMEM(total.shape, total.dtype)]
        + ([pltpu.VMEM(layout.block(stage + 1), blocks[0].dtype)] * n if building else []),
        in_specs=([VMEM] + [ANY] * n if building else []) + [VMEM] * len(held),
        out_specs=[VMEM] * (1 + n if building else 1),
        scratch_shapes=[
            pltpu.SMEM(table.shape, jnp.int32),
            pltpu.SemaphoreType.DMA,
            pltpu.SemaphoreType.DMA,
        ]
        if building
        else [],
        compiler_params=PARAMS,
        cost_estimate=stage_cost(layout, stage, width),
        name="next_stage",
    )(*sources, *held)
    return outs[0], outs[1:]


def last_stage(block, whose, pieces, total, which, rows, first_lane, more=None, dtype=jnp.bfloat16):
    parts, depth = len(pieces[0]), block.shape[1]
    width = sum(x.shape[1] for x in pieces[0])
    lanes = slice(first_lane, first_lane + width)
    held = [block, *[x for piece in pieces for x in piece], total]
    held = in_vmem(*held, *([] if more is None else [more]))
    return pl.pallas_call(
        functools.partial(
            last_kernel, len(pieces), parts, whose, which, lanes, more is not None
        ),
        out_shape=pltpu.VMEM((rows, width), dtype),
        in_specs=[VMEM] * len(held),
        out_specs=VMEM,
        compiler_params=PARAMS,
        cost_estimate=cost(2 * rows * depth * width, 2 * rows * depth + 8 * rows * width),
        name="last_stage",
    )(*held)


def result(kept, got, bias):
    return pl.pallas_call(
        result_kernel,
        out_shape=jax.ShapeDtypeStruct(kept.shape, jnp.bfloat16),
        in_specs=[VMEM] * (2 + len(got)),
        out_specs=VMEM,
        compiler_params=PARAMS,
        cost_estimate=cost(4 * kept.size, 8 * kept.size),
        name="result",
    )(kept, bias.reshape(1, -1), *got)


def device_id(row, rep, replicas):
    return row * replicas + rep


def core_pairs(row_count, replicas):
    return [
        (device_id(row, rep, replicas), device_id(row ^ 1, rep, replicas))
        for row in range(row_count)
        for rep in range(replicas)
    ]


def ring_stages(shard, groups):
    tile_count, tile_coords, tile_values = groups
    replicas, row_count = lax.axis_size("rep"), lax.axis_size("rows")
    rows, chips = shard[0].shape[0], row_count // replicas
    ring = [ring_chip(i, chips) for i in range(chips)]

    def step_on(left, right, hops=1):
        def around(step):
            return [
                (
                    device_id(ring[p] * replicas + c, r, replicas),
                    device_id(ring[(p + step) % chips] * replicas + c, r, replicas),
                )
                for p in range(chips)
                for c in range(replicas)
                for r in range(replicas)
            ]

        return [
            lax.ppermute(left, AXES, around(hops)),
            lax.ppermute(right, AXES, around(-hops)),
        ]

    pairs = core_pairs(row_count, replicas)
    count, coords = (lax.ppermute(x, AXES, pairs) for x in (tile_count, tile_coords))
    shard, tiles, count, coords = lax.optimization_barrier((shard, tile_values, count, coords))
    groups = [(tile_count, tile_coords, tile_values), (count, coords, lax.ppermute(tiles, AXES, pairs))]
    tile_rows = rows * replicas // tile_values.shape[1]
    slots, tile = tile_values.shape[:2]
    layout = Layout(True, chips, replicas, tile_rows, len(groups), tile, slots)
    give = [
        (
            device_id(row, r, replicas),
            device_id(row ^ 1, r, replicas)
            if row % replicas == r
            else device_id(row, 1 - r, replicas),
        )
        for row in range(row_count)
        for r in range(replicas)
    ]
    own = [lax.ppermute(part, AXES, give) for part in shard]
    own, (table, first) = lax.optimization_barrier((own, begin(layout, groups)))
    far = chips // 2
    held = [None, [step_on(part, part) for part in own]]
    total, blocks, lasts = first_stage(layout, table, groups, first, own)

    def pieces(step):
        return [list(piece) for piece in zip(*held[step])]

    for step in range(2, far + 1):
        sent = [[lax.optimization_barrier((x, total))[0] for x in pair] for pair in held[-1]]
        if step == far:
            sent = [(left[: rows // 2], right[rows // 2 :]) for left, right in sent]
        held.append([step_on(*pair) for pair in sent])
        using = table if step < far else None
        total, blocks = next_stage(
            layout, step - 1, using, groups, blocks, pieces(step - 1), total
        )

    def finish(whose, near, ends, first_lane, more=None, dtype=jnp.bfloat16):
        def which():
            rep = lax.axis_index("rep")
            return rep if near else 1 - rep

        return last_stage(lasts[whose], whose, ends, total, which, rows, first_lane, more, dtype)

    other = [(0, 1), (1, 0)]
    lane, got = 0, []
    for pair in held[far]:
        ends = [[x] for x in pair]
        theirs = lax.ppermute(finish(1, False, ends, lane), AXES, pairs)
        got.append(lax.ppermute(finish(0, False, ends, lane, theirs), "rep", other))
        lane += pair[0].shape[1]
    ends = pieces(far)
    mine = lax.ppermute(finish(1, True, ends, 0), AXES, pairs)
    return finish(0, True, ends, 0, mine, jnp.float32), got


def gathered_stages(shard, groups):
    shard = shard[0]
    replicas, rep = lax.axis_size("rep"), lax.axis_index("rep")
    row_count, row = lax.axis_size("rows"), lax.axis_index("rows")
    shard_rows, sections = shard.shape[0], row_count // replicas
    trade = [
        (device_id(s * replicas + c, r, replicas), device_id(s * replicas + r, c, replicas))
        for s in range(sections)
        for r in range(replicas)
        for c in range(replicas)
        if r != c
    ]
    got = lax.ppermute(shard, AXES, trade)
    own = jnp.where(row % replicas == rep, shard, got)
    panels = lax.all_gather(own, "rows", axis=0, tiled=True)
    slots, tile = groups[2].shape[:2]
    layout = Layout(False, sections, replicas, shard_rows * replicas // tile, 1, tile, slots)
    groups = [groups]
    depth, last = layout.block(0)[1], layout.sections - 1
    pieces = [[panels[i * depth : (i + 1) * depth]] for i in range(last + 1)]
    table, first = begin(layout, groups)
    total, blocks, lasts = first_stage(layout, table, groups, first, pieces[0])
    for i in range(1, last):
        using = table if i < last - 1 else None
        total, blocks = next_stage(layout, i, using, groups, blocks, [pieces[i]], total)
    total = last_stage(
        lasts[0], 0, [pieces[last]], total, lambda: 0, depth, 0, None, jnp.float32
    )
    total = total.astype(jnp.bfloat16)

    def part(of):
        return lax.dynamic_slice_in_dim(total, of * shard_rows, shard_rows, 0)

    kept, got = part(rep).astype(jnp.float32), jnp.zeros((), jnp.float32)
    for step in range(1, replicas):
        got += lax.ppermute(
            part((rep + step) % replicas),
            "rep",
            [(r, (r + step) % replicas) for r in range(replicas)],
        ).astype(jnp.float32)
    return kept + got, [jnp.zeros(kept.shape, jnp.bfloat16)]


def shards(features, node_order, layer_weight, layer_bias, tile_values, tile_coords, tile_count):
    ring = lax.axis_size("rep") == 2
    projected = prepare(features, node_order, layer_weight, 2 if ring else 1)
    stages = ring_stages if ring else gathered_stages
    kept, got = stages(projected, (tile_count, tile_coords, tile_values))
    return result(kept, got, layer_bias)


def solution(mesh):
    placed = (
        P(("rows", "rep"), None),
        P(("rows", "rep")),
        P(),
        P(),
        P(("rows", "rep"), None, None),
        P(("rows", "rep"), None),
        P(("rows", "rep")),
    )
    return jax.shard_map(
        shards, mesh=mesh, in_specs=placed, out_specs=P(("rows", "rep"), None), check_vma=False
    )
```

time: 57.5 us -> 49 us (0.85)
  waiting for transfers between devices: 14.8 us -> 8.33 us
  Pallas kernels: 17.9 us -> 15.3 us
  starting transfers between devices: 23 us -> 24.2 us
  other arithmetic: 0.81 us -> 0 us
    ppermute x15 -> x26, waiting for transfers between devices: 14.8 us -> 8.33 us  [the longest x2 5.32 us: ring_stages(): got.append(lax.ppermute(finish(0, False, ends, lane, theirs), 'rep', other))]
    pallas_call x9 -> x13, Pallas kernels: 17.9 us -> 15.3 us  [the longest x3 5.77 us: next_stage(): pl.pallas_call(functools.partial(next_kernel, layout, stage, len(pieces),...]
    ppermute x15 -> x26, starting transfers between devices: 23 us -> 24.2 us  [the longest x8 12.4 us: step_on(): lax.ppermute(left, AXES, around(hops))]
    convert_element_type x1 -> x0, other arithmetic: 0.78 us -> none  [shards(): return jax.nn.relu(kept + got + layer_bias).astype(jnp.bfloat16)]
  transfers between devices with their start and end apart: 15 -> 26, of which waited for: 9 -> 7; matrix products, arithmetic and copies ran while one was open for 0% -> 0% of each run, Pallas kernels for 31% -> 30%
where the time goes in v3:
time: 49 us; the launch traced here: 48.7 us
  starting transfers between devices  24.2 us (49%)
  Pallas kernels  15.3 us (31%)
  waiting for transfers between devices  8.33 us (17%)
  between operations  0.85 us (2%)
    ppermute x8, starting transfers between devices, step_on(): lax.ppermute(left, AXES, around(hops))  12.4 us
    pallas_call x3, Pallas kernels, next_stage(): pl.pallas_call(functools.partial(next_kernel, layout, stage, len(pieces),...  5.77 us
    ppermute x2, waiting for transfers between devices, ring_stages(): got.append(lax.ppermute(finish(0, False, ends, lane, theirs), 'rep', other))  5.32 us
    ppermute x8, starting transfers between devices, step_on(): lax.ppermute(right, AXES, around(-hops))  4.88 us
    pallas_call x1, Pallas kernels, begin(): pl.pallas_call(functools.partial(begin_kernel, layout), out_shape=[pltpu....  3.18 us
    ppermute x2, starting transfers between devices, ring_stages(): own = [lax.ppermute(part, AXES, give) for part in shard]  2.72 us
    ppermute x8, waiting for transfers between devices, step_on(): lax.ppermute(right, AXES, around(-hops))  2.64 us
    ppermute x2, starting transfers between devices, ring_stages(): got.append(lax.ppermute(finish(0, False, ends, lane, theirs), 'rep', other))  2.5 us
  transfers between devices with their start and end apart: 26, of which 7 were waited for; matrix products, arithmetic and copies ran while one was open for 0% of the time, Pallas kernels for 30%

profile of v3, /device:TPU:0, one launch (start us, length us, event | category | flops | bytes accessed | tf_op | source)
XLA Modules:
  0.0 48.7 jit_solution(5959096053634622870)
XLA Ops:
  0.0 0.5 collective-permute-start
  0.5 1.6 %prepare.1 = (bf16[512,128]{1,0:T(8,128)(2,1)S(1)}, bf16[512,128]{1,0:T(8,128)(2,1)S(1)}) custom-call(bf16[512,256]{1,0:T(8,128)(2,1)} %rows_hbm.1, s32[1,512]{1,0:T(1,128)} %bitcast.7, bf16[256,256]{1,0:T(8,128)(2,1)} %weight_hbm.1), custom_call_target="tpu_custom_call" | custom-call | flops 268435456 | bytes 524288 | tf_op jit(solution)/shard_map/prepare/pallas_call | solution.py:56
  2.2 0.5 %collective-permute-start.4 = (bf16[96,128,128]{2,1,0:T(8,128)(2,1)}, bf16[96,128,128]{2,1,0:T(8,128)(2,1)S(1)}, u32[]{:S(2)}, u32[]{:S(2)}) collective-permute-start(bf16[96,128,128]{2,1,0:T(8,128)(2,1)} %refs_1_.5), channel_id=1, source_target_pairs={{0,2},{1,3},{2,0},{3,1},{4,6},{5,7},{6,4},{7,5},{8,10},{9,11},{10,... | collective-permute-start | bytes 9437192 | tf_op jit(solution)/shard_map/ppermute | solution.py:465
  2.7 2.7 %collective-permute-start.3 = (bf16[512,128]{1,0:T(8,128)(2,1)S(1)}, bf16[512,128]{1,0:T(8,128)(2,1)S(1)}, u32[]{:S(2)}, u32[]{:S(2)}) collective-permute-start(bf16[512,128]{1,0:T(8,128)(2,1)S(1)} %get-tuple-element.44), channel_id=1, source_target_pairs={{0,2},{1,0},{2,3},{3,1},{4,6},{5,4},{6,7},{7,5},{8,10},{9,8},{10,1... | collective-permute-start | bytes 393224 | tf_op jit(solution)/shard_map/ppermute | solution.py:479
  6.0 3.2 %begin.1 = (s32[10,128]{1,0:T(8,128)S(1)}, bf16[1024,512]{1,0:T(8,128)(2,1)S(1)}) custom-call(s32[1]{0:T(128)S(6)} %copy.8.refs_0_, s32[1]{0:T(128)} %collective-permute-done.refs_1_, s32[2,96]{1,0:T(2,128)} %bitcast.6, s32[2,96]{1,0:T(2,128)S(1)} %bitcast.4, bf16[96,128,128]{2,1,0:T(8,128)(2,1)} %refs_1_.5), custom_call_target="tpu_custom_call" | custom-call | bytes 2097152 | tf_op jit(solution)/shard_map/begin/pallas_call | solution.py:326
  9.5 2.1 %collective-permute-start.5 = (bf16[512,128]{1,0:T(8,128)(2,1)S(1)}, bf16[512,128]{1,0:T(8,128)(2,1)S(1)}, u32[]{:S(2)}, u32[]{:S(2)}) collective-permute-start(bf16[512,128]{1,0:T(8,128)(2,1)S(1)} %collective-permute-done.2.refs_4_), channel_id=1, source_target_pairs={{0,8},{1,9},{2,10},{3,11},{8,16},{9,17},{10,18},{11,19},{16,24},{1... | collective-permute-start | bytes 393224 | tf_op jit(solution)/shard_map/ppermute | solution.py:458
  11.7 1.6 %collective-permute-start.7 = (bf16[512,128]{1,0:T(8,128)(2,1)S(1)}, bf16[512,128]{1,0:T(8,128)(2,1)S(1)}, u32[]{:S(2)}, u32[]{:S(2)}) collective-permute-start(bf16[512,128]{1,0:T(8,128)(2,1)S(1)} %collective-permute-done.3.refs_5_), channel_id=1, source_target_pairs={{0,8},{1,9},{2,10},{3,11},{8,16},{9,17},{10,18},{11,19},{16,24},{1... | collective-permute-start | bytes 393224 | tf_op jit(solution)/shard_map/ppermute | solution.py:458
  13.2 0.4 collective-permute-start.8
  13.7 2.2 %first_stage.1 = (f32[2048,256]{1,0:T(8,128)S(1)}, bf16[1024,1024]{1,0:T(8,128)(2,1)S(1)}, bf16[1024,1024]{1,0:T(8,128)(2,1)S(1)}, bf16[1024,512]{1,0:T(8,128)(2,1)S(1)}, bf16[1024,512]{1,0:T(8,128)(2,1)S(1)}) custom-call(s32[10,128]{1,0:T(8,128)S(1)} %get-tuple-element.49.refs_0_, bf16[96,128,128]{2,1,0:T(8,128)(2,1)} %refs_1_.5, ...), custom_call_target="tpu_custom_call" | custom-call | flops 536870912 | bytes 8388608 | tf_op jit(solution)/shard_map/first_stage/pallas_call | solution.py:349
  16.0 2.1 %collective-permute-start.6 = (bf16[512,128]{1,0:T(8,128)(2,1)S(1)}, bf16[512,128]{1,0:T(8,128)(2,1)S(1)}, u32[]{:S(2)}, u32[]{:S(2)}) collective-permute-start(bf16[512,128]{1,0:T(8,128)(2,1)S(1)} %collective-permute-done.5.refs_5_), channel_id=1, source_target_pairs={{0,8},{1,9},{2,10},{3,11},{8,16},{9,17},{10,18},{11,19},{16,24},{1... | collective-permute-start | bytes 393224 | tf_op jit(solution)/shard_map/ppermute | solution.py:458
  18.1 1.7 %collective-permute-start.11 = (bf16[512,128]{1,0:T(8,128)(2,1)S(1)}, bf16[512,128]{1,0:T(8,128)(2,1)S(1)}, u32[]{:S(2)}, u32[]{:S(2)}) collective-permute-start(bf16[512,128]{1,0:T(8,128)(2,1)S(1)} %collective-permute-done.7.refs_6_), channel_id=1, source_target_pairs={{0,8},{1,9},{2,10},{3,11},{8,16},{9,17},{10,18},{11,19},{16,24},{1... | collective-permute-start | bytes 393224 | tf_op jit(solution)/shard_map/ppermute | solution.py:458
  20.1 0.4 collective-permute-done.9.refs_8_
  20.5 1.1 %collective-permute-start.13 = (bf16[512,128]{1,0:T(8,128)(2,1)S(1)}, bf16[512,128]{1,0:T(8,128)(2,1)S(1)}, u32[]{:S(2)}, u32[]{:S(2)}) collective-permute-start(bf16[512,128]{1,0:T(8,128)(2,1)S(1)} %collective-permute-done.9.refs_8_), channel_id=1, source_target_pairs={{0,4},{1,5},{2,6},{3,7},{8,0},{9,1},{10,2},{11,3},{16,8},{17,9},{1... | collective-permute-start | bytes 393224 | tf_op jit(solution)/shard_map/ppermute | solution.py:459
  21.6 2.2 %next_stage.3 = (f32[2048,256]{1,0:T(8,128)S(1)}, bf16[1024,1024]{1,0:T(8,128)(2,1)S(1)}, bf16[1024,1024]{1,0:T(8,128)(2,1)S(1)}) custom-call(s32[10,128]{1,0:T(8,128)S(1)} %get-tuple-element.49.refs_0_, bf16[96,128,128]{2,1,0:T(8,128)(2,1)} %refs_1_.5, bf16[96,128,128]{2,1,0:T(8,128)(2,1)S(1)} %collective-permute-done.4.refs_2_, ...), custom_call_target="tpu_custom_call" | custom-call | flops 1073741824 | bytes 12582912 | tf_op jit(solution)/shard_map/next_stage/pallas_call | solution.py:376
  23.9 0.9 %collective-permute-start.10 = (bf16[512,128]{1,0:T(8,128)(2,1)S(1)}, bf16[512,128]{1,0:T(8,128)(2,1)S(1)}, u32[]{:S(2)}, u32[]{:S(2)}) collective-permute-start(bf16[512,128]{1,0:T(8,128)(2,1)S(1)} %collective-permute-done.6.refs_5_), channel_id=1, source_target_pairs={{0,8},{1,9},{2,10},{3,11},{8,16},{9,17},{10,18},{11,19},{16,24},{1... | collective-permute-start | bytes 393224 | tf_op jit(solution)/shard_map/ppermute | solution.py:458
  24.8 1.5 %collective-permute-start.15 = (bf16[512,128]{1,0:T(8,128)(2,1)S(1)}, bf16[512,128]{1,0:T(8,128)(2,1)S(1)}, u32[]{:S(2)}, u32[]{:S(2)}) collective-permute-start(bf16[512,128]{1,0:T(8,128)(2,1)S(1)} %collective-permute-done.11.refs_6_), channel_id=1, source_target_pairs={{0,8},{1,9},{2,10},{3,11},{8,16},{9,17},{10,18},{11,19},{16,24},{1... | collective-permute-start | bytes 393224 | tf_op jit(solution)/shard_map/ppermute | solution.py:458
  26.3 0.5 %collective-permute-start.17 = (bf16[512,128]{1,0:T(8,128)(2,1)S(1)}, bf16[512,128]{1,0:T(8,128)(2,1)S(1)}, u32[]{:S(2)}, u32[]{:S(2)}) collective-permute-start(bf16[512,128]{1,0:T(8,128)(2,1)S(1)} %collective-permute-done.12.refs_7_), channel_id=1, source_target_pairs={{0,4},{1,5},{2,6},{3,7},{8,0},{9,1},{10,2},{11,3},{16,8},{17,9},{1... | collective-permute-start | bytes 393224 | tf_op jit(solution)/shard_map/ppermute | solution.py:459
  26.8 1.2 %collective-permute-start.19 = (bf16[512,128]{1,0:T(8,128)(2,1)S(1)}, bf16[512,128]{1,0:T(8,128)(2,1)S(1)}, u32[]{:S(2)}, u32[]{:S(2)}) collective-permute-start(bf16[512,128]{1,0:T(8,128)(2,1)S(1)} %collective-permute-done.13.refs_8_), channel_id=1, source_target_pairs={{0,4},{1,5},{2,6},{3,7},{8,0},{9,1},{10,2},{11,3},{16,8},{17,9},{1... | collective-permute-start | bytes 393224 | tf_op jit(solution)/shard_map/ppermute | solution.py:459
  28.0 2.3 %next_stage.4 = (f32[2048,256]{1,0:T(8,128)S(1)}, bf16[1024,1024]{1,0:T(8,128)(2,1)S(1)}, bf16[1024,1024]{1,0:T(8,128)(2,1)S(1)}) custom-call(s32[10,128]{1,0:T(8,128)S(1)} %get-tuple-element.49.refs_0_, bf16[96,128,128]{2,1,0:T(8,128)(2,1)} %refs_1_.5, bf16[96,128,128]{2,1,0:T(8,128)(2,1)S(1)} %collective-permute-done.4.refs_2_, ...), custom_call_target="tpu_custom_call" | custom-call | flops 1073741824 | bytes 12582912 | tf_op jit(solution)/shard_map/next_stage/pallas_call | solution.py:376
  30.3 0.8 %collective-permute-start.14 = (bf16[256,128]{1,0:T(8,128)(2,1)S(1)}, bf16[256,128]{1,0:T(8,128)(2,1)S(1)}, u32[]{:S(2)}, u32[]{:S(2)}) collective-permute-start(bf16[256,128]{1,0:T(8,128)(2,1)S(1)} %slice.12), channel_id=1, source_target_pairs={{0,8},{1,9},{2,10},{3,11},{8,16},{9,17},{10,18},{11,19},{16,24},{1... | collective-permute-start | bytes 196616 | tf_op jit(solution)/shard_map/ppermute | solution.py:458
  31.1 1.7 %collective-permute-start.16 = (bf16[256,128]{1,0:T(8,128)(2,1)S(1)}, bf16[256,128]{1,0:T(8,128)(2,1)S(1)}, u32[]{:S(2)}, u32[]{:S(2)}) collective-permute-start(bf16[256,128]{1,0:T(8,128)(2,1)S(1)} %slice.13), channel_id=1, source_target_pairs={{0,8},{1,9},{2,10},{3,11},{8,16},{9,17},{10,18},{11,19},{16,24},{1... | collective-permute-start | bytes 196616 | tf_op jit(solution)/shard_map/ppermute | solution.py:458
  33.2 0.5 %collective-permute-done.19.refs_5_ = bf16[512,128]{1,0:T(8,128)(2,1)S(1)} collective-permute-done((bf16[512,128]{1,0:T(8,128)(2,1)S(1)}, bf16[512,128]{1,0:T(8,128)(2,1)S(1)}, u32[]{:S(2)}, u32[]{:S(2)}) %collective-permute-start.19) | collective-permute-done | bytes 131104 | tf_op jit(solution)/shard_map/ppermute | solution.py:459
  33.7 0.9 %collective-permute-start.20 = (bf16[256,128]{1,0:T(8,128)(2,1)S(1)}, bf16[256,128]{1,0:T(8,128)(2,1)S(1)}, u32[]{:S(2)}, u32[]{:S(2)}) collective-permute-start(bf16[256,128]{1,0:T(8,128)(2,1)S(1)} %slice.15), channel_id=1, source_target_pairs={{0,4},{1,5},{2,6},{3,7},{8,0},{9,1},{10,2},{11,3},{16,8},{17,9},{1... | collective-permute-start | bytes 196616 | tf_op jit(solution)/shard_map/ppermute | solution.py:459
  34.6 1.3 %next_stage.5.refs_4_.refs_2_ = f32[2048,256]{1,0:T(8,128)S(1)} custom-call(bf16[1024,1024]{1,0:T(8,128)(2,1)S(1)} %get-tuple-element.74.refs_0_, bf16[1024,1024]{1,0:T(8,128)(2,1)S(1)} %get-tuple-element.75.refs_1_, bf16[512,128]{1,0:T(8,128)(2,1)S(1)} %collective-permute-done.10.refs_2_, bf16[512,128]{1,0:T(8,128)(2,1)S(1)} %collective-permute-done.15.refs_3_, ...), custom_call_target="tpu_custom_call" | custom-call | flops 1073741824 | bytes 12582912 | tf_op jit(solution)/shard_map/next_stage/pallas_call | solution.py:376
  35.9 1.2 %collective-permute-done.18.refs_2_.refs_1_ = bf16[256,128]{1,0:T(8,128)(2,1)S(1)} collective-permute-done((bf16[256,128]{1,0:T(8,128)(2,1)S(1)}, bf16[256,128]{1,0:T(8,128)(2,1)S(1)}, u32[]{:S(2)}, u32[]{:S(2)}) %collective-permute-start.18) | collective-permute-done | bytes 65568 | tf_op jit(solution)/shard_map/ppermute | solution.py:459
  37.5 0.5 %collective-permute-done.20.refs_3_.refs_1_ = bf16[256,128]{1,0:T(8,128)(2,1)S(1)} collective-permute-done((bf16[256,128]{1,0:T(8,128)(2,1)S(1)}, bf16[256,128]{1,0:T(8,128)(2,1)S(1)}, u32[]{:S(2)}, u32[]{:S(2)}) %collective-permute-start.20) | collective-permute-done | bytes 65568 | tf_op jit(solution)/shard_map/ppermute | solution.py:459
  38.6 0.6 %collective-permute-start.24 = (bf16[512,128]{1,0:T(8,128)(2,1)S(1)}, bf16[512,128]{1,0:T(8,128)(2,1)S(1)}, u32[]{:S(2)}, u32[]{:S(2)}) collective-permute-start(bf16[512,128]{1,0:T(8,128)(2,1)S(1)} %last_stage.10), channel_id=1, source_target_pairs={{0,2},{1,3},{2,0},{3,1},{4,6},{5,7},{6,4},{7,5},{8,10},{9,11},{10,... | collective-permute-start | bytes 393224 | tf_op jit(solution)/shard_map/ppermute | solution.py:509
  39.5 1.8 %collective-permute-start.23 = (bf16[512,128]{1,0:T(8,128)(2,1)S(1)}, bf16[512,128]{1,0:T(8,128)(2,1)S(1)}, u32[]{:S(2)}, u32[]{:S(2)}) collective-permute-start(bf16[512,128]{1,0:T(8,128)(2,1)S(1)} %last_stage.9), channel_id=1, source_target_pairs={{0,1},{1,0},{2,3},{3,2},{4,5},{5,4},{6,7},{7,6},{8,9},{9,8},{10,11... | collective-permute-start | bytes 393224 | tf_op jit(solution)/shard_map/ppermute | solution.py:510
  41.6 0.7 %collective-permute-start.25 = (bf16[512,128]{1,0:T(8,128)(2,1)S(1)}, bf16[512,128]{1,0:T(8,128)(2,1)S(1)}, u32[]{:S(2)}, u32[]{:S(2)}) collective-permute-start(bf16[512,128]{1,0:T(8,128)(2,1)S(1)} %last_stage.11), channel_id=1, source_target_pairs={{0,1},{1,0},{2,3},{3,2},{4,5},{5,4},{6,7},{7,6},{8,9},{9,8},{10,11... | collective-permute-start | bytes 393224 | tf_op jit(solution)/shard_map/ppermute | solution.py:510
  42.6 3.3 %collective-permute-done.23.refs_0_ = bf16[512,128]{1,0:T(8,128)(2,1)S(1)} collective-permute-done((bf16[512,128]{1,0:T(8,128)(2,1)S(1)}, bf16[512,128]{1,0:T(8,128)(2,1)S(1)}, u32[]{:S(2)}, u32[]{:S(2)}) %collective-permute-start.23) | collective-permute-done | bytes 131104 | tf_op jit(solution)/shard_map/ppermute | solution.py:510
  45.9 2.0 %collective-permute-done.25.refs_1_ = bf16[512,128]{1,0:T(8,128)(2,1)S(1)} collective-permute-done((bf16[512,128]{1,0:T(8,128)(2,1)S(1)}, bf16[512,128]{1,0:T(8,128)(2,1)S(1)}, u32[]{:S(2)}, u32[]{:S(2)}) %collective-permute-start.25) | collective-permute-done | bytes 131104 | tf_op jit(solution)/shard_map/ppermute | solution.py:510
  47.9 0.8 %result.1 = bf16[512,256]{1,0:T(8,128)(2,1)} custom-call(f32[512,256]{1,0:T(8,128)S(1)} %last_stage.7.kept, f32[1,256]{1,0:T(1,128)S(1)} %bitcast.5, bf16[512,128]{1,0:T(8,128)(2,1)S(1)} %collective-permute-done.23.refs_0_, bf16[512,128]{1,0:T(8,128)(2,1)S(1)} %collective-permute-done.25.refs_1_), custom_call_target="tpu_custom_call" | custom-call | flops 524288 | bytes 1048576 | tf_op jit(solution)/shard_map/result/pallas_call | solution.py:416
  (39 shorter events, 3.2 us)
Async XLA Ops:
  0.0 2.1 %collective-permute-start = (s32[1]{0:T(128)}, s32[1]{0:T(128)}, u32[]{:S(2)}, u32[]{:S(2)}) collective-permute-start(s32[1]{0:T(128)} %param.13), channel_id=1, source_target_pairs={{0,2},{1,3},{2,0},{3,1},{4,6},{5,7},{6,4},{7,5},{8,10},{9,11},{10,... | collective-permute-start | bytes 20 | tf_op jit(solution)/shard_map/ppermute | solution.py:463
  0.5 1.7 %collective-permute-start.1 = (s32[96,2]{0,1:T(2,128)}, s32[96,2]{0,1:T(2,128)S(1)}, u32[]{:S(2)}, u32[]{:S(2)}) collective-permute-start(s32[96,2]{0,1:T(2,128)} %param.12), channel_id=1, source_target_pairs={{0,2},{1,3},{2,0},{3,1},{4,6},{5,7},{6,4},{7,5},{8,10},{9,11},{10,... | collective-permute-start | bytes 2312 | tf_op jit(solution)/shard_map/ppermute | solution.py:463
  2.2 11.6 %collective-permute-start.4 = (bf16[96,128,128]{2,1,0:T(8,128)(2,1)}, bf16[96,128,128]{2,1,0:T(8,128)(2,1)S(1)}, u32[]{:S(2)}, u32[]{:S(2)}) collective-permute-start(bf16[96,128,128]{2,1,0:T(8,128)(2,1)} %refs_1_.5), channel_id=1, source_target_pairs={{0,2},{1,3},{2,0},{3,1},{4,6},{5,7},{6,4},{7,5},{8,10},{9,11},{10,... | collective-permute-start | bytes 9437192 | tf_op jit(solution)/shard_map/ppermute | solution.py:465
  2.7 6.6 %collective-permute-start.2 = (bf16[512,128]{1,0:T(8,128)(2,1)S(1)}, bf16[512,128]{1,0:T(8,128)(2,1)S(1)}, u32[]{:S(2)}, u32[]{:S(2)}) collective-permute-start(bf16[512,128]{1,0:T(8,128)(2,1)S(1)} %get-tuple-element.43), channel_id=1, source_target_pairs={{0,2},{1,0},{2,3},{3,1},{4,6},{5,4},{6,7},{7,5},{8,10},{9,8},{10,1... | collective-permute-start | bytes 393224 | tf_op jit(solution)/shard_map/ppermute | solution.py:479
  2.7 6.8 %collective-permute-start.3 = (bf16[512,128]{1,0:T(8,128)(2,1)S(1)}, bf16[512,128]{1,0:T(8,128)(2,1)S(1)}, u32[]{:S(2)}, u32[]{:S(2)}) collective-permute-start(bf16[512,128]{1,0:T(8,128)(2,1)S(1)} %get-tuple-element.44), channel_id=1, source_target_pairs={{0,2},{1,0},{2,3},{3,1},{4,6},{5,4},{6,7},{7,5},{8,10},{9,8},{10,1... | collective-permute-start | bytes 393224 | tf_op jit(solution)/shard_map/ppermute | solution.py:479
  9.5 6.4 %collective-permute-start.5 = (bf16[512,128]{1,0:T(8,128)(2,1)S(1)}, bf16[512,128]{1,0:T(8,128)(2,1)S(1)}, u32[]{:S(2)}, u32[]{:S(2)}) collective-permute-start(bf16[512,128]{1,0:T(8,128)(2,1)S(1)} %collective-permute-done.2.refs_4_), channel_id=1, source_target_pairs={{0,8},{1,9},{2,10},{3,11},{8,16},{9,17},{10,18},{11,19},{16,24},{1... | collective-permute-start | bytes 393224 | tf_op jit(solution)/shard_map/ppermute | solution.py:458
  11.7 6.4 %collective-permute-start.7 = (bf16[512,128]{1,0:T(8,128)(2,1)S(1)}, bf16[512,128]{1,0:T(8,128)(2,1)S(1)}, u32[]{:S(2)}, u32[]{:S(2)}) collective-permute-start(bf16[512,128]{1,0:T(8,128)(2,1)S(1)} %collective-permute-done.3.refs_5_), channel_id=1, source_target_pairs={{0,8},{1,9},{2,10},{3,11},{8,16},{9,17},{10,18},{11,19},{16,24},{1... | collective-permute-start | bytes 393224 | tf_op jit(solution)/shard_map/ppermute | solution.py:458
  13.2 6.5 %collective-permute-start.8 = (bf16[512,128]{1,0:T(8,128)(2,1)S(1)}, bf16[512,128]{1,0:T(8,128)(2,1)S(1)}, u32[]{:S(2)}, u32[]{:S(2)}) collective-permute-start(bf16[512,128]{1,0:T(8,128)(2,1)S(1)} %collective-permute-done.2.refs_4_), channel_id=1, source_target_pairs={{0,4},{1,5},{2,6},{3,7},{8,0},{9,1},{10,2},{11,3},{16,8},{17,9},{1... | collective-permute-start | bytes 393224 | tf_op jit(solution)/shard_map/ppermute | solution.py:459
  13.7 6.8 %collective-permute-start.9 = (bf16[512,128]{1,0:T(8,128)(2,1)S(1)}, bf16[512,128]{1,0:T(8,128)(2,1)S(1)}, u32[]{:S(2)}, u32[]{:S(2)}) collective-permute-start(bf16[512,128]{1,0:T(8,128)(2,1)S(1)} %collective-permute-done.3.refs_5_), channel_id=1, source_target_pairs={{0,4},{1,5},{2,6},{3,7},{8,0},{9,1},{10,2},{11,3},{16,8},{17,9},{1... | collective-permute-start | bytes 393224 | tf_op jit(solution)/shard_map/ppermute | solution.py:459
  16.0 7.9 %collective-permute-start.6 = (bf16[512,128]{1,0:T(8,128)(2,1)S(1)}, bf16[512,128]{1,0:T(8,128)(2,1)S(1)}, u32[]{:S(2)}, u32[]{:S(2)}) collective-permute-start(bf16[512,128]{1,0:T(8,128)(2,1)S(1)} %collective-permute-done.5.refs_5_), channel_id=1, source_target_pairs={{0,8},{1,9},{2,10},{3,11},{8,16},{9,17},{10,18},{11,19},{16,24},{1... | collective-permute-start | bytes 393224 | tf_op jit(solution)/shard_map/ppermute | solution.py:458
  18.1 6.7 %collective-permute-start.11 = (bf16[512,128]{1,0:T(8,128)(2,1)S(1)}, bf16[512,128]{1,0:T(8,128)(2,1)S(1)}, u32[]{:S(2)}, u32[]{:S(2)}) collective-permute-start(bf16[512,128]{1,0:T(8,128)(2,1)S(1)} %collective-permute-done.7.refs_6_), channel_id=1, source_target_pairs={{0,8},{1,9},{2,10},{3,11},{8,16},{9,17},{10,18},{11,19},{16,24},{1... | collective-permute-start | bytes 393224 | tf_op jit(solution)/shard_map/ppermute | solution.py:458
  19.8 6.5 %collective-permute-start.12 = (bf16[512,128]{1,0:T(8,128)(2,1)S(1)}, bf16[512,128]{1,0:T(8,128)(2,1)S(1)}, u32[]{:S(2)}, u32[]{:S(2)}) collective-permute-start(bf16[512,128]{1,0:T(8,128)(2,1)S(1)} %collective-permute-done.8.refs_7_), channel_id=1, source_target_pairs={{0,4},{1,5},{2,6},{3,7},{8,0},{9,1},{10,2},{11,3},{16,8},{17,9},{1... | collective-permute-start | bytes 393224 | tf_op jit(solution)/shard_map/ppermute | solution.py:459
  20.5 6.3 %collective-permute-start.13 = (bf16[512,128]{1,0:T(8,128)(2,1)S(1)}, bf16[512,128]{1,0:T(8,128)(2,1)S(1)}, u32[]{:S(2)}, u32[]{:S(2)}) collective-permute-start(bf16[512,128]{1,0:T(8,128)(2,1)S(1)} %collective-permute-done.9.refs_8_), channel_id=1, source_target_pairs={{0,4},{1,5},{2,6},{3,7},{8,0},{9,1},{10,2},{11,3},{16,8},{17,9},{1... | collective-permute-start | bytes 393224 | tf_op jit(solution)/shard_map/ppermute | solution.py:459
  23.9 6.4 %collective-permute-start.10 = (bf16[512,128]{1,0:T(8,128)(2,1)S(1)}, bf16[512,128]{1,0:T(8,128)(2,1)S(1)}, u32[]{:S(2)}, u32[]{:S(2)}) collective-permute-start(bf16[512,128]{1,0:T(8,128)(2,1)S(1)} %collective-permute-done.6.refs_5_), channel_id=1, source_target_pairs={{0,8},{1,9},{2,10},{3,11},{8,16},{9,17},{10,18},{11,19},{16,24},{1... | collective-permute-start | bytes 393224 | tf_op jit(solution)/shard_map/ppermute | solution.py:458
  24.8 6.3 %collective-permute-start.15 = (bf16[512,128]{1,0:T(8,128)(2,1)S(1)}, bf16[512,128]{1,0:T(8,128)(2,1)S(1)}, u32[]{:S(2)}, u32[]{:S(2)}) collective-permute-start(bf16[512,128]{1,0:T(8,128)(2,1)S(1)} %collective-permute-done.11.refs_6_), channel_id=1, source_target_pairs={{0,8},{1,9},{2,10},{3,11},{8,16},{9,17},{10,18},{11,19},{16,24},{1... | collective-permute-start | bytes 393224 | tf_op jit(solution)/shard_map/ppermute | solution.py:458
  26.3 6.5 %collective-permute-start.17 = (bf16[512,128]{1,0:T(8,128)(2,1)S(1)}, bf16[512,128]{1,0:T(8,128)(2,1)S(1)}, u32[]{:S(2)}, u32[]{:S(2)}) collective-permute-start(bf16[512,128]{1,0:T(8,128)(2,1)S(1)} %collective-permute-done.12.refs_7_), channel_id=1, source_target_pairs={{0,4},{1,5},{2,6},{3,7},{8,0},{9,1},{10,2},{11,3},{16,8},{17,9},{1... | collective-permute-start | bytes 393224 | tf_op jit(solution)/shard_map/ppermute | solution.py:459
  26.8 6.9 %collective-permute-start.19 = (bf16[512,128]{1,0:T(8,128)(2,1)S(1)}, bf16[512,128]{1,0:T(8,128)(2,1)S(1)}, u32[]{:S(2)}, u32[]{:S(2)}) collective-permute-start(bf16[512,128]{1,0:T(8,128)(2,1)S(1)} %collective-permute-done.13.refs_8_), channel_id=1, source_target_pairs={{0,4},{1,5},{2,6},{3,7},{8,0},{9,1},{10,2},{11,3},{16,8},{17,9},{1... | collective-permute-start | bytes 393224 | tf_op jit(solution)/shard_map/ppermute | solution.py:459
  30.3 5.6 %collective-permute-start.14 = (bf16[256,128]{1,0:T(8,128)(2,1)S(1)}, bf16[256,128]{1,0:T(8,128)(2,1)S(1)}, u32[]{:S(2)}, u32[]{:S(2)}) collective-permute-start(bf16[256,128]{1,0:T(8,128)(2,1)S(1)} %slice.12), channel_id=1, source_target_pairs={{0,8},{1,9},{2,10},{3,11},{8,16},{9,17},{10,18},{11,19},{16,24},{1... | collective-permute-start | bytes 196616 | tf_op jit(solution)/shard_map/ppermute | solution.py:458
  31.1 6.4 %collective-permute-start.16 = (bf16[256,128]{1,0:T(8,128)(2,1)S(1)}, bf16[256,128]{1,0:T(8,128)(2,1)S(1)}, u32[]{:S(2)}, u32[]{:S(2)}) collective-permute-start(bf16[256,128]{1,0:T(8,128)(2,1)S(1)} %slice.13), channel_id=1, source_target_pairs={{0,8},{1,9},{2,10},{3,11},{8,16},{9,17},{10,18},{11,19},{16,24},{1... | collective-permute-start | bytes 196616 | tf_op jit(solution)/shard_map/ppermute | solution.py:458
  32.8 4.3 %collective-permute-start.18 = (bf16[256,128]{1,0:T(8,128)(2,1)S(1)}, bf16[256,128]{1,0:T(8,128)(2,1)S(1)}, u32[]{:S(2)}, u32[]{:S(2)}) collective-permute-start(bf16[256,128]{1,0:T(8,128)(2,1)S(1)} %slice.14), channel_id=1, source_target_pairs={{0,4},{1,5},{2,6},{3,7},{8,0},{9,1},{10,2},{11,3},{16,8},{17,9},{1... | collective-permute-start | bytes 196616 | tf_op jit(solution)/shard_map/ppermute | solution.py:459
  33.7 4.3 %collective-permute-start.20 = (bf16[256,128]{1,0:T(8,128)(2,1)S(1)}, bf16[256,128]{1,0:T(8,128)(2,1)S(1)}, u32[]{:S(2)}, u32[]{:S(2)}) collective-permute-start(bf16[256,128]{1,0:T(8,128)(2,1)S(1)} %slice.15), channel_id=1, source_target_pairs={{0,4},{1,5},{2,6},{3,7},{8,0},{9,1},{10,2},{11,3},{16,8},{17,9},{1... | collective-permute-start | bytes 196616 | tf_op jit(solution)/shard_map/ppermute | solution.py:459
  37.4 1.8 %collective-permute-start.22 = (bf16[512,128]{1,0:T(8,128)(2,1)S(1)}, bf16[512,128]{1,0:T(8,128)(2,1)S(1)}, u32[]{:S(2)}, u32[]{:S(2)}) collective-permute-start(bf16[512,128]{1,0:T(8,128)(2,1)S(1)} %last_stage.8), channel_id=1, source_target_pairs={{0,2},{1,3},{2,0},{3,1},{4,6},{5,7},{6,4},{7,5},{8,10},{9,11},{10,... | collective-permute-start | bytes 393224 | tf_op jit(solution)/shard_map/ppermute | solution.py:509
  38.3 4.0 %collective-permute-start.21 = (bf16[512,256]{1,0:T(8,128)(2,1)S(1)}, bf16[512,256]{1,0:T(8,128)(2,1)S(1)}, u32[]{:S(2)}, u32[]{:S(2)}) collective-permute-start(bf16[512,256]{1,0:T(8,128)(2,1)S(1)} %last_stage.6), channel_id=1, source_target_pairs={{0,2},{1,3},{2,0},{3,1},{4,6},{5,7},{6,4},{7,5},{8,10},{9,11},{10,... | collective-permute-start | bytes 786440 | tf_op jit(solution)/shard_map/ppermute | solution.py:513
  38.6 2.6 %collective-permute-start.24 = (bf16[512,128]{1,0:T(8,128)(2,1)S(1)}, bf16[512,128]{1,0:T(8,128)(2,1)S(1)}, u32[]{:S(2)}, u32[]{:S(2)}) collective-permute-start(bf16[512,128]{1,0:T(8,128)(2,1)S(1)} %last_stage.10), channel_id=1, source_target_pairs={{0,2},{1,3},{2,0},{3,1},{4,6},{5,7},{6,4},{7,5},{8,10},{9,11},{10,... | collective-permute-start | bytes 393224 | tf_op jit(solution)/shard_map/ppermute | solution.py:509
  39.5 6.4 %collective-permute-start.23 = (bf16[512,128]{1,0:T(8,128)(2,1)S(1)}, bf16[512,128]{1,0:T(8,128)(2,1)S(1)}, u32[]{:S(2)}, u32[]{:S(2)}) collective-permute-start(bf16[512,128]{1,0:T(8,128)(2,1)S(1)} %last_stage.9), channel_id=1, source_target_pairs={{0,1},{1,0},{2,3},{3,2},{4,5},{5,4},{6,7},{7,6},{8,9},{9,8},{10,11... | collective-permute-start | bytes 393224 | tf_op jit(solution)/shard_map/ppermute | solution.py:510
  41.6 6.4 %copy-start = (f32[256]{0:T(256)S(1)}, f32[256]{0:T(256)}, u32[]{:S(2)}) copy-start(f32[256]{0:T(256)} %param.10) | copy-start | bytes 3076
  41.6 6.3 %collective-permute-start.25 = (bf16[512,128]{1,0:T(8,128)(2,1)S(1)}, bf16[512,128]{1,0:T(8,128)(2,1)S(1)}, u32[]{:S(2)}, u32[]{:S(2)}) collective-permute-start(bf16[512,128]{1,0:T(8,128)(2,1)S(1)} %last_stage.11), channel_id=1, source_target_pairs={{0,1},{1,0},{2,3},{3,2},{4,5},{5,4},{6,7},{7,6},{8,9},{9,8},{10,11... | collective-permute-start | bytes 393224 | tf_op jit(solution)/shard_map/ppermute | solution.py:510

commit v4 on v3

--- a/solution.py
+++ b/solution.py
@@ -109,7 +109,7 @@
 
     for g in range(layout.groups):
         block_row = row if g == 0 else row + 1 - 2 * core
-        tile_row, column = coords[g, 0:1], coords[g, 1:2]
+        tile_row, column = coords[g][0:1], coords[g][1:2]
         tile_row = tile_row - block_row * layout.tile_rows
         step = column // (layout.tile_rows * layout.replicas)
         across, right = width, 0
@@ -209,46 +209,30 @@
 
 def begin_kernel(layout, *refs):
     groups = layout.groups
-    counts, coords_hbm, tiles = refs[:groups], refs[groups : 2 * groups], refs[2 * groups]
-    table, block, coords, entries, coords_sems, sem, table_sem = refs[2 * groups + 1 :]
-    loads = [
-        pltpu.make_async_copy(coords_hbm[g], coords.at[g], coords_sems.at[g])
-        for g in range(groups)
-    ]
-    for load in loads:
-        load.start()
-    clear(block)
-    for load in loads:
-        load.wait()
+    counts, coords, table = refs[:groups], refs[groups : 2 * groups], refs[2 * groups]
     plan(layout, counts, coords, table)
-    load = pltpu.make_async_copy(table, entries, table_sem)
-    load.start()
-    load.wait()
-    started = fill(layout, 0, 0, entries, tiles, block, sem)
-    finish_fill(layout, tiles, started, sem)
 
 
 def first_kernel(layout, parts, *refs):
     groups = layout.groups
-    table, tiles, own, refs = refs[0], refs[1 : 1 + groups], refs[1 + groups], refs[2 + groups :]
+    table, tiles, refs = refs[0], refs[1 : 1 + groups], refs[1 + groups :]
     piece, refs = refs[:parts], refs[parts:]
-    outs, scratch = refs[: 1 + 2 * groups], refs[1 + 2 * groups :]
-    total, seconds, lasts = outs[0], outs[1 : 1 + groups], outs[1 + groups :]
-    *firsts, entries, sems, table_sem = scratch
+    total, seconds, lasts = refs[0], refs[1 : 1 + groups], refs[1 + groups : 1 + 2 * groups]
+    *firsts, entries, sems, table_sem = refs[1 + 2 * groups :]
     load = pltpu.make_async_copy(table, entries, table_sem)
     load.start()
     clear(*firsts)
     load.wait()
     last = len(layout.widths) - 1
     started = [jnp.int32(0)] * 3
-    for g in range(1, groups):
-        started[0] += fill(layout, 0, g, entries, tiles[g], firsts[g - 1], sems.at[0])
+    for g in range(groups):
+        started[0] += fill(layout, 0, g, entries, tiles[g], firsts[g], sems.at[0])
     clear(*seconds, *lasts)
     for g in range(groups):
         started[1] += fill(layout, 1, g, entries, tiles[g], seconds[g], sems.at[1])
         started[2] += fill(layout, last, g, entries, tiles[g], lasts[g], sems.at[2])
     finish_fill(layout, tiles[0], started[0], sems.at[0])
-    multiply([own, *firsts], [piece], None, total)
+    multiply(firsts, [piece], None, total)
     finish_fill(layout, tiles[0], started[1], sems.at[1])
     finish_fill(layout, tiles[0], started[2], sems.at[2])
 
@@ -274,33 +258,46 @@
         finish_fill(layout, tiles[0], started, sem)
 
 
-def last_kernel(n_pieces, parts, whose, which, lanes, has_more, block, *refs):
-    pieces, total, out = grouped(refs[: n_pieces * parts], parts), refs[n_pieces * parts], refs[-1]
-    first_row = which() * out.shape[0]
-    strip = min(256, out.shape[0])
-    for top in range(0, out.shape[0], strip):
-        at = pl.multiple_of(first_row + top, strip)
-        result = total[pl.ds(whose * block.shape[0] + at, strip), lanes]
-        if has_more:
-            result += refs[-2][top : top + strip].astype(jnp.float32)
-        column = 0
-        for piece in pieces:
-            depth = piece[0].shape[0]
-            result += jnp.dot(
-                block[pl.ds(at, strip), column : column + depth],
-                whole(piece),
-                preferred_element_type=jnp.float32,
-            )
-            column += depth
-        out[top : top + strip] = result.astype(out.dtype)
-
-
-def result_kernel(kept, bias, *refs):
-    *got, out = refs
+def last_kernel(counts, parts, jobs, groups, *refs):
+    blocks, refs = grouped(refs[: groups * len(counts)], groups), refs[groups * len(counts) :]
+    n = sum(counts) * parts
+    pieces, total, refs = grouped(refs[:n], parts), refs[n], refs[n + 1 :]
+    added, outs = refs[: -len(jobs)], refs[-len(jobs) :]
+    added = iter(added)
+    for (whose, which, chosen, more), out in zip(jobs, outs):
+        extra = next(added) if more else None
+        rows = out.shape[0]
+        first_row = which() * rows
+        width = pieces[0][0].shape[1]
+        lanes = slice(chosen[0] * width, (chosen[-1] + 1) * width)
+        strip = min(256, rows)
+        for top in range(0, rows, strip):
+            at = pl.multiple_of(first_row + top, strip)
+            result = total[pl.ds(whose * blocks[0][0].shape[0] + at, strip), lanes]
+            if more:
+                result += extra[top : top + strip].astype(jnp.float32)
+            first = 0
+            for count, stage in zip(counts, blocks):
+                column = 0
+                for piece in pieces[first : first + count]:
+                    depth = piece[0].shape[0]
+                    result += jnp.dot(
+                        stage[whose][pl.ds(at, strip), column : column + depth],
+                        whole([piece[part] for part in chosen]),
+                        preferred_element_type=jnp.float32,
+                    )
+                    column += depth
+                first += count
+            out[top : top + strip] = result.astype(out.dtype)
+
+
+def result_kernel(bias, *refs):
+    n = len(refs) // 2
+    kept, got, out = refs[:n], refs[n:-1], refs[-1]
     width = got[0].shape[1]
-    for i, part in enumerate(got):
+    for i in range(n):
         lanes = slice(i * width, (i + 1) * width)
-        total = kept[:, lanes] + part[...].astype(jnp.float32) + bias[:, lanes]
+        total = kept[i][...] + got[i][...].astype(jnp.float32) + bias[:, lanes]
         out[:, lanes] = jnp.maximum(total, 0.0).astype(out.dtype)
 
 
@@ -319,29 +316,20 @@
 
 
 def begin(layout, groups):
-    counts, coords, tiles = zip(*groups)
-    n, dtype = layout.groups, tiles[0].dtype
-    coords = [c.T for c in coords]
-    lines = (layout.lines, layout.line)
+    counts, coords, _ = zip(*groups)
+    n = layout.groups
     return pl.pallas_call(
         functools.partial(begin_kernel, layout),
-        out_shape=[pltpu.VMEM(lines, jnp.int32), pltpu.VMEM(layout.block(0), dtype)],
-        in_specs=[SMEM] * n + [ANY] * (n + 1),
-        out_specs=[VMEM] * 2,
-        scratch_shapes=[
-            pltpu.VMEM((n, *coords[0].shape), jnp.int32),
-            pltpu.SMEM(lines, jnp.int32),
-            pltpu.SemaphoreType.DMA((n,)),
-            pltpu.SemaphoreType.DMA,
-            pltpu.SemaphoreType.DMA,
-        ],
+        out_shape=pltpu.VMEM((layout.lines, layout.line), jnp.int32),
+        in_specs=[SMEM] * n + [VMEM] * n,
+        out_specs=VMEM,
         compiler_params=PARAMS,
-        cost_estimate=cost(0, 4 * layout.block(0)[0] * layout.block(0)[1]),
+        cost_estimate=cost(1000000, 4 * layout.lines * layout.line),
         name="begin",
-    )(*counts, *in_hbm(coords[0]), *coords[1:], *in_hbm(tiles[0]))
-
-
-def first_stage(layout, table, groups, own, piece):
+    )(*counts, *[c.T for c in coords])
+
+
+def first_stage(layout, table, groups, piece):
     tiles = [g[2] for g in groups]
     n, width, dtype = layout.groups, sum(x.shape[1] for x in piece), tiles[0].dtype
     last = len(layout.widths) - 1
@@ -351,9 +339,9 @@
         out_shape=[pltpu.VMEM((rows, width), jnp.float32)]
         + [pltpu.VMEM(layout.block(1), dtype)] * n
         + [pltpu.VMEM(layout.block(last), dtype)] * n,
-        in_specs=[VMEM] + [ANY] * n + [VMEM] * (1 + len(piece)),
+        in_specs=[VMEM] + [ANY] * n + [VMEM] * len(piece),
         out_specs=[VMEM] * (2 * n + 1),
-        scratch_shapes=[pltpu.VMEM(layout.block(0), dtype)] * (n - 1)
+        scratch_shapes=[pltpu.VMEM(layout.block(0), dtype)] * n
         + [
             pltpu.SMEM(table.shape, jnp.int32),
             pltpu.SemaphoreType.DMA((3,)),
@@ -362,7 +350,7 @@
         compiler_params=PARAMS,
         cost_estimate=stage_cost(layout, 0, width),
         name="first_stage",
-    )(*in_vmem(table), *in_hbm(tiles[0]), *tiles[1:], *in_vmem(own, *piece))
+    )(*in_vmem(table), *in_hbm(tiles[0]), *tiles[1:], *in_vmem(*piece))
     return outs[0], outs[1 : n + 1], outs[n + 1 :]
 
 
@@ -393,35 +381,39 @@
     return outs[0], outs[1:]
 
 
-def last_stage(block, whose, pieces, total, which, rows, first_lane, more=None, dtype=jnp.bfloat16):
-    parts, depth = len(pieces[0]), block.shape[1]
-    width = sum(x.shape[1] for x in pieces[0])
-    lanes = slice(first_lane, first_lane + width)
-    held = [block, *[x for piece in pieces for x in piece], total]
-    held = in_vmem(*held, *([] if more is None else [more]))
+def last_stages(stages, total, rows, jobs):
+    counts = [len(pieces) for _, pieces in stages]
+    groups, parts = len(stages[0][0]), len(stages[0][1][0])
+    width = stages[0][1][0][0].shape[1]
+    depth = sum(blocks[0].shape[1] for blocks, _ in stages)
+    held = [block for blocks, _ in stages for block in blocks]
+    held += [x for _, pieces in stages for piece in pieces for x in piece] + [total]
+    held = in_vmem(*held, *[job[3] for job in jobs if job[3] is not None])
+    inner = [(whose, which, chosen, more is not None) for whose, which, chosen, more, _ in jobs]
+    lanes = sum(width * len(job[2]) for job in jobs)
     return pl.pallas_call(
-        functools.partial(
-            last_kernel, len(pieces), parts, whose, which, lanes, more is not None
-        ),
-        out_shape=pltpu.VMEM((rows, width), dtype),
+        functools.partial(last_kernel, counts, parts, inner, groups),
+        out_shape=[pltpu.VMEM((rows, width * len(job[2])), job[4]) for job in jobs],
         in_specs=[VMEM] * len(held),
+        out_specs=[VMEM] * len(jobs),
+        compiler_params=PARAMS,
+        cost_estimate=cost(2 * rows * depth * lanes, 2 * rows * depth + 8 * rows * lanes),
+        name="last_stages",
+    )(*held)
+
+
+def result(kept, got, bias):
+    rows, width = kept[0].shape
+    width *= len(kept)
+    return pl.pallas_call(
+        result_kernel,
+        out_shape=jax.ShapeDtypeStruct((rows, width), jnp.bfloat16),
+        in_specs=[VMEM] * (1 + len(kept) + len(got)),
         out_specs=VMEM,
         compiler_params=PARAMS,
-        cost_estimate=cost(2 * rows * depth * width, 2 * rows * depth + 8 * rows * width),
-        name="last_stage",
-    )(*held)
-
-
-def result(kept, got, bias):
-    return pl.pallas_call(
-        result_kernel,
-        out_shape=jax.ShapeDtypeStruct(kept.shape, jnp.bfloat16),
-        in_specs=[VMEM] * (2 + len(got)),
-        out_specs=VMEM,
-        compiler_params=PARAMS,
-        cost_estimate=cost(4 * kept.size, 8 * kept.size),
+        cost_estimate=cost(4 * rows * width, 8 * rows * width),
         name="result",
-    )(kept, bias.reshape(1, -1), *got)
+    )(bias.reshape(1, -1), *kept, *got)
 
 
 def device_id(row, rep, replicas):
@@ -442,22 +434,17 @@
     rows, chips = shard[0].shape[0], row_count // replicas
     ring = [ring_chip(i, chips) for i in range(chips)]
 
-    def step_on(left, right, hops=1):
-        def around(step):
-            return [
-                (
-                    device_id(ring[p] * replicas + c, r, replicas),
-                    device_id(ring[(p + step) % chips] * replicas + c, r, replicas),
-                )
-                for p in range(chips)
-                for c in range(replicas)
-                for r in range(replicas)
-            ]
-
-        return [
-            lax.ppermute(left, AXES, around(hops)),
-            lax.ppermute(right, AXES, around(-hops)),
+    def step_on(array, way):
+        hops = [
+            (
+                device_id(ring[p] * replicas + c, r, replicas),
+                device_id(ring[(p + way) % chips] * replicas + c, r, replicas),
+            )
+            for p in range(chips)
+            for c in range(replicas)
+            for r in range(replicas)
         ]
+        return lax.ppermute(array, AXES, hops)
 
     pairs = core_pairs(row_count, replicas)
     count, coords = (lax.ppermute(x, AXES, pairs) for x in (tile_count, tile_coords))
@@ -477,41 +464,59 @@
         for r in range(replicas)
     ]
     own = [lax.ppermute(part, AXES, give) for part in shard]
-    own, (table, first) = lax.optimization_barrier((own, begin(layout, groups)))
+    table = begin(layout, groups)
+    own = [lax.optimization_barrier((part, table))[0] for part in own]
     far = chips // 2
-    held = [None, [step_on(part, part) for part in own]]
-    total, blocks, lasts = first_stage(layout, table, groups, first, own)
+    ways = 1, -1
+    held = [None, [[step_on(part, way) for way in ways] for part in own]]
+    total, blocks, lasts = first_stage(layout, table, groups, own)
 
     def pieces(step):
         return [list(piece) for piece in zip(*held[step])]
 
     for step in range(2, far + 1):
-        sent = [[lax.optimization_barrier((x, total))[0] for x in pair] for pair in held[-1]]
-        if step == far:
-            sent = [(left[: rows // 2], right[rows // 2 :]) for left, right in sent]
-        held.append([step_on(*pair) for pair in sent])
-        using = table if step < far else None
-        total, blocks = next_stage(
-            layout, step - 1, using, groups, blocks, pieces(step - 1), total
-        )
-
-    def finish(whose, near, ends, first_lane, more=None, dtype=jnp.bfloat16):
-        def which():
-            rep = lax.axis_index("rep")
-            return rep if near else 1 - rep
-
-        return last_stage(lasts[whose], whose, ends, total, which, rows, first_lane, more, dtype)
-
-    other = [(0, 1), (1, 0)]
-    lane, got = 0, []
-    for pair in held[far]:
-        ends = [[x] for x in pair]
-        theirs = lax.ppermute(finish(1, False, ends, lane), AXES, pairs)
-        got.append(lax.ppermute(finish(0, False, ends, lane, theirs), "rep", other))
-        lane += pair[0].shape[1]
-    ends = pieces(far)
-    mine = lax.ppermute(finish(1, True, ends, 0), AXES, pairs)
-    return finish(0, True, ends, 0, mine, jnp.float32), got
+        sent, earlier = [], total
+        for pair in held[-1]:
+            if step == far:
+                earlier = earlier, pair
+            sent.append([lax.optimization_barrier((x, earlier))[0] for x in pair])
+            earlier = total, pair
+        if step < far:
+            held.append([[step_on(x, way) for x, way in zip(pair, ways)] for pair in sent])
+            total, blocks = next_stage(
+                layout, step - 1, table, groups, blocks, pieces(step - 1), total
+            )
+        else:
+            held.append([[step_on(sent[i][i], way)] for i, way in enumerate(ways)])
+            total, _ = next_stage(layout, step - 1, None, groups, blocks, pieces(step - 1), total)
+
+    def finish(parts, *jobs, after=None):
+        stages = [(lasts, [[x for part in parts for x in held[far][part]]])]
+        sums = total if after is None else lax.optimization_barrier((total, after))[0]
+        return last_stages(stages, sums, rows, jobs)
+
+    def near():
+        return lax.axis_index("rep")
+
+    def away():
+        return 1 - lax.axis_index("rep")
+
+    short, other = jnp.bfloat16, [(0, 1), (1, 0)]
+    parts = list(range(len(own)))
+    theirs, given = [], None
+    for part in parts:
+        (given,) = finish(parts[: part + 1], (1, away, [part], None, short), after=given)
+        theirs.append(lax.ppermute(given, AXES, pairs))
+    got, mine, summed = [], [], None
+    for part in parts:
+        jobs = [(0, away, [part], theirs[part], short)]
+        if part == parts[-1]:
+            jobs += [(1, near, [p], None, short) for p in parts]
+        summed, *rest = finish(parts[: part + 1], *jobs, after=summed)
+        got.append(lax.ppermute(summed, "rep", other))
+        mine += [lax.ppermute(x, AXES, pairs) for x in rest]
+    jobs = [(0, near, [part], mine[part], jnp.float32) for part in parts]
+    return finish(parts, *jobs, after=got[0]), got
 
 
 def gathered_stages(shard, groups):
@@ -534,14 +539,13 @@
     groups = [groups]
     depth, last = layout.block(0)[1], layout.sections - 1
     pieces = [[panels[i * depth : (i + 1) * depth]] for i in range(last + 1)]
-    table, first = begin(layout, groups)
-    total, blocks, lasts = first_stage(layout, table, groups, first, pieces[0])
+    table = begin(layout, groups)
+    total, blocks, lasts = first_stage(layout, table, groups, pieces[0])
     for i in range(1, last):
         using = table if i < last - 1 else None
         total, blocks = next_stage(layout, i, using, groups, blocks, [pieces[i]], total)
-    total = last_stage(
-        lasts[0], 0, [pieces[last]], total, lambda: 0, depth, 0, None, jnp.float32
-    )
+    ending = [(lasts, [pieces[last]])]
+    (total,) = last_stages(ending, total, depth, [(0, lambda: 0, [0], None, jnp.float32)])
     total = total.astype(jnp.bfloat16)
 
     def part(of):
@@ -554,7 +558,7 @@
             "rep",
             [(r, (r + step) % replicas) for r in range(replicas)],
         ).astype(jnp.float32)
-    return kept + got, [jnp.zeros(kept.shape, jnp.bfloat16)]
+    return [kept + got], [jnp.zeros(kept.shape, jnp.bfloat16)]
 
 
 def shards(features, node_order, layer_weight, layer_bias, tile_values, tile_coords, tile_count):

time: 49 us -> 47.1 us (0.961)
  Pallas kernels: 15.3 us -> 13 us
  starting transfers between devices: 24.2 us -> 22.5 us
  waiting for transfers between devices: 8.33 us -> 9.79 us
  local copies, waits for them, and re-layouts: 0.03 us -> 0.68 us
    pallas_call x8 -> x7, Pallas kernels: 5.7 us -> 3.45 us  [the longest x5 1.83 us: last_stages(): pl.pallas_call(functools.partial(last_kernel, counts, parts, inner, group...]
    ppermute x21 -> x20, starting transfers between devices: 20.5 us -> 18.7 us  [the longest x14 16.3 us: step_on(): return lax.ppermute(array, AXES, hops)]
    ppermute x21 -> x20, waiting for transfers between devices: 8.02 us -> 9.2 us  [the longest x2 5.1 us: ring_stages(): got.append(lax.ppermute(summed, 'rep', other))]
    unnamed x2 -> x4, local copies, waits for them, and re-layouts: 0.01 us -> 0.68 us
  transfers between devices with their start and end apart: 26 -> 25, of which waited for: 7 -> 8; matrix products, arithmetic and copies ran while one was open for 0% -> 0% of each run, Pallas kernels for 30% -> 26%
where the time goes in v4:
time: 47.1 us; the launch traced here: 46.8 us
  starting transfers between devices  22.5 us (48%)
  Pallas kernels  13 us (28%)
  waiting for transfers between devices  9.79 us (21%)
  between operations  0.82 us (2%)
  local copies, waits for them, and re-layouts  0.68 us (1%)
    ppermute x14, starting transfers between devices, step_on(): return lax.ppermute(array, AXES, hops)  16.3 us
    pallas_call x3, Pallas kernels, next_stage(): pl.pallas_call(functools.partial(next_kernel, layout, stage, len(pieces),...  5.46 us
    ppermute x2, waiting for transfers between devices, ring_stages(): got.append(lax.ppermute(summed, 'rep', other))  5.1 us
    ppermute x14, waiting for transfers between devices, step_on(): return lax.ppermute(array, AXES, hops)  3.76 us
    ppermute x2, starting transfers between devices, ring_stages(): own = [lax.ppermute(part, AXES, give) for part in shard]  2.72 us
    pallas_call x1, Pallas kernels, first_stage(): pl.pallas_call(functools.partial(first_kernel, layout, len(piece)), out_s...  2.51 us
    pallas_call x5, Pallas kernels, last_stages(): pl.pallas_call(functools.partial(last_kernel, counts, parts, inner, group...  1.83 us
    ppermute x2, starting transfers between devices, ring_stages(): got.append(lax.ppermute(summed, 'rep', other))  1.76 us
  transfers between devices with their start and end apart: 25, of which 8 were waited for; matrix products, arithmetic and copies ran while one was open for 0% of the time, Pallas kernels for 26%

profile of v4, /device:TPU:0, one launch (start us, length us, event | category | flops | bytes accessed | tf_op | source)
XLA Modules:
  0.0 46.8 jit_solution(4168754399452574556)
XLA Ops:
  0.0 0.5 collective-permute-start
  0.5 1.6 %prepare.1 = (bf16[512,128]{1,0:T(8,128)(2,1)S(1)}, bf16[512,128]{1,0:T(8,128)(2,1)S(1)}) custom-call(bf16[512,256]{1,0:T(8,128)(2,1)} %rows_hbm.1, s32[1,512]{1,0:T(1,128)} %bitcast.7, bf16[256,256]{1,0:T(8,128)(2,1)} %weight_hbm.1), custom_call_target="tpu_custom_call" | custom-call | flops 268435456 | bytes 524288 | tf_op jit(solution)/shard_map/prepare/pallas_call | solution.py:56
  2.2 0.5 %collective-permute-start.2 = (bf16[96,128,128]{2,1,0:T(8,128)(2,1)}, bf16[96,128,128]{2,1,0:T(8,128)(2,1)S(1)}, u32[]{:S(2)}, u32[]{:S(2)}) collective-permute-start(bf16[96,128,128]{2,1,0:T(8,128)(2,1)} %refs_1_.5), channel_id=1, source_target_pairs={{0,2},{1,3},{2,0},{3,1},{4,6},{5,7},{6,4},{7,5},{8,10},{9,11},{10,... | collective-permute-start | bytes 9437192 | tf_op jit(solution)/shard_map/ppermute | solution.py:452
  2.7 2.7 %collective-permute-start.4 = (bf16[512,128]{1,0:T(8,128)(2,1)S(1)}, bf16[512,128]{1,0:T(8,128)(2,1)S(1)}, u32[]{:S(2)}, u32[]{:S(2)}) collective-permute-start(bf16[512,128]{1,0:T(8,128)(2,1)S(1)} %get-tuple-element.50), channel_id=1, source_target_pairs={{0,2},{1,0},{2,3},{3,1},{4,6},{5,4},{6,7},{7,5},{8,10},{9,8},{10,1... | collective-permute-start | bytes 393224 | tf_op jit(solution)/shard_map/ppermute | solution.py:466
  6.1 0.7 %copy-done.1 = s32[96,2]{0,1:T(2,128)S(1)} copy-done((s32[96,2]{0,1:T(2,128)S(1)}, s32[96,2]{0,1:T(2,128)}, u32[]{:S(2)}) %copy-start.1) | copy-done | bytes 792
  6.7 0.8 %begin.1.refs_0_ = s32[10,128]{1,0:T(8,128)S(1)} custom-call(s32[1]{0:T(128)S(6)} %copy.8.refs_0_, s32[1]{0:T(128)} %collective-permute-done.refs_1_, s32[2,96]{1,0:T(2,128)S(1)} %bitcast.5, s32[2,96]{1,0:T(2,128)S(1)} %bitcast.6), custom_call_target="tpu_custom_call" | custom-call | flops 1000000 | bytes 5120 | tf_op jit(solution)/shard_map/begin/pallas_call | solution.py:321
  7.6 0.6 %collective-permute-done.3.refs_3_ = bf16[512,128]{1,0:T(8,128)(2,1)S(1)} collective-permute-done((bf16[512,128]{1,0:T(8,128)(2,1)S(1)}, bf16[512,128]{1,0:T(8,128)(2,1)S(1)}, u32[]{:S(2)}, u32[]{:S(2)}) %collective-permute-start.3) | collective-permute-done | bytes 131104 | tf_op jit(solution)/shard_map/ppermute | solution.py:466
  8.1 2.6 %collective-permute-start.5 = (bf16[512,128]{1,0:T(8,128)(2,1)S(1)}, bf16[512,128]{1,0:T(8,128)(2,1)S(1)}, u32[]{:S(2)}, u32[]{:S(2)}) collective-permute-start(bf16[512,128]{1,0:T(8,128)(2,1)S(1)} %collective-permute-done.3.refs_3_), channel_id=1, source_target_pairs={{0,8},{1,9},{2,10},{3,11},{8,16},{9,17},{10,18},{11,19},{16,24},{1... | collective-permute-start | bytes 393224 | tf_op jit(solution)/shard_map/ppermute | solution.py:447
  10.8 2.0 %collective-permute-start.9 = (bf16[512,128]{1,0:T(8,128)(2,1)S(1)}, bf16[512,128]{1,0:T(8,128)(2,1)S(1)}, u32[]{:S(2)}, u32[]{:S(2)}) collective-permute-start(bf16[512,128]{1,0:T(8,128)(2,1)S(1)} %collective-permute-done.4.refs_4_), channel_id=1, source_target_pairs={{0,4},{1,5},{2,6},{3,7},{8,0},{9,1},{10,2},{11,3},{16,8},{17,9},{1... | collective-permute-start | bytes 393224 | tf_op jit(solution)/shard_map/ppermute | solution.py:447
  12.8 2.5 %first_stage.1 = (f32[2048,256]{1,0:T(8,128)S(1)}, bf16[1024,1024]{1,0:T(8,128)(2,1)S(1)}, bf16[1024,1024]{1,0:T(8,128)(2,1)S(1)}, bf16[1024,512]{1,0:T(8,128)(2,1)S(1)}, bf16[1024,512]{1,0:T(8,128)(2,1)S(1)}) custom-call(s32[10,128]{1,0:T(8,128)S(1)} %begin.1.refs_0_, bf16[96,128,128]{2,1,0:T(8,128)(2,1)} %refs_1_.5, ...), custom_call_target="tpu_custom_call" | custom-call | flops 536870912 | bytes 8388608 | tf_op jit(solution)/shard_map/first_stage/pallas_call | solution.py:337
  15.3 1.9 %collective-permute-start.6 = (bf16[512,128]{1,0:T(8,128)(2,1)S(1)}, bf16[512,128]{1,0:T(8,128)(2,1)S(1)}, u32[]{:S(2)}, u32[]{:S(2)}) collective-permute-start(bf16[512,128]{1,0:T(8,128)(2,1)S(1)} %collective-permute-done.5.refs_5_), channel_id=1, source_target_pairs={{0,8},{1,9},{2,10},{3,11},{8,16},{9,17},{10,18},{11,19},{16,24},{1... | collective-permute-start | bytes 393224 | tf_op jit(solution)/shard_map/ppermute | solution.py:447
  17.4 1.7 %collective-permute-done.9.refs_8_ = bf16[512,128]{1,0:T(8,128)(2,1)S(1)} collective-permute-done((bf16[512,128]{1,0:T(8,128)(2,1)S(1)}, bf16[512,128]{1,0:T(8,128)(2,1)S(1)}, u32[]{:S(2)}, u32[]{:S(2)}) %collective-permute-start.9) | collective-permute-done | bytes 131104 | tf_op jit(solution)/shard_map/ppermute | solution.py:447
  19.3 1.8 %collective-permute-start.11 = (bf16[512,128]{1,0:T(8,128)(2,1)S(1)}, bf16[512,128]{1,0:T(8,128)(2,1)S(1)}, u32[]{:S(2)}, u32[]{:S(2)}) collective-permute-start(bf16[512,128]{1,0:T(8,128)(2,1)S(1)} %collective-permute-done.7.refs_6_), channel_id=1, source_target_pairs={{0,8},{1,9},{2,10},{3,11},{8,16},{9,17},{10,18},{11,19},{16,24},{1... | collective-permute-start | bytes 393224 | tf_op jit(solution)/shard_map/ppermute | solution.py:447
  21.1 2.0 %next_stage.3 = (f32[2048,256]{1,0:T(8,128)S(1)}, bf16[1024,1024]{1,0:T(8,128)(2,1)S(1)}, bf16[1024,1024]{1,0:T(8,128)(2,1)S(1)}) custom-call(s32[10,128]{1,0:T(8,128)S(1)} %begin.1.refs_0_, bf16[96,128,128]{2,1,0:T(8,128)(2,1)} %refs_1_.5, bf16[96,128,128]{2,1,0:T(8,128)(2,1)S(1)} %collective-permute-done.2.refs_2_, ...), custom_call_target="tpu_custom_call" | custom-call | flops 1073741824 | bytes 12582912 | tf_op jit(solution)/shard_map/next_stage/pallas_call | solution.py:364
  23.2 1.6 %collective-permute-start.10 = (bf16[512,128]{1,0:T(8,128)(2,1)S(1)}, bf16[512,128]{1,0:T(8,128)(2,1)S(1)}, u32[]{:S(2)}, u32[]{:S(2)}) collective-permute-start(bf16[512,128]{1,0:T(8,128)(2,1)S(1)} %collective-permute-done.6.refs_5_), channel_id=1, source_target_pairs={{0,8},{1,9},{2,10},{3,11},{8,16},{9,17},{10,18},{11,19},{16,24},{1... | collective-permute-start | bytes 393224 | tf_op jit(solution)/shard_map/ppermute | solution.py:447
  24.8 0.5 %collective-permute-start.14 = (bf16[512,128]{1,0:T(8,128)(2,1)S(1)}, bf16[512,128]{1,0:T(8,128)(2,1)S(1)}, u32[]{:S(2)}, u32[]{:S(2)}) collective-permute-start(bf16[512,128]{1,0:T(8,128)(2,1)S(1)} %collective-permute-done.12.refs_7_), channel_id=1, source_target_pairs={{0,4},{1,5},{2,6},{3,7},{8,0},{9,1},{10,2},{11,3},{16,8},{17,9},{1... | collective-permute-start | bytes 393224 | tf_op jit(solution)/shard_map/ppermute | solution.py:447
  25.5 1.8 %collective-permute-start.17 = (bf16[512,128]{1,0:T(8,128)(2,1)S(1)}, bf16[512,128]{1,0:T(8,128)(2,1)S(1)}, u32[]{:S(2)}, u32[]{:S(2)}) collective-permute-start(bf16[512,128]{1,0:T(8,128)(2,1)S(1)} %collective-permute-done.11.refs_6_), channel_id=1, source_target_pairs={{0,8},{1,9},{2,10},{3,11},{8,16},{9,17},{10,18},{11,19},{16,24},{1... | collective-permute-start | bytes 393224 | tf_op jit(solution)/shard_map/ppermute | solution.py:447
  27.3 2.1 %next_stage.4 = (f32[2048,256]{1,0:T(8,128)S(1)}, bf16[1024,1024]{1,0:T(8,128)(2,1)S(1)}, bf16[1024,1024]{1,0:T(8,128)(2,1)S(1)}) custom-call(s32[10,128]{1,0:T(8,128)S(1)} %begin.1.refs_0_, bf16[96,128,128]{2,1,0:T(8,128)(2,1)} %refs_1_.5, bf16[96,128,128]{2,1,0:T(8,128)(2,1)S(1)} %collective-permute-done.2.refs_2_, ...), custom_call_target="tpu_custom_call" | custom-call | flops 1073741824 | bytes 12582912 | tf_op jit(solution)/shard_map/next_stage/pallas_call | solution.py:364
  29.5 0.6 %collective-permute-done.14.refs_4_ = bf16[512,128]{1,0:T(8,128)(2,1)S(1)} collective-permute-done((bf16[512,128]{1,0:T(8,128)(2,1)S(1)}, bf16[512,128]{1,0:T(8,128)(2,1)S(1)}, u32[]{:S(2)}, u32[]{:S(2)}) %collective-permute-start.14) | collective-permute-done | bytes 131104 | tf_op jit(solution)/shard_map/ppermute | solution.py:447
  30.0 1.6 %collective-permute-start.15 = (bf16[512,128]{1,0:T(8,128)(2,1)S(1)}, bf16[512,128]{1,0:T(8,128)(2,1)S(1)}, u32[]{:S(2)}, u32[]{:S(2)}) collective-permute-start(bf16[512,128]{1,0:T(8,128)(2,1)S(1)} %collective-permute-done.10.refs_2_), channel_id=1, source_target_pairs={{0,8},{1,9},{2,10},{3,11},{8,16},{9,17},{10,18},{11,19},{16,24},{1... | collective-permute-start | bytes 393224 | tf_op jit(solution)/shard_map/ppermute | solution.py:447
  31.6 1.8 %collective-permute-start.18 = (bf16[512,128]{1,0:T(8,128)(2,1)S(1)}, bf16[512,128]{1,0:T(8,128)(2,1)S(1)}, u32[]{:S(2)}, u32[]{:S(2)}) collective-permute-start(bf16[512,128]{1,0:T(8,128)(2,1)S(1)} %collective-permute-done.16.refs_5_), channel_id=1, source_target_pairs={{0,4},{1,5},{2,6},{3,7},{8,0},{9,1},{10,2},{11,3},{16,8},{17,9},{1... | collective-permute-start | bytes 393224 | tf_op jit(solution)/shard_map/ppermute | solution.py:447
  33.4 1.3 %next_stage.5.refs_3_.refs_4_ = f32[2048,256]{1,0:T(8,128)S(1)} custom-call(bf16[1024,1024]{1,0:T(8,128)(2,1)S(1)} %get-tuple-element.71.refs_0_, bf16[1024,1024]{1,0:T(8,128)(2,1)S(1)} %get-tuple-element.72.refs_1_, bf16[512,128]{1,0:T(8,128)(2,1)S(1)} %collective-permute-done.10.refs_2_, bf16[512,128]{1,0:T(8,128)(2,1)S(1)} %collective-permute-done.17.refs_3_, ...), custom_call_target="tpu_custom_call" | custom-call | flops 1073741824 | bytes 12582912 | tf_op jit(solution)/shard_map/next_stage/pallas_call | solution.py:364
  35.4 1.2 %collective-permute-done.18.refs_3_ = bf16[512,128]{1,0:T(8,128)(2,1)S(1)} collective-permute-done((bf16[512,128]{1,0:T(8,128)(2,1)S(1)}, bf16[512,128]{1,0:T(8,128)(2,1)S(1)}, u32[]{:S(2)}, u32[]{:S(2)}) %collective-permute-start.18) | collective-permute-done | bytes 131104 | tf_op jit(solution)/shard_map/ppermute | solution.py:447
  37.2 0.7 %collective-permute-start.20 = (bf16[512,128]{1,0:T(8,128)(2,1)S(1)}, bf16[512,128]{1,0:T(8,128)(2,1)S(1)}, u32[]{:S(2)}, u32[]{:S(2)}) collective-permute-start(bf16[512,128]{1,0:T(8,128)(2,1)S(1)} %last_stages.6), channel_id=1, source_target_pairs={{0,1},{1,0},{2,3},{3,2},{4,5},{5,4},{6,7},{7,6},{8,9},{9,8},{10,11... | collective-permute-start | bytes 393224 | tf_op jit(solution)/shard_map/ppermute | solution.py:516
  37.9 0.3 collective-permute-done.21.refs_5_
  38.3 0.6 %last_stages.8 = (bf16[512,128]{1,0:T(8,128)(2,1)S(1)}, bf16[512,128]{1,0:T(8,128)(2,1)S(1)}, bf16[512,128]{1,0:T(8,128)(2,1)S(1)}) custom-call(bf16[1024,512]{1,0:T(8,128)(2,1)S(1)} %get-tuple-element.52.refs_0_, bf16[1024,512]{1,0:T(8,128)(2,1)S(1)} %get-tuple-element.53.refs_1_, bf16[512,128]{1,0:T(8,128)(2,1)S(1)} %collective-permute-done.15.refs_2_, ...), custom_call_target="tpu_custom_call" | custom-call | flops 201326592 | bytes 2097152 | tf_op jit(solution)/shard_map/last_stages/pallas_call | solution.py:394
  39.1 0.4 collective-permute-start.23
  39.4 1.1 %collective-permute-start.24 = (bf16[512,128]{1,0:T(8,128)(2,1)S(1)}, bf16[512,128]{1,0:T(8,128)(2,1)S(1)}, u32[]{:S(2)}, u32[]{:S(2)}) collective-permute-start(bf16[512,128]{1,0:T(8,128)(2,1)S(1)} %get-tuple-element.80), channel_id=1, source_target_pairs={{0,1},{1,0},{2,3},{3,2},{4,5},{5,4},{6,7},{7,6},{8,9},{9,8},{10,11... | collective-permute-start | bytes 393224 | tf_op jit(solution)/shard_map/ppermute | solution.py:516
  40.5 3.1 %collective-permute-done.20.refs_2_ = bf16[512,128]{1,0:T(8,128)(2,1)S(1)} collective-permute-done((bf16[512,128]{1,0:T(8,128)(2,1)S(1)}, bf16[512,128]{1,0:T(8,128)(2,1)S(1)}, u32[]{:S(2)}, u32[]{:S(2)}) %collective-permute-start.20) | collective-permute-done | bytes 131104 | tf_op jit(solution)/shard_map/ppermute | solution.py:516
  43.6 0.4 last_stages.9
  44.0 2.0 %collective-permute-done.24.refs_3_ = bf16[512,128]{1,0:T(8,128)(2,1)S(1)} collective-permute-done((bf16[512,128]{1,0:T(8,128)(2,1)S(1)}, bf16[512,128]{1,0:T(8,128)(2,1)S(1)}, u32[]{:S(2)}, u32[]{:S(2)}) %collective-permute-start.24) | collective-permute-done | bytes 131104 | tf_op jit(solution)/shard_map/ppermute | solution.py:516
  46.0 0.8 %result.1 = bf16[512,256]{1,0:T(8,128)(2,1)} custom-call(f32[1,256]{1,0:T(1,128)S(1)} %bitcast.4, f32[512,128]{1,0:T(8,128)S(1)} %get-tuple-element.78.refs_0_, f32[512,128]{1,0:T(8,128)S(1)} %get-tuple-element.79.refs_1_, bf16[512,128]{1,0:T(8,128)(2,1)S(1)} %collective-permute-done.20.refs_2_, bf16[512,128]{1,0:T(8,128)(2,1)S(1)} %collective-permute-done.24.refs_3_), custom_call_target="tpu_custom_call" | custom-call | flops 524288 | bytes 1048576 | tf_op jit(solution)/shard_map/result/pallas_call | solution.py:408
  (34 shorter events, 2.4 us)
Async XLA Ops:
  0.0 2.1 %collective-permute-start = (s32[1]{0:T(128)}, s32[1]{0:T(128)}, u32[]{:S(2)}, u32[]{:S(2)}) collective-permute-start(s32[1]{0:T(128)} %param.13), channel_id=1, source_target_pairs={{0,2},{1,3},{2,0},{3,1},{4,6},{5,7},{6,4},{7,5},{8,10},{9,11},{10,... | collective-permute-start | bytes 20 | tf_op jit(solution)/shard_map/ppermute | solution.py:450
  0.5 1.7 %collective-permute-start.1 = (s32[96,2]{0,1:T(2,128)}, s32[96,2]{0,1:T(2,128)S(1)}, u32[]{:S(2)}, u32[]{:S(2)}) collective-permute-start(s32[96,2]{0,1:T(2,128)} %param.12), channel_id=1, source_target_pairs={{0,2},{1,3},{2,0},{3,1},{4,6},{5,7},{6,4},{7,5},{8,10},{9,11},{10,... | collective-permute-start | bytes 2312 | tf_op jit(solution)/shard_map/ppermute | solution.py:450
  2.2 10.7 %collective-permute-start.2 = (bf16[96,128,128]{2,1,0:T(8,128)(2,1)}, bf16[96,128,128]{2,1,0:T(8,128)(2,1)S(1)}, u32[]{:S(2)}, u32[]{:S(2)}) collective-permute-start(bf16[96,128,128]{2,1,0:T(8,128)(2,1)} %refs_1_.5), channel_id=1, source_target_pairs={{0,2},{1,3},{2,0},{3,1},{4,6},{5,7},{6,4},{7,5},{8,10},{9,11},{10,... | collective-permute-start | bytes 9437192 | tf_op jit(solution)/shard_map/ppermute | solution.py:452
  2.7 5.5 %collective-permute-start.3 = (bf16[512,128]{1,0:T(8,128)(2,1)S(1)}, bf16[512,128]{1,0:T(8,128)(2,1)S(1)}, u32[]{:S(2)}, u32[]{:S(2)}) collective-permute-start(bf16[512,128]{1,0:T(8,128)(2,1)S(1)} %get-tuple-element.48), channel_id=1, source_target_pairs={{0,2},{1,0},{2,3},{3,1},{4,6},{5,4},{6,7},{7,5},{8,10},{9,8},{10,1... | collective-permute-start | bytes 393224 | tf_op jit(solution)/shard_map/ppermute | solution.py:466
  2.7 8.0 %collective-permute-start.4 = (bf16[512,128]{1,0:T(8,128)(2,1)S(1)}, bf16[512,128]{1,0:T(8,128)(2,1)S(1)}, u32[]{:S(2)}, u32[]{:S(2)}) collective-permute-start(bf16[512,128]{1,0:T(8,128)(2,1)S(1)} %get-tuple-element.50), channel_id=1, source_target_pairs={{0,2},{1,0},{2,3},{3,1},{4,6},{5,4},{6,7},{7,5},{8,10},{9,8},{10,1... | collective-permute-start | bytes 393224 | tf_op jit(solution)/shard_map/ppermute | solution.py:466
  6.0 0.7 %copy-start.1 = (s32[96,2]{0,1:T(2,128)S(1)}, s32[96,2]{0,1:T(2,128)}, u32[]{:S(2)}) copy-start(s32[96,2]{0,1:T(2,128)} %param.12) | copy-start | bytes 2308
  8.1 7.2 %collective-permute-start.5 = (bf16[512,128]{1,0:T(8,128)(2,1)S(1)}, bf16[512,128]{1,0:T(8,128)(2,1)S(1)}, u32[]{:S(2)}, u32[]{:S(2)}) collective-permute-start(bf16[512,128]{1,0:T(8,128)(2,1)S(1)} %collective-permute-done.3.refs_3_), channel_id=1, source_target_pairs={{0,8},{1,9},{2,10},{3,11},{8,16},{9,17},{10,18},{11,19},{16,24},{1... | collective-permute-start | bytes 393224 | tf_op jit(solution)/shard_map/ppermute | solution.py:447
  10.7 6.5 %collective-permute-start.8 = (bf16[512,128]{1,0:T(8,128)(2,1)S(1)}, bf16[512,128]{1,0:T(8,128)(2,1)S(1)}, u32[]{:S(2)}, u32[]{:S(2)}) collective-permute-start(bf16[512,128]{1,0:T(8,128)(2,1)S(1)} %collective-permute-done.3.refs_3_), channel_id=1, source_target_pairs={{0,4},{1,5},{2,6},{3,7},{8,0},{9,1},{10,2},{11,3},{16,8},{17,9},{1... | collective-permute-start | bytes 393224 | tf_op jit(solution)/shard_map/ppermute | solution.py:447
  10.8 8.4 %collective-permute-start.9 = (bf16[512,128]{1,0:T(8,128)(2,1)S(1)}, bf16[512,128]{1,0:T(8,128)(2,1)S(1)}, u32[]{:S(2)}, u32[]{:S(2)}) collective-permute-start(bf16[512,128]{1,0:T(8,128)(2,1)S(1)} %collective-permute-done.4.refs_4_), channel_id=1, source_target_pairs={{0,4},{1,5},{2,6},{3,7},{8,0},{9,1},{10,2},{11,3},{16,8},{17,9},{1... | collective-permute-start | bytes 393224 | tf_op jit(solution)/shard_map/ppermute | solution.py:447
  12.7 6.6 %collective-permute-start.7 = (bf16[512,128]{1,0:T(8,128)(2,1)S(1)}, bf16[512,128]{1,0:T(8,128)(2,1)S(1)}, u32[]{:S(2)}, u32[]{:S(2)}) collective-permute-start(bf16[512,128]{1,0:T(8,128)(2,1)S(1)} %collective-permute-done.4.refs_4_), channel_id=1, source_target_pairs={{0,8},{1,9},{2,10},{3,11},{8,16},{9,17},{10,18},{11,19},{16,24},{1... | collective-permute-start | bytes 393224 | tf_op jit(solution)/shard_map/ppermute | solution.py:447
  15.3 7.8 %collective-permute-start.6 = (bf16[512,128]{1,0:T(8,128)(2,1)S(1)}, bf16[512,128]{1,0:T(8,128)(2,1)S(1)}, u32[]{:S(2)}, u32[]{:S(2)}) collective-permute-start(bf16[512,128]{1,0:T(8,128)(2,1)S(1)} %collective-permute-done.5.refs_5_), channel_id=1, source_target_pairs={{0,8},{1,9},{2,10},{3,11},{8,16},{9,17},{10,18},{11,19},{16,24},{1... | collective-permute-start | bytes 393224 | tf_op jit(solution)/shard_map/ppermute | solution.py:447
  17.3 7.6 %collective-permute-start.12 = (bf16[512,128]{1,0:T(8,128)(2,1)S(1)}, bf16[512,128]{1,0:T(8,128)(2,1)S(1)}, u32[]{:S(2)}, u32[]{:S(2)}) collective-permute-start(bf16[512,128]{1,0:T(8,128)(2,1)S(1)} %collective-permute-done.8.refs_7_), channel_id=1, source_target_pairs={{0,4},{1,5},{2,6},{3,7},{8,0},{9,1},{10,2},{11,3},{16,8},{17,9},{1... | collective-permute-start | bytes 393224 | tf_op jit(solution)/shard_map/ppermute | solution.py:447
  19.1 6.2 %collective-permute-start.13 = (bf16[512,128]{1,0:T(8,128)(2,1)S(1)}, bf16[512,128]{1,0:T(8,128)(2,1)S(1)}, u32[]{:S(2)}, u32[]{:S(2)}) collective-permute-start(bf16[512,128]{1,0:T(8,128)(2,1)S(1)} %collective-permute-done.9.refs_8_), channel_id=1, source_target_pairs={{0,4},{1,5},{2,6},{3,7},{8,0},{9,1},{10,2},{11,3},{16,8},{17,9},{1... | collective-permute-start | bytes 393224 | tf_op jit(solution)/shard_map/ppermute | solution.py:447
  19.3 6.2 %collective-permute-start.11 = (bf16[512,128]{1,0:T(8,128)(2,1)S(1)}, bf16[512,128]{1,0:T(8,128)(2,1)S(1)}, u32[]{:S(2)}, u32[]{:S(2)}) collective-permute-start(bf16[512,128]{1,0:T(8,128)(2,1)S(1)} %collective-permute-done.7.refs_6_), channel_id=1, source_target_pairs={{0,8},{1,9},{2,10},{3,11},{8,16},{9,17},{10,18},{11,19},{16,24},{1... | collective-permute-start | bytes 393224 | tf_op jit(solution)/shard_map/ppermute | solution.py:447
  23.2 6.3 %collective-permute-start.10 = (bf16[512,128]{1,0:T(8,128)(2,1)S(1)}, bf16[512,128]{1,0:T(8,128)(2,1)S(1)}, u32[]{:S(2)}, u32[]{:S(2)}) collective-permute-start(bf16[512,128]{1,0:T(8,128)(2,1)S(1)} %collective-permute-done.6.refs_5_), channel_id=1, source_target_pairs={{0,8},{1,9},{2,10},{3,11},{8,16},{9,17},{10,18},{11,19},{16,24},{1... | collective-permute-start | bytes 393224 | tf_op jit(solution)/shard_map/ppermute | solution.py:447
  24.8 5.2 %collective-permute-start.14 = (bf16[512,128]{1,0:T(8,128)(2,1)S(1)}, bf16[512,128]{1,0:T(8,128)(2,1)S(1)}, u32[]{:S(2)}, u32[]{:S(2)}) collective-permute-start(bf16[512,128]{1,0:T(8,128)(2,1)S(1)} %collective-permute-done.12.refs_7_), channel_id=1, source_target_pairs={{0,4},{1,5},{2,6},{3,7},{8,0},{9,1},{10,2},{11,3},{16,8},{17,9},{1... | collective-permute-start | bytes 393224 | tf_op jit(solution)/shard_map/ppermute | solution.py:447
  25.3 6.3 %collective-permute-start.16 = (bf16[512,128]{1,0:T(8,128)(2,1)S(1)}, bf16[512,128]{1,0:T(8,128)(2,1)S(1)}, u32[]{:S(2)}, u32[]{:S(2)}) collective-permute-start(bf16[512,128]{1,0:T(8,128)(2,1)S(1)} %collective-permute-done.13.refs_8_), channel_id=1, source_target_pairs={{0,4},{1,5},{2,6},{3,7},{8,0},{9,1},{10,2},{11,3},{16,8},{17,9},{1... | collective-permute-start | bytes 393224 | tf_op jit(solution)/shard_map/ppermute | solution.py:447
  25.5 6.1 %collective-permute-start.17 = (bf16[512,128]{1,0:T(8,128)(2,1)S(1)}, bf16[512,128]{1,0:T(8,128)(2,1)S(1)}, u32[]{:S(2)}, u32[]{:S(2)}) collective-permute-start(bf16[512,128]{1,0:T(8,128)(2,1)S(1)} %collective-permute-done.11.refs_6_), channel_id=1, source_target_pairs={{0,8},{1,9},{2,10},{3,11},{8,16},{9,17},{10,18},{11,19},{16,24},{1... | collective-permute-start | bytes 393224 | tf_op jit(solution)/shard_map/ppermute | solution.py:447
  30.0 5.0 %collective-permute-start.15 = (bf16[512,128]{1,0:T(8,128)(2,1)S(1)}, bf16[512,128]{1,0:T(8,128)(2,1)S(1)}, u32[]{:S(2)}, u32[]{:S(2)}) collective-permute-start(bf16[512,128]{1,0:T(8,128)(2,1)S(1)} %collective-permute-done.10.refs_2_), channel_id=1, source_target_pairs={{0,8},{1,9},{2,10},{3,11},{8,16},{9,17},{10,18},{11,19},{16,24},{1... | collective-permute-start | bytes 393224 | tf_op jit(solution)/shard_map/ppermute | solution.py:447
  31.6 5.0 %collective-permute-start.18 = (bf16[512,128]{1,0:T(8,128)(2,1)S(1)}, bf16[512,128]{1,0:T(8,128)(2,1)S(1)}, u32[]{:S(2)}, u32[]{:S(2)}) collective-permute-start(bf16[512,128]{1,0:T(8,128)(2,1)S(1)} %collective-permute-done.16.refs_5_), channel_id=1, source_target_pairs={{0,4},{1,5},{2,6},{3,7},{8,0},{9,1},{10,2},{11,3},{16,8},{17,9},{1... | collective-permute-start | bytes 393224 | tf_op jit(solution)/shard_map/ppermute | solution.py:447
  35.3 1.6 %collective-permute-start.19 = (bf16[512,128]{1,0:T(8,128)(2,1)S(1)}, bf16[512,128]{1,0:T(8,128)(2,1)S(1)}, u32[]{:S(2)}, u32[]{:S(2)}) collective-permute-start(bf16[512,128]{1,0:T(8,128)(2,1)S(1)} %last_stages.5), channel_id=1, source_target_pairs={{0,2},{1,3},{2,0},{3,1},{4,6},{5,7},{6,4},{7,5},{8,10},{9,11},{10,... | collective-permute-start | bytes 393224 | tf_op jit(solution)/shard_map/ppermute | solution.py:509
  36.9 1.4 %collective-permute-start.21 = (bf16[512,128]{1,0:T(8,128)(2,1)S(1)}, bf16[512,128]{1,0:T(8,128)(2,1)S(1)}, u32[]{:S(2)}, u32[]{:S(2)}) collective-permute-start(bf16[512,128]{1,0:T(8,128)(2,1)S(1)} %last_stages.7), channel_id=1, source_target_pairs={{0,2},{1,3},{2,0},{3,1},{4,6},{5,7},{6,4},{7,5},{8,10},{9,11},{10,... | collective-permute-start | bytes 393224 | tf_op jit(solution)/shard_map/ppermute | solution.py:509
  37.2 6.4 %collective-permute-start.20 = (bf16[512,128]{1,0:T(8,128)(2,1)S(1)}, bf16[512,128]{1,0:T(8,128)(2,1)S(1)}, u32[]{:S(2)}, u32[]{:S(2)}) collective-permute-start(bf16[512,128]{1,0:T(8,128)(2,1)S(1)} %last_stages.6), channel_id=1, source_target_pairs={{0,1},{1,0},{2,3},{3,2},{4,5},{5,4},{6,7},{7,6},{8,9},{9,8},{10,11... | collective-permute-start | bytes 393224 | tf_op jit(solution)/shard_map/ppermute | solution.py:516
  38.8 4.8 %collective-permute-start.22 = (bf16[512,128]{1,0:T(8,128)(2,1)S(1)}, bf16[512,128]{1,0:T(8,128)(2,1)S(1)}, u32[]{:S(2)}, u32[]{:S(2)}) collective-permute-start(bf16[512,128]{1,0:T(8,128)(2,1)S(1)} %get-tuple-element.76), channel_id=1, source_target_pairs={{0,2},{1,3},{2,0},{3,1},{4,6},{5,7},{6,4},{7,5},{8,10},{9,11},{10,... | collective-permute-start | bytes 393224 | tf_op jit(solution)/shard_map/ppermute | solution.py:517
  39.1 4.6 %collective-permute-start.23 = (bf16[512,128]{1,0:T(8,128)(2,1)S(1)}, bf16[512,128]{1,0:T(8,128)(2,1)S(1)}, u32[]{:S(2)}, u32[]{:S(2)}) collective-permute-start(bf16[512,128]{1,0:T(8,128)(2,1)S(1)} %get-tuple-element.77), channel_id=1, source_target_pairs={{0,2},{1,3},{2,0},{3,1},{4,6},{5,7},{6,4},{7,5},{8,10},{9,11},{10,... | collective-permute-start | bytes 393224 | tf_op jit(solution)/shard_map/ppermute | solution.py:517
  39.4 6.6 %copy-start = (f32[256]{0:T(256)S(1)}, f32[256]{0:T(256)}, u32[]{:S(2)}) copy-start(f32[256]{0:T(256)} %param.10) | copy-start | bytes 3076
  39.4 6.6 %collective-permute-start.24 = (bf16[512,128]{1,0:T(8,128)(2,1)S(1)}, bf16[512,128]{1,0:T(8,128)(2,1)S(1)}, u32[]{:S(2)}, u32[]{:S(2)}) collective-permute-start(bf16[512,128]{1,0:T(8,128)(2,1)S(1)} %get-tuple-element.80), channel_id=1, source_target_pairs={{0,1},{1,0},{2,3},{3,2},{4,5},{5,4},{6,7},{7,6},{8,9},{9,8},{10,11... | collective-permute-start | bytes 393224 | tf_op jit(solution)/shard_map/ppermute | solution.py:516

commit v5 on v4

--- a/solution.py
+++ b/solution.py
@@ -188,11 +188,12 @@
     return [refs[i : i + parts] for i in range(0, len(refs), parts)]
 
 
-def multiply(blocks, pieces, total, out):
-    strip = min(256, blocks[0].shape[0])
+def multiply(blocks, pieces, total, out, first_row=0):
     for g, block in enumerate(blocks):
+        strip = min(256, block.shape[0])
         for top in range(0, block.shape[0], strip):
-            to = slice(g * block.shape[0] + top, g * block.shape[0] + top + strip)
+            start = first_row + g * block.shape[0] + top
+            to = slice(start, start + strip)
             result = None if total is None else total[to]
             column = 0
             for piece in pieces:
@@ -211,12 +212,13 @@
     groups = layout.groups
     counts, coords, table = refs[:groups], refs[groups : 2 * groups], refs[2 * groups]
     plan(layout, counts, coords, table)
+    clear(*refs[2 * groups + 1 :])
 
 
 def first_kernel(layout, parts, *refs):
     groups = layout.groups
     table, tiles, refs = refs[0], refs[1 : 1 + groups], refs[1 + groups :]
-    piece, refs = refs[:parts], refs[parts:]
+    piece, refs = refs[:parts], refs[parts + groups :]
     total, seconds, lasts = refs[0], refs[1 : 1 + groups], refs[1 + groups : 1 + 2 * groups]
     *firsts, entries, sems, table_sem = refs[1 + 2 * groups :]
     load = pltpu.make_async_copy(table, entries, table_sem)
@@ -227,7 +229,7 @@
     started = [jnp.int32(0)] * 3
     for g in range(groups):
         started[0] += fill(layout, 0, g, entries, tiles[g], firsts[g], sems.at[0])
-    clear(*seconds, *lasts)
+    clear(*lasts)
     for g in range(groups):
         started[1] += fill(layout, 1, g, entries, tiles[g], seconds[g], sems.at[1])
         started[2] += fill(layout, last, g, entries, tiles[g], lasts[g], sems.at[2])
@@ -243,17 +245,19 @@
         table, tiles, refs = refs[0], refs[1 : 1 + groups], refs[1 + groups :]
     blocks, refs = refs[:groups], refs[groups:]
     pieces, refs = grouped(refs[: n_pieces * parts], parts), refs[n_pieces * parts :]
-    total, next_total, *rest = refs
+    total, refs = refs[0], refs[1 + (groups if building else 0) :]
+    next_total, *rest = refs
     if building:
         *next_blocks, entries, sem, table_sem = rest
         load = pltpu.make_async_copy(table, entries, table_sem)
         load.start()
-        clear(*next_blocks)
+    multiply(blocks[:1], pieces, total, next_total)
+    if building:
         load.wait()
         started = jnp.int32(0)
         for g in range(groups):
             started += fill(layout, stage + 1, g, entries, tiles[g], next_blocks[g], sem)
-    multiply(blocks, pieces, total, next_total)
+    multiply(blocks[1:], pieces, total, next_total, blocks[0].shape[0])
     if building:
         finish_fill(layout, tiles[0], started, sem)
 
@@ -316,20 +320,23 @@
 
 
 def begin(layout, groups):
-    counts, coords, _ = zip(*groups)
+    counts, coords, tiles = zip(*groups)
     n = layout.groups
-    return pl.pallas_call(
+    middle = range(1, len(layout.widths) - 1)
+    outs = pl.pallas_call(
         functools.partial(begin_kernel, layout),
-        out_shape=pltpu.VMEM((layout.lines, layout.line), jnp.int32),
+        out_shape=[pltpu.VMEM((layout.lines, layout.line), jnp.int32)]
+        + [pltpu.VMEM(layout.block(i), tiles[0].dtype) for i in middle for _ in range(n)],
         in_specs=[SMEM] * n + [VMEM] * n,
-        out_specs=VMEM,
+        out_specs=[VMEM] * (1 + n * len(middle)),
         compiler_params=PARAMS,
         cost_estimate=cost(1000000, 4 * layout.lines * layout.line),
         name="begin",
     )(*counts, *[c.T for c in coords])
-
-
-def first_stage(layout, table, groups, piece):
+    return outs[0], [None, *grouped(outs[1:], n)]
+
+
+def first_stage(layout, table, groups, piece, cleared):
     tiles = [g[2] for g in groups]
     n, width, dtype = layout.groups, sum(x.shape[1] for x in piece), tiles[0].dtype
     last = len(layout.widths) - 1
@@ -339,7 +346,7 @@
         out_shape=[pltpu.VMEM((rows, width), jnp.float32)]
         + [pltpu.VMEM(layout.block(1), dtype)] * n
         + [pltpu.VMEM(layout.block(last), dtype)] * n,
-        in_specs=[VMEM] + [ANY] * n + [VMEM] * len(piece),
+        in_specs=[VMEM] + [ANY] * n + [VMEM] * (len(piece) + n),
         out_specs=[VMEM] * (2 * n + 1),
         scratch_shapes=[pltpu.VMEM(layout.block(0), dtype)] * n
         + [
@@ -347,26 +354,29 @@
             pltpu.SemaphoreType.DMA((3,)),
             pltpu.SemaphoreType.DMA,
         ],
+        input_output_aliases={1 + n + len(piece) + i: 1 + i for i in range(n)},
         compiler_params=PARAMS,
         cost_estimate=stage_cost(layout, 0, width),
         name="first_stage",
-    )(*in_vmem(table), *in_hbm(tiles[0]), *tiles[1:], *in_vmem(*piece))
+    )(*in_vmem(table), *in_hbm(tiles[0]), *tiles[1:], *in_vmem(*piece, *cleared))
     return outs[0], outs[1 : n + 1], outs[n + 1 :]
 
 
-def next_stage(layout, stage, table, groups, blocks, pieces, total):
+def next_stage(layout, stage, table, groups, blocks, pieces, total, cleared=None):
     tiles = [g[2] for g in groups]
     width, n = total.shape[1], layout.groups
-    building = table is not None
+    building = cleared is not None
     parts = len(pieces[0])
     held = in_vmem(*blocks, *[x for piece in pieces for x in piece], total)
     sources = [*in_vmem(table), *in_hbm(tiles[0]), *tiles[1:]] if building else []
+    targets = in_vmem(*cleared) if building else []
+    first = len(sources) + len(held)
     outs = pl.pallas_call(
         functools.partial(next_kernel, layout, stage, len(pieces), parts, building),
         out_shape=[pltpu.VMEM(total.shape, total.dtype)]
-        + ([pltpu.VMEM(layout.block(stage + 1), blocks[0].dtype)] * n if building else []),
-        in_specs=([VMEM] + [ANY] * n if building else []) + [VMEM] * len(held),
-        out_specs=[VMEM] * (1 + n if building else 1),
+        + [pltpu.VMEM(x.shape, x.dtype) for x in targets],
+        in_specs=([VMEM] + [ANY] * n if building else []) + [VMEM] * (len(held) + len(targets)),
+        out_specs=[VMEM] * (1 + len(targets)),
         scratch_shapes=[
             pltpu.SMEM(table.shape, jnp.int32),
             pltpu.SemaphoreType.DMA,
@@ -374,10 +384,11 @@
         ]
         if building
         else [],
+        input_output_aliases={first + i: 1 + i for i in range(len(targets))},
         compiler_params=PARAMS,
         cost_estimate=stage_cost(layout, stage, width),
         name="next_stage",
-    )(*sources, *held)
+    )(*sources, *held, *targets)
     return outs[0], outs[1:]
 
 
@@ -464,12 +475,12 @@
         for r in range(replicas)
     ]
     own = [lax.ppermute(part, AXES, give) for part in shard]
-    table = begin(layout, groups)
+    table, cleared = begin(layout, groups)
     own = [lax.optimization_barrier((part, table))[0] for part in own]
     far = chips // 2
     ways = 1, -1
     held = [None, [[step_on(part, way) for way in ways] for part in own]]
-    total, blocks, lasts = first_stage(layout, table, groups, own)
+    total, blocks, lasts = first_stage(layout, table, groups, own, cleared[1])
 
     def pieces(step):
         return [list(piece) for piece in zip(*held[step])]
@@ -484,11 +495,11 @@
         if step < far:
             held.append([[step_on(x, way) for x, way in zip(pair, ways)] for pair in sent])
             total, blocks = next_stage(
-                layout, step - 1, table, groups, blocks, pieces(step - 1), total
+                layout, step - 1, table, groups, blocks, pieces(step - 1), total, cleared[step]
             )
         else:
             held.append([[step_on(sent[i][i], way)] for i, way in enumerate(ways)])
-            total, _ = next_stage(layout, step - 1, None, groups, blocks, pieces(step - 1), total)
+            total, _ = next_stage(layout, step - 1, table, groups, blocks, pieces(step - 1), total)
 
     def finish(parts, *jobs, after=None):
         stages = [(lasts, [[x for part in parts for x in held[far][part]]])]
@@ -539,11 +550,11 @@
     groups = [groups]
     depth, last = layout.block(0)[1], layout.sections - 1
     pieces = [[panels[i * depth : (i + 1) * depth]] for i in range(last + 1)]
-    table = begin(layout, groups)
-    total, blocks, lasts = first_stage(layout, table, groups, pieces[0])
+    table, cleared = begin(layout, groups)
+    total, blocks, lasts = first_stage(layout, table, groups, pieces[0], cleared[1])
     for i in range(1, last):
-        using = table if i < last - 1 else None
-        total, blocks = next_stage(layout, i, using, groups, blocks, [pieces[i]], total)
+        using = cleared[i + 1] if i < last - 1 else None
+        total, blocks = next_stage(layout, i, table, groups, blocks, [pieces[i]], total, using)
     ending = [(lasts, [pieces[last]])]
     (total,) = last_stages(ending, total, depth, [(0, lambda: 0, [0], None, jnp.float32)])
     total = total.astype(jnp.bfloat16)

time: 47.1 us -> 46.4 us (0.985)
  starting transfers between devices: 22.5 us -> 20.3 us
  waiting for transfers between devices: 9.79 us -> 11.3 us
    ppermute x14, starting transfers between devices: 16.3 us -> 14.6 us  [step_on(): return lax.ppermute(array, AXES, hops)]
    ppermute x14, waiting for transfers between devices: 3.76 us -> 5.26 us  [step_on(): return lax.ppermute(array, AXES, hops)]
    pallas_call x1, Pallas kernels: 0.82 us -> 1.82 us  [begin(): pl.pallas_call(functools.partial(begin_kernel, layout), out_shape=[pltpu....]
    pallas_call x3, Pallas kernels: 5.46 us -> 4.7 us  [next_stage(): pl.pallas_call(functools.partial(next_kernel, layout, stage, len(pieces),...]
    ppermute x2, waiting for transfers between devices: 0.58 us -> 0.01 us  [ring_stages(): own = [lax.ppermute(part, AXES, give) for part in shard]]
    ppermute x2, starting transfers between devices: 1.76 us -> 1.2 us  [ring_stages(): got.append(lax.ppermute(summed, 'rep', other))]
    ppermute x2, waiting for transfers between devices: 0.33 us -> 0.9 us  [ring_stages(): theirs.append(lax.ppermute(given, AXES, pairs))]
where the time goes in v5:
time: 46.4 us; the launch traced here: 46.1 us
  starting transfers between devices  20.3 us (44%)
  Pallas kernels  13 us (28%)
  waiting for transfers between devices  11.3 us (24%)
  between operations  0.81 us (2%)
  local copies, waits for them, and re-layouts  0.68 us (1%)
    ppermute x14, starting transfers between devices, step_on(): return lax.ppermute(array, AXES, hops)  14.6 us
    ppermute x14, waiting for transfers between devices, step_on(): return lax.ppermute(array, AXES, hops)  5.26 us
    ppermute x2, waiting for transfers between devices, ring_stages(): got.append(lax.ppermute(summed, 'rep', other))  5.1 us
    pallas_call x3, Pallas kernels, next_stage(): pl.pallas_call(functools.partial(next_kernel, layout, stage, len(pieces),...  4.7 us
    ppermute x2, starting transfers between devices, ring_stages(): own = [lax.ppermute(part, AXES, give) for part in shard]  2.72 us
    pallas_call x1, Pallas kernels, first_stage(): pl.pallas_call(functools.partial(first_kernel, layout, len(piece)), out_s...  2.22 us
    pallas_call x5, Pallas kernels, last_stages(): pl.pallas_call(functools.partial(last_kernel, counts, parts, inner, group...  1.83 us
    pallas_call x1, Pallas kernels, begin(): pl.pallas_call(functools.partial(begin_kernel, layout), out_shape=[pltpu....  1.82 us
  transfers between devices with their start and end apart: 25, of which 8 were waited for; matrix products, arithmetic and copies ran while one was open for 0% of the time, Pallas kernels for 26%

profile of v5, /device:TPU:0, one launch (start us, length us, event | category | flops | bytes accessed | tf_op | source)
XLA Modules:
  0.0 46.1 jit_solution(2841423304728146380)
XLA Ops:
  0.0 0.5 collective-permute-start
  0.5 1.6 %prepare.1 = (bf16[512,128]{1,0:T(8,128)(2,1)S(1)}, bf16[512,128]{1,0:T(8,128)(2,1)S(1)}) custom-call(bf16[512,256]{1,0:T(8,128)(2,1)} %rows_hbm.1, s32[1,512]{1,0:T(1,128)} %bitcast.7, bf16[256,256]{1,0:T(8,128)(2,1)} %weight_hbm.1), custom_call_target="tpu_custom_call" | custom-call | flops 268435456 | bytes 524288 | tf_op jit(solution)/shard_map/prepare/pallas_call | solution.py:56
  2.2 0.5 %collective-permute-start.2 = (bf16[96,128,128]{2,1,0:T(8,128)(2,1)}, bf16[96,128,128]{2,1,0:T(8,128)(2,1)S(1)}, u32[]{:S(2)}, u32[]{:S(2)}) collective-permute-start(bf16[96,128,128]{2,1,0:T(8,128)(2,1)} %refs_1_.5), channel_id=1, source_target_pairs={{0,2},{1,3},{2,0},{3,1},{4,6},{5,7},{6,4},{7,5},{8,10},{9,11},{10,... | collective-permute-start | bytes 9437192 | tf_op jit(solution)/shard_map/ppermute | solution.py:463
  2.7 2.7 %collective-permute-start.4 = (bf16[512,128]{1,0:T(8,128)(2,1)S(1)}, bf16[512,128]{1,0:T(8,128)(2,1)S(1)}, u32[]{:S(2)}, u32[]{:S(2)}) collective-permute-start(bf16[512,128]{1,0:T(8,128)(2,1)S(1)} %get-tuple-element.58), channel_id=1, source_target_pairs={{0,2},{1,0},{2,3},{3,1},{4,6},{5,4},{6,7},{7,5},{8,10},{9,8},{10,1... | collective-permute-start | bytes 393224 | tf_op jit(solution)/shard_map/ppermute | solution.py:477
  6.1 0.7 %copy-done.1 = s32[96,2]{0,1:T(2,128)S(1)} copy-done((s32[96,2]{0,1:T(2,128)S(1)}, s32[96,2]{0,1:T(2,128)}, u32[]{:S(2)}) %copy-start.1) | copy-done | bytes 792
  6.7 1.8 %begin.1 = (s32[10,128]{1,0:T(8,128)S(1)}, bf16[1024,1024]{1,0:T(8,128)(2,1)S(1)}, bf16[1024,1024]{1,0:T(8,128)(2,1)S(1)}, bf16[1024,1024]{1,0:T(8,128)(2,1)S(1)...) custom-call(s32[1]{0:T(128)S(6)} %copy.20.refs_0_, ...), custom_call_target="tpu_custom_call" | custom-call | flops 1000000 | bytes 5120 | tf_op jit(solution)/shard_map/begin/pallas_call | solution.py:326
  8.6 2.2 %collective-permute-start.5 = (bf16[512,128]{1,0:T(8,128)(2,1)S(1)}, bf16[512,128]{1,0:T(8,128)(2,1)S(1)}, u32[]{:S(2)}, u32[]{:S(2)}) collective-permute-start(bf16[512,128]{1,0:T(8,128)(2,1)S(1)} %collective-permute-done.3.refs_3_), channel_id=1, source_target_pairs={{0,8},{1,9},{2,10},{3,11},{8,16},{9,17},{10,18},{11,19},{16,24},{1... | collective-permute-start | bytes 393224 | tf_op jit(solution)/shard_map/ppermute | solution.py:458
  10.8 2.0 %collective-permute-start.7 = (bf16[512,128]{1,0:T(8,128)(2,1)S(1)}, bf16[512,128]{1,0:T(8,128)(2,1)S(1)}, u32[]{:S(2)}, u32[]{:S(2)}) collective-permute-start(bf16[512,128]{1,0:T(8,128)(2,1)S(1)} %collective-permute-done.4.refs_4_), channel_id=1, source_target_pairs={{0,8},{1,9},{2,10},{3,11},{8,16},{9,17},{10,18},{11,19},{16,24},{1... | collective-permute-start | bytes 393224 | tf_op jit(solution)/shard_map/ppermute | solution.py:458
  12.8 2.2 %first_stage.1 = (f32[2048,256]{1,0:T(8,128)S(1)}, bf16[1024,1024]{1,0:T(8,128)(2,1)S(1)}, bf16[1024,1024]{1,0:T(8,128)(2,1)S(1)}, bf16[1024,512]{1,0:T(8,128)(2,1)S(1)}, bf16[1024,512]{1,0:T(8,128)(2,1)S(1)}) custom-call(s32[10,128]{1,0:T(8,128)S(1)} %get-tuple-element.54.refs_0_, ...), custom_call_target="tpu_custom_call", output_to_operand_aliasing={{1}: (5, {}), {2}: (6, {})} | custom-call | flops 536870912 | bytes 8388608 | tf_op jit(solution)/shard_map/first_stage/pallas_call | solution.py:344
  15.0 2.1 %collective-permute-start.6 = (bf16[512,128]{1,0:T(8,128)(2,1)S(1)}, bf16[512,128]{1,0:T(8,128)(2,1)S(1)}, u32[]{:S(2)}, u32[]{:S(2)}) collective-permute-start(bf16[512,128]{1,0:T(8,128)(2,1)S(1)} %collective-permute-done.5.refs_5_), channel_id=1, source_target_pairs={{0,8},{1,9},{2,10},{3,11},{8,16},{9,17},{10,18},{11,19},{16,24},{1... | collective-permute-start | bytes 393224 | tf_op jit(solution)/shard_map/ppermute | solution.py:458
  17.1 0.7 %collective-permute-done.7.refs_6_ = bf16[512,128]{1,0:T(8,128)(2,1)S(1)} collective-permute-done((bf16[512,128]{1,0:T(8,128)(2,1)S(1)}, bf16[512,128]{1,0:T(8,128)(2,1)S(1)}, u32[]{:S(2)}, u32[]{:S(2)}) %collective-permute-start.7) | collective-permute-done | bytes 131104 | tf_op jit(solution)/shard_map/ppermute | solution.py:458
  17.8 1.9 %collective-permute-start.11 = (bf16[512,128]{1,0:T(8,128)(2,1)S(1)}, bf16[512,128]{1,0:T(8,128)(2,1)S(1)}, u32[]{:S(2)}, u32[]{:S(2)}) collective-permute-start(bf16[512,128]{1,0:T(8,128)(2,1)S(1)} %collective-permute-done.7.refs_6_), channel_id=1, source_target_pairs={{0,8},{1,9},{2,10},{3,11},{8,16},{9,17},{10,18},{11,19},{16,24},{1... | collective-permute-start | bytes 393224 | tf_op jit(solution)/shard_map/ppermute | solution.py:458
  19.9 1.8 %next_stage.3 = (f32[2048,256]{1,0:T(8,128)S(1)}, bf16[1024,1024]{1,0:T(8,128)(2,1)S(1)}, bf16[1024,1024]{1,0:T(8,128)(2,1)S(1)}) custom-call(s32[10,128]{1,0:T(8,128)S(1)} %get-tuple-element.54.refs_0_, bf16[96,128,128]{2,1,0:T(8,128)(2,1)} %refs_1_.5, ...), custom_call_target="tpu_custom_call", output_to_operand_aliasing={{1}: (10, {}), {2}: (11, {})} | custom-call | flops 1073741824 | bytes 12582912 | tf_op jit(solution)/shard_map/next_stage/pallas_call | solution.py:374
  21.7 1.9 %collective-permute-start.10 = (bf16[512,128]{1,0:T(8,128)(2,1)S(1)}, bf16[512,128]{1,0:T(8,128)(2,1)S(1)}, u32[]{:S(2)}, u32[]{:S(2)}) collective-permute-start(bf16[512,128]{1,0:T(8,128)(2,1)S(1)} %collective-permute-done.6.refs_5_), channel_id=1, source_target_pairs={{0,8},{1,9},{2,10},{3,11},{8,16},{9,17},{10,18},{11,19},{16,24},{1... | collective-permute-start | bytes 393224 | tf_op jit(solution)/shard_map/ppermute | solution.py:458
  23.8 1.8 %collective-permute-start.17 = (bf16[512,128]{1,0:T(8,128)(2,1)S(1)}, bf16[512,128]{1,0:T(8,128)(2,1)S(1)}, u32[]{:S(2)}, u32[]{:S(2)}) collective-permute-start(bf16[512,128]{1,0:T(8,128)(2,1)S(1)} %collective-permute-done.11.refs_6_), channel_id=1, source_target_pairs={{0,8},{1,9},{2,10},{3,11},{8,16},{9,17},{10,18},{11,19},{16,24},{1... | collective-permute-start | bytes 393224 | tf_op jit(solution)/shard_map/ppermute | solution.py:458
  25.8 1.6 %next_stage.4 = (f32[2048,256]{1,0:T(8,128)S(1)}, bf16[1024,1024]{1,0:T(8,128)(2,1)S(1)}, bf16[1024,1024]{1,0:T(8,128)(2,1)S(1)}) custom-call(s32[10,128]{1,0:T(8,128)S(1)} %get-tuple-element.54.refs_0_, bf16[96,128,128]{2,1,0:T(8,128)(2,1)} %refs_1_.5, ...), custom_call_target="tpu_custom_call", output_to_operand_aliasing={{1}: (10, {}), {2}: (11, {})} | custom-call | flops 1073741824 | bytes 12582912 | tf_op jit(solution)/shard_map/next_stage/pallas_call | solution.py:374
  27.5 1.6 %collective-permute-done.14.refs_4_ = bf16[512,128]{1,0:T(8,128)(2,1)S(1)} collective-permute-done((bf16[512,128]{1,0:T(8,128)(2,1)S(1)}, bf16[512,128]{1,0:T(8,128)(2,1)S(1)}, u32[]{:S(2)}, u32[]{:S(2)}) %collective-permute-start.14) | collective-permute-done | bytes 131104 | tf_op jit(solution)/shard_map/ppermute | solution.py:458
  29.1 1.7 %collective-permute-start.15 = (bf16[512,128]{1,0:T(8,128)(2,1)S(1)}, bf16[512,128]{1,0:T(8,128)(2,1)S(1)}, u32[]{:S(2)}, u32[]{:S(2)}) collective-permute-start(bf16[512,128]{1,0:T(8,128)(2,1)S(1)} %collective-permute-done.10.refs_2_), channel_id=1, source_target_pairs={{0,8},{1,9},{2,10},{3,11},{8,16},{9,17},{10,18},{11,19},{16,24},{1... | collective-permute-start | bytes 393224 | tf_op jit(solution)/shard_map/ppermute | solution.py:458
  30.9 0.5 %collective-permute-start.18 = (bf16[512,128]{1,0:T(8,128)(2,1)S(1)}, bf16[512,128]{1,0:T(8,128)(2,1)S(1)}, u32[]{:S(2)}, u32[]{:S(2)}) collective-permute-start(bf16[512,128]{1,0:T(8,128)(2,1)S(1)} %collective-permute-done.16.refs_5_), channel_id=1, source_target_pairs={{0,4},{1,5},{2,6},{3,7},{8,0},{9,1},{10,2},{11,3},{16,8},{17,9},{1... | collective-permute-start | bytes 393224 | tf_op jit(solution)/shard_map/ppermute | solution.py:458
  31.3 1.3 %next_stage.5.refs_3_.refs_4_ = f32[2048,256]{1,0:T(8,128)S(1)} custom-call(bf16[1024,1024]{1,0:T(8,128)(2,1)S(1)} %get-tuple-element.85.refs_0_, bf16[1024,1024]{1,0:T(8,128)(2,1)S(1)} %get-tuple-element.86.refs_1_, bf16[512,128]{1,0:T(8,128)(2,1)S(1)} %collective-permute-done.10.refs_2_, bf16[512,128]{1,0:T(8,128)(2,1)S(1)} %collective-permute-done.17.refs_3_, ...), custom_call_target="tpu_custom_call" | custom-call | flops 1073741824 | bytes 12582912 | tf_op jit(solution)/shard_map/next_stage/pallas_call | solution.py:374
  32.6 1.5 %collective-permute-done.15.refs_2_ = bf16[512,128]{1,0:T(8,128)(2,1)S(1)} collective-permute-done((bf16[512,128]{1,0:T(8,128)(2,1)S(1)}, bf16[512,128]{1,0:T(8,128)(2,1)S(1)}, u32[]{:S(2)}, u32[]{:S(2)}) %collective-permute-start.15) | collective-permute-done | bytes 131104 | tf_op jit(solution)/shard_map/ppermute | solution.py:458
  34.1 0.3 last_stages.5
  34.4 1.4 %collective-permute-done.18.refs_3_ = bf16[512,128]{1,0:T(8,128)(2,1)S(1)} collective-permute-done((bf16[512,128]{1,0:T(8,128)(2,1)S(1)}, bf16[512,128]{1,0:T(8,128)(2,1)S(1)}, u32[]{:S(2)}, u32[]{:S(2)}) %collective-permute-start.18) | collective-permute-done | bytes 131104 | tf_op jit(solution)/shard_map/ppermute | solution.py:458
  36.2 0.3 last_stages.6
  36.6 0.9 %collective-permute-done.21.refs_5_ = bf16[512,128]{1,0:T(8,128)(2,1)S(1)} collective-permute-done((bf16[512,128]{1,0:T(8,128)(2,1)S(1)}, bf16[512,128]{1,0:T(8,128)(2,1)S(1)}, u32[]{:S(2)}, u32[]{:S(2)}) %collective-permute-start.21) | collective-permute-done | bytes 131104 | tf_op jit(solution)/shard_map/ppermute | solution.py:520
  37.5 0.6 %last_stages.8 = (bf16[512,128]{1,0:T(8,128)(2,1)S(1)}, bf16[512,128]{1,0:T(8,128)(2,1)S(1)}, bf16[512,128]{1,0:T(8,128)(2,1)S(1)}) custom-call(bf16[1024,512]{1,0:T(8,128)(2,1)S(1)} %get-tuple-element.62.refs_0_, bf16[1024,512]{1,0:T(8,128)(2,1)S(1)} %get-tuple-element.63.refs_1_, bf16[512,128]{1,0:T(8,128)(2,1)S(1)} %collective-permute-done.15.refs_2_, ...), custom_call_target="tpu_custom_call" | custom-call | flops 201326592 | bytes 2097152 | tf_op jit(solution)/shard_map/last_stages/pallas_call | solution.py:405
  38.3 0.4 collective-permute-start.23
  38.7 1.1 %collective-permute-start.24 = (bf16[512,128]{1,0:T(8,128)(2,1)S(1)}, bf16[512,128]{1,0:T(8,128)(2,1)S(1)}, u32[]{:S(2)}, u32[]{:S(2)}) collective-permute-start(bf16[512,128]{1,0:T(8,128)(2,1)S(1)} %get-tuple-element.94), channel_id=1, source_target_pairs={{0,1},{1,0},{2,3},{3,2},{4,5},{5,4},{6,7},{7,6},{8,9},{9,8},{10,11... | collective-permute-start | bytes 393224 | tf_op jit(solution)/shard_map/ppermute | solution.py:527
  39.7 3.1 %collective-permute-done.20.refs_2_ = bf16[512,128]{1,0:T(8,128)(2,1)S(1)} collective-permute-done((bf16[512,128]{1,0:T(8,128)(2,1)S(1)}, bf16[512,128]{1,0:T(8,128)(2,1)S(1)}, u32[]{:S(2)}, u32[]{:S(2)}) %collective-permute-start.20) | collective-permute-done | bytes 131104 | tf_op jit(solution)/shard_map/ppermute | solution.py:527
  42.9 0.4 last_stages.9
  43.3 2.0 %collective-permute-done.24.refs_3_ = bf16[512,128]{1,0:T(8,128)(2,1)S(1)} collective-permute-done((bf16[512,128]{1,0:T(8,128)(2,1)S(1)}, bf16[512,128]{1,0:T(8,128)(2,1)S(1)}, u32[]{:S(2)}, u32[]{:S(2)}) %collective-permute-start.24) | collective-permute-done | bytes 131104 | tf_op jit(solution)/shard_map/ppermute | solution.py:527
  45.3 0.8 %result.1 = bf16[512,256]{1,0:T(8,128)(2,1)} custom-call(f32[1,256]{1,0:T(1,128)S(1)} %bitcast.4, f32[512,128]{1,0:T(8,128)S(1)} %get-tuple-element.92.refs_0_, f32[512,128]{1,0:T(8,128)S(1)} %get-tuple-element.93.refs_1_, bf16[512,128]{1,0:T(8,128)(2,1)S(1)} %collective-permute-done.20.refs_2_, bf16[512,128]{1,0:T(8,128)(2,1)S(1)} %collective-permute-done.24.refs_3_), custom_call_target="tpu_custom_call" | custom-call | flops 524288 | bytes 1048576 | tf_op jit(solution)/shard_map/result/pallas_call | solution.py:419
  (34 shorter events, 1.5 us)
Async XLA Ops:
  0.0 2.1 %collective-permute-start = (s32[1]{0:T(128)}, s32[1]{0:T(128)}, u32[]{:S(2)}, u32[]{:S(2)}) collective-permute-start(s32[1]{0:T(128)} %param.13), channel_id=1, source_target_pairs={{0,2},{1,3},{2,0},{3,1},{4,6},{5,7},{6,4},{7,5},{8,10},{9,11},{10,... | collective-permute-start | bytes 20 | tf_op jit(solution)/shard_map/ppermute | solution.py:461
  0.5 1.7 %collective-permute-start.1 = (s32[96,2]{0,1:T(2,128)}, s32[96,2]{0,1:T(2,128)S(1)}, u32[]{:S(2)}, u32[]{:S(2)}) collective-permute-start(s32[96,2]{0,1:T(2,128)} %param.12), channel_id=1, source_target_pairs={{0,2},{1,3},{2,0},{3,1},{4,6},{5,7},{6,4},{7,5},{8,10},{9,11},{10,... | collective-permute-start | bytes 2312 | tf_op jit(solution)/shard_map/ppermute | solution.py:461
  2.2 10.6 %collective-permute-start.2 = (bf16[96,128,128]{2,1,0:T(8,128)(2,1)}, bf16[96,128,128]{2,1,0:T(8,128)(2,1)S(1)}, u32[]{:S(2)}, u32[]{:S(2)}) collective-permute-start(bf16[96,128,128]{2,1,0:T(8,128)(2,1)} %refs_1_.5), channel_id=1, source_target_pairs={{0,2},{1,3},{2,0},{3,1},{4,6},{5,7},{6,4},{7,5},{8,10},{9,11},{10,... | collective-permute-start | bytes 9437192 | tf_op jit(solution)/shard_map/ppermute | solution.py:463
  2.7 5.9 %collective-permute-start.3 = (bf16[512,128]{1,0:T(8,128)(2,1)S(1)}, bf16[512,128]{1,0:T(8,128)(2,1)S(1)}, u32[]{:S(2)}, u32[]{:S(2)}) collective-permute-start(bf16[512,128]{1,0:T(8,128)(2,1)S(1)} %get-tuple-element.56), channel_id=1, source_target_pairs={{0,2},{1,0},{2,3},{3,1},{4,6},{5,4},{6,7},{7,5},{8,10},{9,8},{10,1... | collective-permute-start | bytes 393224 | tf_op jit(solution)/shard_map/ppermute | solution.py:477
  2.7 8.0 %collective-permute-start.4 = (bf16[512,128]{1,0:T(8,128)(2,1)S(1)}, bf16[512,128]{1,0:T(8,128)(2,1)S(1)}, u32[]{:S(2)}, u32[]{:S(2)}) collective-permute-start(bf16[512,128]{1,0:T(8,128)(2,1)S(1)} %get-tuple-element.58), channel_id=1, source_target_pairs={{0,2},{1,0},{2,3},{3,1},{4,6},{5,4},{6,7},{7,5},{8,10},{9,8},{10,1... | collective-permute-start | bytes 393224 | tf_op jit(solution)/shard_map/ppermute | solution.py:477
  6.0 0.7 %copy-start.1 = (s32[96,2]{0,1:T(2,128)S(1)}, s32[96,2]{0,1:T(2,128)}, u32[]{:S(2)}) copy-start(s32[96,2]{0,1:T(2,128)} %param.12) | copy-start | bytes 2308
  8.6 6.4 %collective-permute-start.5 = (bf16[512,128]{1,0:T(8,128)(2,1)S(1)}, bf16[512,128]{1,0:T(8,128)(2,1)S(1)}, u32[]{:S(2)}, u32[]{:S(2)}) collective-permute-start(bf16[512,128]{1,0:T(8,128)(2,1)S(1)} %collective-permute-done.3.refs_3_), channel_id=1, source_target_pairs={{0,8},{1,9},{2,10},{3,11},{8,16},{9,17},{10,18},{11,19},{16,24},{1... | collective-permute-start | bytes 393224 | tf_op jit(solution)/shard_map/ppermute | solution.py:458
  10.7 6.4 %collective-permute-start.8 = (bf16[512,128]{1,0:T(8,128)(2,1)S(1)}, bf16[512,128]{1,0:T(8,128)(2,1)S(1)}, u32[]{:S(2)}, u32[]{:S(2)}) collective-permute-start(bf16[512,128]{1,0:T(8,128)(2,1)S(1)} %collective-permute-done.3.refs_3_), channel_id=1, source_target_pairs={{0,4},{1,5},{2,6},{3,7},{8,0},{9,1},{10,2},{11,3},{16,8},{17,9},{1... | collective-permute-start | bytes 393224 | tf_op jit(solution)/shard_map/ppermute | solution.py:458
  10.8 7.1 %collective-permute-start.7 = (bf16[512,128]{1,0:T(8,128)(2,1)S(1)}, bf16[512,128]{1,0:T(8,128)(2,1)S(1)}, u32[]{:S(2)}, u32[]{:S(2)}) collective-permute-start(bf16[512,128]{1,0:T(8,128)(2,1)S(1)} %collective-permute-done.4.refs_4_), channel_id=1, source_target_pairs={{0,8},{1,9},{2,10},{3,11},{8,16},{9,17},{10,18},{11,19},{16,24},{1... | collective-permute-start | bytes 393224 | tf_op jit(solution)/shard_map/ppermute | solution.py:458
  12.8 7.0 %collective-permute-start.9 = (bf16[512,128]{1,0:T(8,128)(2,1)S(1)}, bf16[512,128]{1,0:T(8,128)(2,1)S(1)}, u32[]{:S(2)}, u32[]{:S(2)}) collective-permute-start(bf16[512,128]{1,0:T(8,128)(2,1)S(1)} %collective-permute-done.4.refs_4_), channel_id=1, source_target_pairs={{0,4},{1,5},{2,6},{3,7},{8,0},{9,1},{10,2},{11,3},{16,8},{17,9},{1... | collective-permute-start | bytes 393224 | tf_op jit(solution)/shard_map/ppermute | solution.py:458
  15.0 6.7 %collective-permute-start.6 = (bf16[512,128]{1,0:T(8,128)(2,1)S(1)}, bf16[512,128]{1,0:T(8,128)(2,1)S(1)}, u32[]{:S(2)}, u32[]{:S(2)}) collective-permute-start(bf16[512,128]{1,0:T(8,128)(2,1)S(1)} %collective-permute-done.5.refs_5_), channel_id=1, source_target_pairs={{0,8},{1,9},{2,10},{3,11},{8,16},{9,17},{10,18},{11,19},{16,24},{1... | collective-permute-start | bytes 393224 | tf_op jit(solution)/shard_map/ppermute | solution.py:458
  17.1 6.5 %collective-permute-start.12 = (bf16[512,128]{1,0:T(8,128)(2,1)S(1)}, bf16[512,128]{1,0:T(8,128)(2,1)S(1)}, u32[]{:S(2)}, u32[]{:S(2)}) collective-permute-start(bf16[512,128]{1,0:T(8,128)(2,1)S(1)} %collective-permute-done.8.refs_7_), channel_id=1, source_target_pairs={{0,4},{1,5},{2,6},{3,7},{8,0},{9,1},{10,2},{11,3},{16,8},{17,9},{1... | collective-permute-start | bytes 393224 | tf_op jit(solution)/shard_map/ppermute | solution.py:458
  17.8 6.0 %collective-permute-start.11 = (bf16[512,128]{1,0:T(8,128)(2,1)S(1)}, bf16[512,128]{1,0:T(8,128)(2,1)S(1)}, u32[]{:S(2)}, u32[]{:S(2)}) collective-permute-start(bf16[512,128]{1,0:T(8,128)(2,1)S(1)} %collective-permute-done.7.refs_6_), channel_id=1, source_target_pairs={{0,8},{1,9},{2,10},{3,11},{8,16},{9,17},{10,18},{11,19},{16,24},{1... | collective-permute-start | bytes 393224 | tf_op jit(solution)/shard_map/ppermute | solution.py:458
  19.7 5.9 %collective-permute-start.13 = (bf16[512,128]{1,0:T(8,128)(2,1)S(1)}, bf16[512,128]{1,0:T(8,128)(2,1)S(1)}, u32[]{:S(2)}, u32[]{:S(2)}) collective-permute-start(bf16[512,128]{1,0:T(8,128)(2,1)S(1)} %collective-permute-done.9.refs_8_), channel_id=1, source_target_pairs={{0,4},{1,5},{2,6},{3,7},{8,0},{9,1},{10,2},{11,3},{16,8},{17,9},{1... | collective-permute-start | bytes 393224 | tf_op jit(solution)/shard_map/ppermute | solution.py:458
  21.7 5.8 %collective-permute-start.10 = (bf16[512,128]{1,0:T(8,128)(2,1)S(1)}, bf16[512,128]{1,0:T(8,128)(2,1)S(1)}, u32[]{:S(2)}, u32[]{:S(2)}) collective-permute-start(bf16[512,128]{1,0:T(8,128)(2,1)S(1)} %collective-permute-done.6.refs_5_), channel_id=1, source_target_pairs={{0,8},{1,9},{2,10},{3,11},{8,16},{9,17},{10,18},{11,19},{16,24},{1... | collective-permute-start | bytes 393224 | tf_op jit(solution)/shard_map/ppermute | solution.py:458
  23.6 5.5 %collective-permute-start.14 = (bf16[512,128]{1,0:T(8,128)(2,1)S(1)}, bf16[512,128]{1,0:T(8,128)(2,1)S(1)}, u32[]{:S(2)}, u32[]{:S(2)}) collective-permute-start(bf16[512,128]{1,0:T(8,128)(2,1)S(1)} %collective-permute-done.12.refs_7_), channel_id=1, source_target_pairs={{0,4},{1,5},{2,6},{3,7},{8,0},{9,1},{10,2},{11,3},{16,8},{17,9},{1... | collective-permute-start | bytes 393224 | tf_op jit(solution)/shard_map/ppermute | solution.py:458
  23.8 7.1 %collective-permute-start.17 = (bf16[512,128]{1,0:T(8,128)(2,1)S(1)}, bf16[512,128]{1,0:T(8,128)(2,1)S(1)}, u32[]{:S(2)}, u32[]{:S(2)}) collective-permute-start(bf16[512,128]{1,0:T(8,128)(2,1)S(1)} %collective-permute-done.11.refs_6_), channel_id=1, source_target_pairs={{0,8},{1,9},{2,10},{3,11},{8,16},{9,17},{10,18},{11,19},{16,24},{1... | collective-permute-start | bytes 393224 | tf_op jit(solution)/shard_map/ppermute | solution.py:458
  25.6 5.2 %collective-permute-start.16 = (bf16[512,128]{1,0:T(8,128)(2,1)S(1)}, bf16[512,128]{1,0:T(8,128)(2,1)S(1)}, u32[]{:S(2)}, u32[]{:S(2)}) collective-permute-start(bf16[512,128]{1,0:T(8,128)(2,1)S(1)} %collective-permute-done.13.refs_8_), channel_id=1, source_target_pairs={{0,4},{1,5},{2,6},{3,7},{8,0},{9,1},{10,2},{11,3},{16,8},{17,9},{1... | collective-permute-start | bytes 393224 | tf_op jit(solution)/shard_map/ppermute | solution.py:458
  29.1 5.0 %collective-permute-start.15 = (bf16[512,128]{1,0:T(8,128)(2,1)S(1)}, bf16[512,128]{1,0:T(8,128)(2,1)S(1)}, u32[]{:S(2)}, u32[]{:S(2)}) collective-permute-start(bf16[512,128]{1,0:T(8,128)(2,1)S(1)} %collective-permute-done.10.refs_2_), channel_id=1, source_target_pairs={{0,8},{1,9},{2,10},{3,11},{8,16},{9,17},{10,18},{11,19},{16,24},{1... | collective-permute-start | bytes 393224 | tf_op jit(solution)/shard_map/ppermute | solution.py:458
  30.9 5.0 %collective-permute-start.18 = (bf16[512,128]{1,0:T(8,128)(2,1)S(1)}, bf16[512,128]{1,0:T(8,128)(2,1)S(1)}, u32[]{:S(2)}, u32[]{:S(2)}) collective-permute-start(bf16[512,128]{1,0:T(8,128)(2,1)S(1)} %collective-permute-done.16.refs_5_), channel_id=1, source_target_pairs={{0,4},{1,5},{2,6},{3,7},{8,0},{9,1},{10,2},{11,3},{16,8},{17,9},{1... | collective-permute-start | bytes 393224 | tf_op jit(solution)/shard_map/ppermute | solution.py:458
  34.4 1.8 %collective-permute-start.19 = (bf16[512,128]{1,0:T(8,128)(2,1)S(1)}, bf16[512,128]{1,0:T(8,128)(2,1)S(1)}, u32[]{:S(2)}, u32[]{:S(2)}) collective-permute-start(bf16[512,128]{1,0:T(8,128)(2,1)S(1)} %last_stages.5), channel_id=1, source_target_pairs={{0,2},{1,3},{2,0},{3,1},{4,6},{5,7},{6,4},{7,5},{8,10},{9,11},{10,... | collective-permute-start | bytes 393224 | tf_op jit(solution)/shard_map/ppermute | solution.py:520
  36.1 1.4 %collective-permute-start.21 = (bf16[512,128]{1,0:T(8,128)(2,1)S(1)}, bf16[512,128]{1,0:T(8,128)(2,1)S(1)}, u32[]{:S(2)}, u32[]{:S(2)}) collective-permute-start(bf16[512,128]{1,0:T(8,128)(2,1)S(1)} %last_stages.7), channel_id=1, source_target_pairs={{0,2},{1,3},{2,0},{3,1},{4,6},{5,7},{6,4},{7,5},{8,10},{9,11},{10,... | collective-permute-start | bytes 393224 | tf_op jit(solution)/shard_map/ppermute | solution.py:520
  36.5 6.4 %collective-permute-start.20 = (bf16[512,128]{1,0:T(8,128)(2,1)S(1)}, bf16[512,128]{1,0:T(8,128)(2,1)S(1)}, u32[]{:S(2)}, u32[]{:S(2)}) collective-permute-start(bf16[512,128]{1,0:T(8,128)(2,1)S(1)} %last_stages.6), channel_id=1, source_target_pairs={{0,1},{1,0},{2,3},{3,2},{4,5},{5,4},{6,7},{7,6},{8,9},{9,8},{10,11... | collective-permute-start | bytes 393224 | tf_op jit(solution)/shard_map/ppermute | solution.py:527
  38.1 4.8 %collective-permute-start.22 = (bf16[512,128]{1,0:T(8,128)(2,1)S(1)}, bf16[512,128]{1,0:T(8,128)(2,1)S(1)}, u32[]{:S(2)}, u32[]{:S(2)}) collective-permute-start(bf16[512,128]{1,0:T(8,128)(2,1)S(1)} %get-tuple-element.90), channel_id=1, source_target_pairs={{0,2},{1,3},{2,0},{3,1},{4,6},{5,7},{6,4},{7,5},{8,10},{9,11},{10,... | collective-permute-start | bytes 393224 | tf_op jit(solution)/shard_map/ppermute | solution.py:528
  38.3 4.6 %collective-permute-start.23 = (bf16[512,128]{1,0:T(8,128)(2,1)S(1)}, bf16[512,128]{1,0:T(8,128)(2,1)S(1)}, u32[]{:S(2)}, u32[]{:S(2)}) collective-permute-start(bf16[512,128]{1,0:T(8,128)(2,1)S(1)} %get-tuple-element.91), channel_id=1, source_target_pairs={{0,2},{1,3},{2,0},{3,1},{4,6},{5,7},{6,4},{7,5},{8,10},{9,11},{10,... | collective-permute-start | bytes 393224 | tf_op jit(solution)/shard_map/ppermute | solution.py:528
  38.7 6.6 %copy-start = (f32[256]{0:T(256)S(1)}, f32[256]{0:T(256)}, u32[]{:S(2)}) copy-start(f32[256]{0:T(256)} %param.10) | copy-start | bytes 3076
  38.7 6.6 %collective-permute-start.24 = (bf16[512,128]{1,0:T(8,128)(2,1)S(1)}, bf16[512,128]{1,0:T(8,128)(2,1)S(1)}, u32[]{:S(2)}, u32[]{:S(2)}) collective-permute-start(bf16[512,128]{1,0:T(8,128)(2,1)S(1)} %get-tuple-element.94), channel_id=1, source_target_pairs={{0,1},{1,0},{2,3},{3,2},{4,5},{5,4},{6,7},{7,6},{8,9},{9,8},{10,11... | collective-permute-start | bytes 393224 | tf_op jit(solution)/shard_map/ppermute | solution.py:527
